TPU v7x, 32 devices: a whole 2x2x4 slice. The times are simulated.
32 devices in a mesh: dp: 16 (over z, x, core), mp: 2 (over y).
Axes of the slice: x: 2, y: 2, z: 4, core: 2. Of those that a mesh axis runs over, the one named last changes fastest.
Arguments:
- prompt_hidden: bfloat16 [8192, 5120], P('dp'), may hold values from -6 to 6
- w_key: bfloat16 [5120, 512], P(None, 'mp'), may hold values from -0.078125 to 0.078125
- w_value: bfloat16 [5120, 512], P(None, 'mp'), may hold values from -0.078125 to 0.078125
- queries: bfloat16 [8192, 4096], P('dp', 'mp'), may hold values from -170 to 170
- resp_key: bfloat16 [8192, 512], P('dp', 'mp'), may hold values from -6.1 to 6.1
- resp_value: bfloat16 [8192, 512], P('dp', 'mp'), may hold values from -6 to 6
- cotangent: bfloat16 [8192, 4096], P('dp', 'mp'), may hold values from -6 to 6
- group_offset: int32 [32], P('dp'), may hold values from 0 to 3, as said below
- resp_length: int32 [32], P('dp'), may hold values from 1 to 256
Outputs:
- attn_out: bfloat16 [8192, 4096], P('dp', 'mp')
- query_grad: bfloat16 [8192, 4096], P('dp', 'mp')
- resp_key_grad: bfloat16 [8192, 512], P('dp', 'mp')
- resp_value_grad: bfloat16 [8192, 512], P('dp', 'mp')
- hidden_grad: bfloat16 [8192, 5120], P('dp', 'mp')
- w_key_grad: float32 [5120, 512], P('dp', 'mp')
- w_value_grad: float32 [5120, 512], P('dp', 'mp')
Inputs may be any that keep to these rules, and one draw needn't show every extreme that they name: `group_offset`: counted cyclically along dp.
All inputs are finite; a program needn't handle non-finite values.
Results may differ from a plain program's by a relative error of at most 0.0095.
Values may be sent and summed in bfloat16 or wider, within the bound.
No kernel may reach another device: no remote copies, remote signals or barrier semaphores. Data moves between devices by JAX's collectives and lax.ppermute only.
A program may use at most 256 MiB of HBM per device.

v0:
```python
import jax
import jax.numpy as jnp
from jax import lax
from jax.sharding import PartitionSpec as P

HD = 128
REACH = 4


def from_behind(block, axis, distance):
    devices = range(lax.axis_size(axis))
    route = [((i - distance) % len(devices), i) for i in devices]
    return lax.ppermute(block, axis, route)


def attend(query, key_rows, value_rows, length, dout):
    row_count = query.shape[0]
    heads_kv = key_rows.shape[1] // HD
    group_size = query.shape[1] // key_rows.shape[1]
    prompt_len = key_rows.shape[0] - row_count
    query_heads = query.reshape(row_count, heads_kv, group_size, HD)
    key_heads = key_rows.reshape(-1, heads_kv, HD)
    value_heads = value_rows.reshape(-1, heads_kv, HD)
    score_scale = HD ** (-0.5)
    scores = (
        jnp.einsum("qgnd,kgd->gnqk", query_heads, key_heads, preferred_element_type=jnp.float32)
        * score_scale
    )
    position = jnp.arange(row_count, dtype=jnp.int32)
    key_position = jnp.arange(key_rows.shape[0], dtype=jnp.int32) - prompt_len
    allowed = key_position[None, :] <= position[:, None]
    scores = jnp.where(allowed, scores, -jnp.inf)
    peak_score = jnp.max(scores, axis=-1, keepdims=True)
    shifted = jnp.exp(scores - peak_score)
    probs = shifted / jnp.sum(shifted, axis=-1, keepdims=True)
    weights = probs.astype(jnp.bfloat16)
    live_rows = (position < length)[:, None, None, None]
    attended = jnp.einsum(
        "gnqk,kgd->qgnd", weights, value_heads, preferred_element_type=jnp.float32
    )
    attended = jnp.where(live_rows, attended, 0.0).reshape(row_count, -1).astype(jnp.bfloat16)
    grad_out = jnp.where(
        live_rows, dout.reshape(row_count, heads_kv, group_size, HD), jnp.zeros((), jnp.bfloat16)
    )
    prob_grad = jnp.einsum(
        "qgnd,kgd->gnqk", grad_out, value_heads, preferred_element_type=jnp.float32
    )
    delta_sum = jnp.sum(probs * prob_grad, axis=-1, keepdims=True)
    score_grad = (probs * (prob_grad - delta_sum) * score_scale).astype(jnp.bfloat16)
    query_grad = jnp.einsum(
        "gnqk,kgd->qgnd", score_grad, key_heads, preferred_element_type=jnp.float32
    )
    query_grad = query_grad.reshape(row_count, -1).astype(jnp.bfloat16)
    key_grad = jnp.einsum(
        "gnqk,qgnd->kgd", score_grad, query_heads, preferred_element_type=jnp.float32
    )
    value_grad = jnp.einsum("gnqk,qgnd->kgd", weights, grad_out, preferred_element_type=jnp.float32)
    key_grad = key_grad.reshape(key_rows.shape[0], -1)
    value_grad = value_grad.reshape(key_rows.shape[0], -1)
    return (attended, query_grad, key_grad, value_grad)


def body(
    prompt_hidden,
    w_key,
    w_value,
    queries,
    resp_key,
    resp_value,
    cotangent,
    group_offset,
    resp_length,
):
    prompt_len = prompt_hidden.shape[0]
    slot_count = group_offset.shape[0]
    resp_len = queries.shape[0] // slot_count
    own_key = jnp.dot(prompt_hidden, w_key, preferred_element_type=jnp.float32).astype(jnp.bfloat16)
    own_value = jnp.dot(prompt_hidden, w_value, preferred_element_type=jnp.float32).astype(
        jnp.bfloat16
    )
    own_pair = jnp.stack([own_key, own_value])
    received = [own_pair]
    for distance in range(1, REACH):
        received.append(from_behind(own_pair, "dp", distance))
    stacked = jnp.stack(received)
    partials = jnp.zeros((REACH, 2, prompt_len, w_key.shape[1]), jnp.float32)
    attended_list, query_list, key_list, value_list = ([], [], [], [])
    for slot_index in range(slot_count):
        offset = group_offset[slot_index]
        chosen = lax.dynamic_index_in_dim(stacked, offset, 0, keepdims=False)
        lower = slot_index * resp_len
        key_rows = jnp.concatenate([chosen[0], resp_key[lower : lower + resp_len]], axis=0)
        value_rows = jnp.concatenate([chosen[1], resp_value[lower : lower + resp_len]], axis=0)
        attended, query_grad, key_grad, value_grad = attend(
            queries[lower : lower + resp_len],
            key_rows,
            value_rows,
            resp_length[slot_index],
            cotangent[lower : lower + resp_len],
        )
        attended_list.append(attended)
        query_list.append(query_grad)
        key_list.append(key_grad[prompt_len:].astype(jnp.bfloat16))
        value_list.append(value_grad[prompt_len:].astype(jnp.bfloat16))
        grad_pair = jnp.stack([key_grad[:prompt_len], value_grad[:prompt_len]])
        selector = (jnp.arange(REACH, dtype=jnp.int32) == offset).astype(jnp.float32)
        partials = partials + selector[:, None, None, None] * grad_pair[None]
    totals = partials[0]
    for distance in range(1, REACH):
        totals = totals + from_behind(partials[distance], "dp", -distance)
    grads_bf = totals.astype(jnp.bfloat16)
    partial_hidden = jnp.dot(grads_bf[0], w_key.T, preferred_element_type=jnp.float32) + jnp.dot(
        grads_bf[1], w_value.T, preferred_element_type=jnp.float32
    )
    hidden_grad = lax.psum_scatter(partial_hidden, "mp", scatter_dimension=1, tiled=True).astype(
        jnp.bfloat16
    )
    weight_term = jnp.einsum(
        "pd,spk->dsk", prompt_hidden, grads_bf, preferred_element_type=jnp.float32
    )
    weight_grads = lax.psum_scatter(weight_term, "dp", scatter_dimension=0, tiled=True)
    return (
        jnp.concatenate(attended_list, axis=0),
        jnp.concatenate(query_list, axis=0),
        jnp.concatenate(key_list, axis=0),
        jnp.concatenate(value_list, axis=0),
        hidden_grad,
        weight_grads[:, 0, :],
        weight_grads[:, 1, :],
    )


def solution(mesh):
    placed = (
        P("dp", None),
        P(None, "mp"),
        P(None, "mp"),
        P("dp", "mp"),
        P("dp", "mp"),
        P("dp", "mp"),
        P("dp", "mp"),
        P("dp"),
        P("dp"),
    )
    return jax.shard_map(
        body,
        mesh=mesh,
        in_specs=placed,
        out_specs=(
            P("dp", "mp"),
            P("dp", "mp"),
            P("dp", "mp"),
            P("dp", "mp"),
            P("dp", "mp"),
            P("dp", "mp"),
            P("dp", "mp"),
        ),
        check_vma=False,
    )
```

profile of v0, /device:TPU:0, one launch (start us, length us, event | category | flops | bytes accessed | tf_op | source)
XLA Modules:
  0.0 445.3 jit_solution(7937179493903161171)
XLA Ops:
  8.1 5.0 %fusion.51 = bf16[1,512,256]{1,2,0:T(8,128)(2,1)S(1)} fusion(bf16[512,5120]{1,0:T(8,128)(2,1)} %param.9, bf16[5120,256]{1,0:T(8,128)(2,1)} %param.10), kind=kOutput, calls=%fused_computation.61 | convolution fusion | flops 1342308352 | bytes 8126464 | tf_op jit(solution)/shard_map/dot_general | solution.py:77
  13.6 1.6 fusion.52
  15.2 0.9 fusion.96
  16.1 2.9 collective-permute-start.1
  19.0 3.3 collective-permute-start.2
  26.7 1.0 fusion.99
  27.8 0.8 copy.89
  28.7 0.8 copy.96
  29.5 1.0 fusion.100
  30.6 0.8 copy.93
  31.3 3.1 fusion.98
  34.4 2.3 copy.160
  36.7 2.3 copy.162
  38.9 3.1 fusion.97
  42.1 2.3 copy.151
  44.4 2.3 copy.156
  48.6 1.3 compare_convert_fusion
  49.9 0.9 iota_compare_fusion
  50.8 1.6 pad_maximum_fusion
  52.4 0.8 constant_dynamic-slice_fusion.3
  53.2 0.8 copy.88
  54.2 7.8 %fusion.58 = f32[2,768,256,8]{2,1,3,0:T(8,128)} fusion(bf16[256,2,8,128]{0,3,2,1:T(8,128)(2,1)} %bitcast.252, pred[256]{0:T(512)(128)(4,1)S(1)} %iota_compare_fusion.1, bf16[256,2,128]{0,2,1:T(8,128)(2,1)} %bitcast.274, bf16[512,2,128]{0,2,1:T(8,128)(2,1)S(1)} %bitcast.260), kind=kOutput, calls=%fused_computation.76 | convolution fusion | flops 806617088 | bytes 14024960 | tf_op jit(solution)/shard_map/qgnd,kgd->gnqk/dot_general | solution.py:45
  62.1 10.3 %fusion.103 = (f32[2,8,256]{2,1,0:T(8,128)}, f32[2,8,256,768]{2,3,1,0:T(8,128)}) fusion(pred[256,768]{0,1:T(8,128)(4,1)S(1)} %copy-done.10, bf16[256,2,8,128]{0,3,2,1:T(8,128)(2,1)} %bitcast.266, bf16[256,2,128]{2,0,1:T(8,128)(2,1)} %copy.96, bf16[512,2,128]{2,0,1:T(8,128)(2,1)S(1)} %copy.95), kind=kOutput, calls=%fused_computation.144 | convolution fusion | flops 818676480 | bytes 14237696 | tf_op jit(solution)/shard_map/sub | solution.py:34
  72.4 7.0 %fusion.46 = f32[768,2,128]{0,2,1:T(8,128)S(1)} fusion(bf16[256,2,8,128]{0,3,2,1:T(8,128)(2,1)} %bitcast.253, pred[256]{0:T(512)(128)(4,1)S(1)} %iota_compare_fusion.1, f32[2,8,256,768]{2,3,1,0:T(8,128)} %get-tuple-element.45, f32[2,8,256]{2,1,0:T(8,128)} %get-tuple-element.44), kind=kOutput, calls=%fused_computation.56 | convolution fusion | flops 812122112 | bytes 14434560 | tf_op jit(solution)/shard_map/gnqk,qgnd->kgd/dot_general | solution.py:57
  79.4 18.8 %fusion.49 = f32[768,2,128]{0,2,1:T(8,128)} fusion(bf16[256,2,8,128]{0,3,2,1:T(8,128)(2,1)} %bitcast.267, f32[2,768,256,8]{2,1,3,0:T(8,128)} %fusion.58, f32[2,8,256,768]{2,3,1,0:T(8,128)} %get-tuple-element.45, f32[2,8,256]{2,1,0:T(8,128)} %get-tuple-element.44), kind=kOutput, calls=%fused_computation.57 | convolution fusion | flops 827331328 | bytes 27017216 | tf_op jit(solution)/shard_map/gnqk,qgnd->kgd/dot_general | solution.py:54
  98.2 1.9 slice.150
  100.1 9.8 %fusion.104 = (f32[2,8,256]{2,1,0:T(8,128)S(1)}, f32[2,8,256,768]{2,3,1,0:T(8,128)}) fusion(pred[256,768]{0,1:T(8,128)(4,1)} %iota_compare_fusion, bf16[256,2,8,128]{0,3,2,1:T(8,128)(2,1)} %bitcast.264, bf16[256,2,128]{2,0,1:T(8,128)(2,1)} %copy.89, bf16[512,2,128]{2,0,1:T(8,128)(2,1)} %copy.88), kind=kOutput, calls=%fused_computation.145 | convolution fusion | flops 818676480 | bytes 14237696 | tf_op jit(solution)/shard_map/sub | solution.py:34
  110.0 8.6 %fusion.57 = f32[2,768,256,8]{2,1,3,0:T(8,128)} fusion(bf16[256,2,8,128]{0,3,2,1:T(8,128)(2,1)} %bitcast.250, pred[256]{0:T(512)(128)(4,1)S(1)} %iota_compare_fusion.2, bf16[256,2,128]{0,2,1:T(8,128)(2,1)S(1)} %bitcast.272, bf16[512,2,128]{0,2,1:T(8,128)(2,1)S(1)} %bitcast.258), kind=kOutput, calls=%fused_computation.75 | convolution fusion | flops 806617088 | bytes 14024960 | tf_op jit(solution)/shard_map/qgnd,kgd->gnqk/dot_general | solution.py:45
  118.6 3.1 fusion.43
  121.7 18.7 %fusion.50 = f32[768,2,128]{0,2,1:T(8,128)} fusion(bf16[256,2,8,128]{0,3,2,1:T(8,128)(2,1)} %bitcast.265, f32[2,768,256,8]{2,1,3,0:T(8,128)} %fusion.57, f32[2,8,256,768]{2,3,1,0:T(8,128)} %get-tuple-element.47, f32[2,8,256]{2,1,0:T(8,128)} %copy-done.15), kind=kOutput, calls=%fused_computation.58 | convolution fusion | flops 827331328 | bytes 27017216 | tf_op jit(solution)/shard_map/gnqk,qgnd->kgd/dot_general | solution.py:54
  140.4 1.2 slice.149
  141.6 1.3 slice.148
  142.9 1.2 pad_maximum_fusion.3
  144.1 0.7 multiply_add_fusion
  145.2 1.8 collective-permute-start.3
  147.6 1.3 collective-permute-start.4
  148.9 20.8 %collective-permute-done.3 = f32[2,512,256]{1,2,0:T(8,128)S(1)} collective-permute-done((f32[2,512,256]{1,2,0:T(8,128)S(1)}, f32[2,512,256]{1,2,0:T(8,128)S(1)}, u32[]{:S(2)}, u32[]{:S(2)}) %collective-permute-start.3) | collective-permute-done | bytes 1048608 | tf_op jit(solution)/shard_map/ppermute | solution.py:13
  169.7 22.5 %collective-permute-done.5 = f32[2,512,256]{1,2,0:T(8,128)S(1)} collective-permute-done((f32[2,512,256]{1,2,0:T(8,128)S(1)}, f32[2,512,256]{1,2,0:T(8,128)S(1)}, u32[]{:S(2)}, u32[]{:S(2)}) %collective-permute-start.5) | collective-permute-done | bytes 1048608 | tf_op jit(solution)/shard_map/ppermute | solution.py:13
  192.2 12.2 %collective-permute-done.4 = f32[2,512,256]{1,2,0:T(8,128)S(1)} collective-permute-done((f32[2,512,256]{1,2,0:T(8,128)S(1)}, f32[2,512,256]{1,2,0:T(8,128)S(1)}, u32[]{:S(2)}, u32[]{:S(2)}) %collective-permute-start.4) | collective-permute-done | bytes 1048608 | tf_op jit(solution)/shard_map/ppermute | solution.py:13
  204.9 5.7 %convolution_bitcast_fusion = f32[5120,2,256]{0,2,1:T(8,128)} fusion(bf16[2,512,256]{1,2,0:T(8,128)(2,1)S(1)} %fusion.56, bf16[512,5120]{1,0:T(8,128)(2,1)S(1)} %bitcast.249), kind=kOutput, calls=%fused_computation.21 | convolution fusion | flops 2684354560 | bytes 16252928 | tf_op jit(solution)/shard_map/pd,spk->dsk/dot_general | solution.py:118
  210.6 16.1 %copy.122 = f32[5120,2,256]{2,1,0:T(2,128)} copy(f32[5120,2,256]{0,2,1:T(8,128)} %convolution_bitcast_fusion) | data formatting | bytes 20971520 | tf_op jit(solution)/shard_map/pd,spk->dsk/dot_general | solution.py:118
  226.8 1.6 fusion.63
  228.5 5.6 %convolution_add_fusion = f32[512,5120]{1,0:T(8,128)} fusion(f32[512,5120]{1,0:T(8,128)S(1)} %fusion.63, bf16[5120,256]{1,0:T(8,128)(2,1)S(1)} %copy-done.3, bf16[2,512,256]{1,2,0:T(8,128)(2,1)S(1)} %fusion.56), kind=kOutput, calls=%fused_computation.20 | convolution fusion | flops 1344798720 | bytes 23855104 | tf_op jit(solution)/shard_map/dot_general | solution.py:112
  235.4 1.0 slice.178
  236.4 1.0 slice.180
  237.4 1.0 slice.179
  238.3 1.0 slice.181
  239.3 7.9 %select_convert_fusion = bf16[2,128,8,256]{3,1,2,0:T(8,128)(2,1)} fusion(pred[256]{0:T(512)(128)(4,1)S(1)} %iota_compare_fusion.1, bf16[256,2,128]{0,2,1:T(8,128)(2,1)} %bitcast.275, bf16[512,2,128]{0,2,1:T(8,128)(2,1)} %bitcast.261, f32[2,8,256,768]{2,3,1,0:T(8,128)} %get-tuple-element.45, f32[2,8,256]{2,1,0:T(8,128)} %get-tuple-element.44), kind=kOutput, calls=%fused_computation.49 | convolution fusion | flops 813432832 | bytes 14041344 | tf_op jit(solution)/shard_map/gnqk,kgd->qgnd/dot_general | solution.py:38
  247.2 2.5 copy.101
  249.7 20.2 %fusion.33 = bf16[2,128,8,256]{3,1,2,0:T(8,128)(2,1)} fusion(f32[2,768,256,8]{2,1,3,0:T(8,128)} %fusion.58, bf16[256,2,128]{2,0,1:T(8,128)(2,1)} %copy.96, bf16[512,2,128]{2,0,1:T(8,128)(2,1)} %copy-done.9, f32[2,8,256,768]{2,3,1,0:T(8,128)} %get-tuple-element.45, f32[2,8,256]{2,1,0:T(8,128)} %get-tuple-element.44), kind=kOutput, calls=%fused_computation.51 | convolution fusion | flops 828642048 | bytes 26624000 | tf_op jit(solution)/shard_map/gnqk,kgd->qgnd/dot_general | solution.py:50
  269.9 2.3 copy.113
  272.2 0.8 copy.121
  272.9 0.8 copy.117
  273.7 7.0 %select_convert_fusion.1 = bf16[2,128,8,256]{3,1,2,0:T(8,128)(2,1)} fusion(pred[256]{0:T(512)(128)(4,1)S(1)} %iota_compare_fusion.2, bf16[256,2,128]{0,2,1:T(8,128)(2,1)S(1)} %bitcast.273, bf16[512,2,128]{0,2,1:T(8,128)(2,1)S(1)} %bitcast.259, f32[2,8,256,768]{2,3,1,0:T(8,128)} %get-tuple-element.47, f32[2,8,256]{2,1,0:T(8,128)} %copy-done.15), kind=kOutput, calls=%fused_computation.50 | convolution fusion | flops 813432832 | bytes 14041344 | tf_op jit(solution)/shard_map/gnqk,kgd->qgnd/dot_general | solution.py:38
  280.7 2.4 copy.100
  283.1 20.4 %fusion.34 = bf16[2,128,8,256]{3,1,2,0:T(8,128)(2,1)} fusion(f32[2,768,256,8]{2,1,3,0:T(8,128)} %fusion.57, bf16[256,2,128]{2,0,1:T(8,128)(2,1)} %copy.89, bf16[512,2,128]{2,0,1:T(8,128)(2,1)} %copy.88, f32[2,8,256,768]{2,3,1,0:T(8,128)} %get-tuple-element.47, f32[2,8,256]{2,1,0:T(8,128)} %copy-done.15), kind=kOutput, calls=%fused_computation.52 | convolution fusion | flops 828642048 | bytes 26624000 | tf_op jit(solution)/shard_map/gnqk,kgd->qgnd/dot_general | solution.py:50
  303.5 2.3 copy.112
  306.0 0.8 pad_maximum_fusion.6
  306.8 4.9 %pad_maximum_fusion.1 = (bf16[512,2048]{1,0:T(8,128)(2,1)}, bf16[512,2048]{1,0:T(8,128)(2,1)}) fusion(bf16[256,2048]{1,0:T(8,128)(2,1)} %copy.101, bf16[256,2048]{1,0:T(8,128)(2,1)} %copy.100, bf16[256,2048]{1,0:T(8,128)(2,1)} %copy.113, bf16[256,2048]{1,0:T(8,128)(2,1)} %copy.112), kind=kLoop, calls=%fused_computation.47 | loop fusion | flops 8388608 | bytes 8388608 | tf_op jit(solution)/shard_map/concatenate | solution.py:123
  311.7 118.3 %all-reduce.3.cloned.1.call-done = f32[5120,2,256]{2,1,0:T(2,128)} async-done(((f32[5120,2,256]{2,1,0:T(2,128)}), f32[5120,2,256]{2,1,0:T(2,128)}) %all-reduce.3.cloned.1.call-update) | async-done | bytes 10485776
  430.0 1.9 constant_dynamic-slice_fusion.5
  431.9 0.7 copy.165
  432.6 0.7 copy.166
  433.3 4.3 convert_element_type.115
  (63 shorter events, 6.0 us)
Async XLA Ops:
  8.0 5.6 %copy-start = (bf16[5120,256]{1,0:T(8,128)(2,1)S(1)}, bf16[5120,256]{1,0:T(8,128)(2,1)}, u32[]{:S(2)}) copy-start(bf16[5120,256]{1,0:T(8,128)(2,1)} %param.11) | copy-start | bytes 7864324
  8.0 14.3 %copy-start.11 = (s32[2]{0:T(128)S(1)}, s32[2]{0:T(128)}, u32[]{:S(2)}) copy-start(s32[2]{0:T(128)} %param.16) | copy-start | bytes 28
  8.0 17.5 %copy-start.12 = (s32[2]{0:T(128)S(1)}, s32[2]{0:T(128)}, u32[]{:S(2)}) copy-start(s32[2]{0:T(128)} %param.17) | copy-start | bytes 28
  8.0 421.9 %all-reduce.3.cloned.1.call-start = ((), (), s32[]{:S(2)}) async-start(), calls=%async_computation.2 | async-start | bytes 20971520
  8.1 5.5 %copy-start.1 = (bf16[512,5120]{1,0:T(8,128)(2,1)S(1)}, bf16[512,5120]{1,0:T(8,128)(2,1)}, u32[]{:S(2)}) copy-start(bf16[512,5120]{1,0:T(8,128)(2,1)} %param.9) | copy-start | bytes 15728644
  16.1 34.7 %collective-permute-start.1 = (bf16[2,512,256]{1,2,0:T(8,128)(2,1)}, bf16[2,512,256]{1,2,0:T(8,128)(2,1)}, u32[]{:S(2)}, u32[]{:S(2)}) collective-permute-start(bf16[2,512,256]{1,2,0:T(8,128)(2,1)} %get-tuple-element.35), channel_id=1, source_target_pairs={{28,0},{30,2},{0,4},{2,6},{4,8},{6,10},{8,12},{10,14},{12,16},{14,... | collective-permute-start | bytes 1572872 | tf_op jit(solution)/shard_map/ppermute | solution.py:13
  19.0 31.7 %collective-permute-start = (bf16[2,512,256]{1,2,0:T(8,128)(2,1)}, bf16[2,512,256]{1,2,0:T(8,128)(2,1)}, u32[]{:S(2)}, u32[]{:S(2)}) collective-permute-start(bf16[2,512,256]{1,2,0:T(8,128)(2,1)} %get-tuple-element.35), channel_id=1, source_target_pairs={{30,0},{0,2},{2,4},{4,6},{6,8},{8,10},{10,12},{12,14},{14,16},{16,... | collective-permute-start | bytes 1572872 | tf_op jit(solution)/shard_map/ppermute | solution.py:13
  19.0 31.7 %collective-permute-start.2 = (bf16[2,512,256]{1,2,0:T(8,128)(2,1)}, bf16[2,512,256]{1,2,0:T(8,128)(2,1)}, u32[]{:S(2)}, u32[]{:S(2)}) collective-permute-start(bf16[2,512,256]{1,2,0:T(8,128)(2,1)} %get-tuple-element.35), channel_id=1, source_target_pairs={{26,0},{28,2},{30,4},{0,6},{2,8},{4,10},{6,12},{8,14},{10,16},{12,... | collective-permute-start | bytes 1572872 | tf_op jit(solution)/shard_map/ppermute | solution.py:13
  53.2 19.2 %copy-start.6 = (bf16[1,1,512,256]{2,3,1,0:T(8,128)(2,1)}, bf16[1,1,512,256]{2,3,1,0:T(8,128)(2,1)S(1)}, u32[]{:S(2)}) copy-start(bf16[1,1,512,256]{2,3,1,0:T(8,128)(2,1)S(1)} %get-tuple-element.29) | copy-start | bytes 786436
  54.2 18.2 %copy-start.9 = (bf16[512,2,128]{2,0,1:T(8,128)(2,1)}, bf16[512,2,128]{2,0,1:T(8,128)(2,1)S(1)}, u32[]{:S(2)}) copy-start(bf16[512,2,128]{2,0,1:T(8,128)(2,1)S(1)} %copy.95) | copy-start | bytes 786436
  54.2 7.9 %copy-start.10 = (pred[256,768]{0,1:T(8,128)(4,1)S(1)}, pred[256,768]{0,1:T(8,128)(4,1)}, u32[]{:S(2)}) copy-start(pred[256,768]{0,1:T(8,128)(4,1)} %iota_compare_fusion) | copy-start | bytes 589828
  79.4 18.9 %copy-start.4 = (f32[768,2,128]{0,2,1:T(8,128)}, f32[768,2,128]{0,2,1:T(8,128)S(1)}, u32[]{:S(2)}) copy-start(f32[768,2,128]{0,2,1:T(8,128)S(1)} %fusion.46) | copy-start | bytes 2359300
  98.2 11.8 %copy-start.5 = (bf16[1,1,512,256]{2,3,1,0:T(8,128)(2,1)S(1)}, bf16[1,1,512,256]{2,3,1,0:T(8,128)(2,1)}, u32[]{:S(2)}) copy-start(bf16[1,1,512,256]{2,3,1,0:T(8,128)(2,1)} %get-tuple-element.30) | copy-start | bytes 786436
  110.0 8.6 %copy-start.15 = (f32[2,8,256]{2,1,0:T(8,128)}, f32[2,8,256]{2,1,0:T(8,128)S(1)}, u32[]{:S(2)}) copy-start(f32[2,8,256]{2,1,0:T(8,128)S(1)} %get-tuple-element.46) | copy-start | bytes 49156
  110.0 8.6 %copy-start.2 = (bf16[256,2048]{0,1:T(8,128)(2,1)S(1)}, bf16[256,2048]{0,1:T(8,128)(2,1)}, u32[]{:S(2)}) copy-start(bf16[256,2048]{0,1:T(8,128)(2,1)} %copy.151) | copy-start | bytes 3145732
  110.0 8.6 %copy-start.14 = (f32[2,8,256,768]{2,3,1,0:T(8,128)S(1)}, f32[2,8,256,768]{2,3,1,0:T(8,128)}, u32[]{:S(2)}) copy-start(f32[2,8,256,768]{2,3,1,0:T(8,128)} %get-tuple-element.47) | copy-start | bytes 37748740
  121.7 21.2 %slice-start.2 = ((f32[768,2,128]{0,2,1:T(8,128)}), f32[512,2,128]{0,2,1:T(8,128)S(1)}, s32[]{:S(2)}) async-start(f32[768,2,128]{0,2,1:T(8,128)} %copy-done.4), calls=%async_computation.5 | async-start | bytes 1048576 | tf_op jit(solution)/shard_map/slice | solution.py:105
  140.4 64.5 %slice-start = ((s8[5242880]{0:T(1024)(128)(4,1)}), s8[4194304]{0:T(1024)(128)(4,1)S(1)}, s32[]{:S(2)}) async-start(s8[5242880]{0:T(1024)(128)(4,1)} %bitcast.248), calls=%async_computation.3 | async-start | bytes 8388608
  144.1 60.7 %slice-start.1 = ((s8[5242880]{0:T(1024)(128)(4,1)}), s8[1048576]{0:T(1024)(128)(4,1)S(1)}, s32[]{:S(2)}) async-start(s8[5242880]{0:T(1024)(128)(4,1)} %bitcast.248), calls=%async_computation.4 | async-start | bytes 2097152
  145.2 24.5 %collective-permute-start.3 = (f32[2,512,256]{1,2,0:T(8,128)S(1)}, f32[2,512,256]{1,2,0:T(8,128)S(1)}, u32[]{:S(2)}, u32[]{:S(2)}) collective-permute-start(f32[2,512,256]{1,2,0:T(8,128)S(1)} %get-tuple-element.23), channel_id=1, source_target_pairs={{2,0},{4,2},{6,4},{8,6},{10,8},{12,10},{14,12},{16,14},{18,16},{20... | collective-permute-start | bytes 3145736 | tf_op jit(solution)/shard_map/ppermute | solution.py:13
  147.1 45.1 %collective-permute-start.5 = (f32[2,512,256]{1,2,0:T(8,128)S(1)}, f32[2,512,256]{1,2,0:T(8,128)S(1)}, u32[]{:S(2)}, u32[]{:S(2)}) collective-permute-start(f32[2,512,256]{1,2,0:T(8,128)S(1)} %get-tuple-element.24), channel_id=1, source_target_pairs={{6,0},{8,2},{10,4},{12,6},{14,8},{16,10},{18,12},{20,14},{22,16},{... | collective-permute-start | bytes 3145736 | tf_op jit(solution)/shard_map/ppermute | solution.py:13
  147.6 56.7 %collective-permute-start.4 = (f32[2,512,256]{1,2,0:T(8,128)S(1)}, f32[2,512,256]{1,2,0:T(8,128)S(1)}, u32[]{:S(2)}, u32[]{:S(2)}) collective-permute-start(f32[2,512,256]{1,2,0:T(8,128)S(1)} %get-tuple-element.25), channel_id=1, source_target_pairs={{4,0},{6,2},{8,4},{10,6},{12,8},{14,10},{16,12},{18,14},{20,16},{2... | collective-permute-start | bytes 3145736 | tf_op jit(solution)/shard_map/ppermute | solution.py:13
  226.7 206.6 %reduce-scatter.2.cloned.1.call-start = ((), (), s32[]{:S(2)}) async-start(), calls=%async_computation.1 | async-start | bytes 15728640 | tf_op jit(solution)/shard_map/reduce_scatter | solution.py:115
  226.8 1.7 copy-start.3
  228.5 5.7 %copy-start.13 = (u32[32]{0:T(128)S(1)}, u32[32]{0:T(128)}, u32[]{:S(2)}) copy-start(u32[32]{0:T(128)} %constant.23) | copy-start | bytes 388
  283.1 22.9 %copy-start.7 = (bf16[256,256]{1,0:T(8,128)(2,1)S(1)}, bf16[256,256]{1,0:T(8,128)(2,1)}, u32[]{:S(2)}) copy-start(bf16[256,256]{1,0:T(8,128)(2,1)} %copy.121) | copy-start | bytes 393220
  283.1 22.9 %copy-start.8 = (bf16[256,256]{1,0:T(8,128)(2,1)S(1)}, bf16[256,256]{1,0:T(8,128)(2,1)}, u32[]{:S(2)}) copy-start(bf16[256,256]{1,0:T(8,128)(2,1)} %copy.117) | copy-start | bytes 393220
Sparse Core Ops, SparseCore 0:
  226.8 203.1 all-reduce.2
Sparse Core Ops, SparseCore 1:
  234.2 124.1 reduce-scatter.1
where the time goes:
time: 450 us; the launch traced here: 445 us
  waiting for transfers between devices  174 us (39%)
  matrix products  159 us (35%)
  local copies, waits for them, and re-layouts  63.4 us (14%)
  between operations  20.7 us (5%)
  other arithmetic  18.4 us (4%)
  starting transfers between devices  9.98 us (2%)
    unnamed x3, waiting for transfers between devices  118 us
    ppermute x6, waiting for transfers between devices, from_behind(): return lax.ppermute(block, axis, route)  55.4 us
    dot_general x2, matrix products, attend(): jnp.einsum('gnqk,kgd->qgnd', score_grad, key_heads, preferred_element_typ...  40.6 us
    dot_general x2, matrix products, attend(): jnp.einsum('gnqk,qgnd->kgd', score_grad, query_heads, preferred_element_t...  37.6 us
    sub x2, matrix products, attend(): shifted = jnp.exp(scores - peak_score)  20.1 us
    dot_general x2, matrix products, attend(): jnp.einsum('qgnd,kgd->gnqk', grad_out, value_heads, preferred_element_typ...  16.4 us
    dot_general x1, local copies, waits for them, and re-layouts, body(): jnp.einsum('pd,spk->dsk', prompt_hidden, grads_bf, preferred_element_type...  16.1 us
    dot_general x2, matrix products, attend(): jnp.einsum('gnqk,kgd->qgnd', weights, value_heads, preferred_element_type...  14.9 us
  transfers between devices with their start and end apart: 8, of which 4 were waited for; matrix products, arithmetic and copies ran while one was open for 25% of the time, Pallas kernels for 0%

commit v1 on v0

v1 whole, which is shorter than its diff:
```python
import functools
import math

import jax
import jax.numpy as jnp
from jax import lax
from jax.experimental import pallas as pl
from jax.experimental.pallas import tpu as pltpu
from jax.sharding import PartitionSpec as P

HD = 128
REACH = 4
LOG2E = 1.4426950408889634
BF = jnp.bfloat16
F32 = jnp.float32
NT = (((1,), (1,)), ((), ()))
NN = (((1,), (0,)), ((), ()))
TN = (((0,), (0,)), ((), ()))
MIB = 1024 * 1024


def mm(a, b, dims=NN):
    return lax.dot_general(a, b, dims, preferred_element_type=F32)


def permute(block, axis, target):
    return lax.ppermute(block, axis, [(i, target(i)) for i in range(lax.axis_size(axis))])


def project_kernel(h_ref, wk_ref, wv_ref, *rest):
    *outs, acc = rest
    step = pl.program_id(0)
    width = wk_ref.shape[1]
    key = mm(h_ref[...], wk_ref[...])
    value = mm(h_ref[...], wv_ref[...])

    @pl.when(step == 0)
    def _():
        acc[:, :width] = key
        acc[:, width:] = value

    @pl.when(step > 0)
    def _():
        acc[:, :width] += key
        acc[:, width:] += value

    @pl.when(step == pl.num_programs(0) - 1)
    def _():
        for g, out in enumerate(outs):
            out[0] = acc[:, g * HD : (g + 1) * HD].astype(BF)
            out[1] = acc[:, width + g * HD : width + (g + 1) * HD].astype(BF)


def project(hidden, w_key, w_value):
    rows, depth = hidden.shape
    width = w_key.shape[1]
    tile = 512
    groups = width // HD
    return pl.pallas_call(
        project_kernel,
        out_shape=[jax.ShapeDtypeStruct((2, rows, HD), BF)] * groups,
        grid=(depth // tile,),
        in_specs=[
            pl.BlockSpec((rows, tile), lambda i: (0, i)),
            pl.BlockSpec((tile, width), lambda i: (i, 0)),
            pl.BlockSpec((tile, width), lambda i: (i, 0)),
        ],
        out_specs=[pl.BlockSpec((2, rows, HD), lambda i: (0, 0, 0))] * groups,
        scratch_shapes=[pltpu.VMEM((rows, 2 * width), F32)],
        compiler_params=pltpu.CompilerParams(vmem_limit_bytes=32 * MIB),
        cost_estimate=pl.CostEstimate(
            flops=4 * rows * depth * width,
            bytes_accessed=2 * depth * (rows + 2 * width),
            transcendentals=0,
        ),
        name="project",
    )(hidden, w_key, w_value)


def attend_kernel(heads, sel_ref, len_ref, q_ref, do_ref, *rest):
    kv_refs, (rk_ref, rv_ref), rest = rest[:REACH], rest[REACH : REACH + 2], rest[REACH + 2 :]
    (o_ref, dq_ref, rdk_ref, rdv_ref, part_ref, k_s, v_s, kt_s, vt_s, dk_s, dv_s, first_s) = rest[-12:]
    r = pl.program_id(0)
    plen = kv_refs[0].shape[1]
    rlen = q_ref.shape[0]
    sel = sel_ref[r]
    for j, ref in enumerate(kv_refs):

        @pl.when(sel == j)
        def _():
            k_s[:plen] = ref[0]
            v_s[:plen] = ref[1]

    k_s[plen:] = rk_ref[...]
    v_s[plen:] = rv_ref[...]
    kt_s[...] = k_s[...].T
    vt_s[...] = v_s[...].T
    scale = HD**-0.5
    c = scale * LOG2E
    live = lax.broadcasted_iota(jnp.int32, (1, rlen), 1) < len_ref[r]
    livef = live.astype(F32)
    key_pos = lax.broadcasted_iota(jnp.int32, (rlen, rlen), 0)
    allowed = key_pos <= lax.broadcasted_iota(jnp.int32, (rlen, rlen), 1)
    for h in range(heads):
        cols = pl.ds(h * HD, HD)
        q = q_ref[:, cols]
        s = mm(k_s[...], q, NT)
        sp = s[:plen]
        sr = jnp.where(allowed, s[plen:], -jnp.inf)
        m = jnp.maximum(jnp.max(sp, axis=0, keepdims=True), jnp.max(sr, axis=0, keepdims=True))
        e = jnp.concatenate([jnp.exp2((sp - m) * c), jnp.exp2((sr - m) * c)], axis=0)
        eb = e.astype(BF)
        inv = livef / jnp.sum(e, axis=0, keepdims=True)
        ot = mm(vt_s[...], eb) * inv
        o_ref[:, cols] = ot.T.astype(BF)
        dob = (do_ref[:, cols].T.astype(F32) * inv).astype(BF)
        delta = jnp.sum(dob.astype(F32) * ot, axis=0, keepdims=True)
        ds = (e * (mm(v_s[...], dob) - delta)).astype(BF)
        dq_ref[:, cols] = (mm(kt_s[...], ds) * scale).T.astype(BF)
        dv = mm(eb, dob, NT)
        dk = mm(ds, q)
        if h == 0:
            dk_s[...] = dk
            dv_s[...] = dv
        else:
            dk_s[...] += dk
            dv_s[...] += dv
    rdk_ref[...] = (dk_s[plen:] * scale).astype(BF)
    rdv_ref[...] = dv_s[plen:].astype(BF)

    @pl.when(r == 0)
    def _():
        first_s[0] = dk_s[:plen]
        first_s[1] = dv_s[:plen]

    @pl.when(r == 1)
    def _():
        one, two = sel_ref[0], sel_ref[1]
        for j in range(REACH):

            @pl.when((one != j) & (two != j))
            def _():
                part_ref[j] = jnp.zeros(part_ref.shape[1:], BF)

            @pl.when((one == j) & (two != j))
            def _():
                part_ref[j, 0] = (first_s[0] * scale).astype(BF)
                part_ref[j, 1] = first_s[1].astype(BF)

            @pl.when((one != j) & (two == j))
            def _():
                part_ref[j, 0] = (dk_s[:plen] * scale).astype(BF)
                part_ref[j, 1] = dv_s[:plen].astype(BF)

            @pl.when((one == j) & (two == j))
            def _():
                part_ref[j, 0] = ((first_s[0] + dk_s[:plen]) * scale).astype(BF)
                part_ref[j, 1] = (first_s[1] + dv_s[:plen]).astype(BF)


def attend(g, sel, lengths, q, dout, kvs, rk, rv, prev):
    rows, width = q.shape
    slots = sel.shape[0]
    rlen = rows // slots
    gw = width // (rk.shape[1] // HD)
    heads = gw // HD
    plen = kvs[0].shape[1]
    klen = plen + rlen
    wide = pl.BlockSpec((rlen, gw), lambda r, *_: (r, g))
    narrow = pl.BlockSpec((rlen, HD), lambda r, *_: (r, g))
    pair = pl.BlockSpec((2, plen, HD), lambda r, *_: (0, 0, 0))
    ins = [q, dout, *kvs, rk, rv]
    in_specs = [wide, wide] + [pair] * REACH + [narrow, narrow]
    aliases = {}
    if prev is not None:
        aliases = {2 + len(ins) + i: i for i in range(4)}
        ins += list(prev)
        in_specs += [pl.BlockSpec(memory_space=pl.ANY)] * 4
    return pl.pallas_call(
        functools.partial(attend_kernel, heads),
        out_shape=[jax.ShapeDtypeStruct(q.shape, BF)] * 2
        + [jax.ShapeDtypeStruct(rk.shape, BF)] * 2
        + [jax.ShapeDtypeStruct((REACH, 2, plen, HD), BF)],
        grid_spec=pltpu.PrefetchScalarGridSpec(
            num_scalar_prefetch=2,
            grid=(slots,),
            in_specs=in_specs,
            out_specs=[wide, wide, narrow, narrow]
            + [pl.BlockSpec((REACH, 2, plen, HD), lambda r, *_: (0, 0, 0, 0))],
            scratch_shapes=[pltpu.VMEM((klen, HD), BF)] * 2
            + [pltpu.VMEM((HD, klen), BF)] * 2
            + [pltpu.VMEM((klen, HD), F32)] * 2
            + [pltpu.VMEM((2, plen, HD), F32)],
        ),
        input_output_aliases=aliases,
        compiler_params=pltpu.CompilerParams(vmem_limit_bytes=40 * MIB),
        cost_estimate=pl.CostEstimate(
            flops=slots * heads * 24 * rlen * klen * HD,
            bytes_accessed=8 * MIB,
            transcendentals=slots * heads * rlen * klen,
        ),
        name=f"attend_{g}",
    )(sel, lengths, *ins)


def weight_kernel(side_ref, h_ref, grad_ref, keep_ref, send_ref, both):
    pairs, half = keep_ref.shape[:2]
    for j in range(2):
        both[:, j * HD : (j + 1) * HD] = mm(h_ref[...], grad_ref[j], TN).astype(BF)
    side = side_ref[0]
    for p in range(pairs):
        keep_ref[p] = both[pl.ds(pl.multiple_of((2 * p + side) * half, half), half), :]
        send_ref[p] = both[pl.ds(pl.multiple_of((2 * p + 1 - side) * half, half), half), :]


def weight_terms(side, hidden, grad, parts):
    rows, depth = hidden.shape
    chunk = depth // parts
    pairs = HD // math.gcd(2 * chunk, HD)
    tile = 2 * chunk * pairs
    out = jax.ShapeDtypeStruct((parts // 2, chunk, 2 * HD), BF)
    spec = pl.BlockSpec((pairs, chunk, 2 * HD), lambda i, *_: (i, 0, 0))
    return pl.pallas_call(
        weight_kernel,
        out_shape=[out, out],
        grid_spec=pltpu.PrefetchScalarGridSpec(
            num_scalar_prefetch=1,
            grid=(depth // tile,),
            in_specs=[
                pl.BlockSpec((rows, tile), lambda i, *_: (0, i)),
                pl.BlockSpec((2, rows, HD), lambda i, *_: (0, 0, 0)),
            ],
            out_specs=[spec, spec],
            scratch_shapes=[pltpu.VMEM((tile, 2 * HD), BF)],
        ),
        compiler_params=pltpu.CompilerParams(vmem_limit_bytes=32 * MIB),
        cost_estimate=pl.CostEstimate(
            flops=4 * rows * depth * HD,
            bytes_accessed=2 * depth * (rows + 2 * HD),
            transcendentals=0,
        ),
        name="weight_terms",
    )(side, hidden, grad)


def halve(keep, send, index, size):
    count = keep.shape[0]
    bit = 1
    held = keep.astype(F32) + permute(send, "dp", lambda i: i ^ 1).astype(F32)
    while count > 1:
        bit *= 2
        mine = (index // bit) % 2
        split = held.reshape(count // 2, 2, *held.shape[1:])
        out = lax.dynamic_index_in_dim(split, 1 - mine, 1, keepdims=False).astype(BF)
        stay = lax.dynamic_index_in_dim(split, mine, 1, keepdims=False)
        held = stay + permute(out, "dp", lambda i: i ^ bit).astype(F32)
        count //= 2
    return held[0]


def hidden_kernel(half_ref, own_ref, far_ref, wk_ref, wv_ref, wa_ref, wb_ref, out_ref):
    total = mm(own_ref[0], wk_ref[...], NT) + mm(own_ref[1], wv_ref[...], NT)
    total += mm(far_ref[0], wa_ref[...], NT) + mm(far_ref[1], wb_ref[...], NT)
    out_ref[...] = total.astype(BF)


def hidden_grads(half, own, far, w_key, w_value, far_a, far_b):
    rows, width = own.shape[1:]
    cols = far_a.shape[0]
    tile = 512
    whole = pl.BlockSpec((2, rows, width), lambda i, *_: (0, 0, 0))
    near = pl.BlockSpec((tile, width), lambda i, half: (half[0] * (cols // tile) + i, 0))
    away = pl.BlockSpec((tile, width), lambda i, *_: (i, 0))
    return pl.pallas_call(
        hidden_kernel,
        out_shape=jax.ShapeDtypeStruct((rows, cols), BF),
        grid_spec=pltpu.PrefetchScalarGridSpec(
            num_scalar_prefetch=1,
            grid=(cols // tile,),
            in_specs=[whole, whole, near, near, away, away],
            out_specs=pl.BlockSpec((rows, tile), lambda i, *_: (0, i)),
        ),
        compiler_params=pltpu.CompilerParams(vmem_limit_bytes=32 * MIB),
        cost_estimate=pl.CostEstimate(
            flops=8 * rows * cols * width,
            bytes_accessed=2 * cols * (rows + 4 * width),
            transcendentals=0,
        ),
        name="hidden_grads",
    )(half, own, far, w_key, w_value, far_a, far_b)


def body(
    prompt_hidden,
    w_key,
    w_value,
    queries,
    resp_key,
    resp_value,
    cotangent,
    group_offset,
    resp_length,
):
    size = lax.axis_size("dp")
    index = lax.axis_index("dp")
    core = index % 2
    half = lax.axis_index("mp")
    groups = w_key.shape[1] // HD
    cols = w_key.shape[0] // 2

    mine = jnp.where(
        core == 0,
        lax.dynamic_slice_in_dim(w_key, (1 - half) * cols, cols, 0),
        lax.dynamic_slice_in_dim(w_value, (1 - half) * cols, cols, 0),
    )
    far_a = permute(mine, "mp", lambda i: 1 - i)
    far_b = permute(far_a, "dp", lambda i: i ^ 1)

    def other(i):
        return (i + 1) % size if i % 2 == 0 else (i + 3) % size

    def back(i):
        return (i - 1) % size if i % 2 == 1 else (i - 3) % size

    sel = jnp.where((group_offset % 2 == 1) & (core == 0), 4 - group_offset, group_offset)

    pairs = project(prompt_hidden, w_key, w_value)
    received = []
    for pair in pairs:
        two = permute(pair, "dp", lambda i: (i + 2) % size)
        one = permute(pair, "dp", other)
        three = permute(two, "dp", lambda i: i ^ 1)
        received.append([pair, one, two, three])

    prev = None
    owns = []
    fars = []
    terms = []
    for g in range(groups):
        *prev, part = attend(
            g, sel, resp_length, queries, cotangent, received[g], resp_key, resp_value, prev
        )
        swapped = permute(part[3], "dp", lambda i: i ^ 1)
        from_other = permute(part[1], "dp", back)
        two = (part[2].astype(F32) + swapped.astype(F32)).astype(BF)
        from_two = permute(two, "dp", lambda i: (i - 2) % size)
        grad = (part[0].astype(F32) + from_other.astype(F32) + from_two.astype(F32)).astype(BF)
        owns.append(grad)
        fars.append(permute(grad, "mp", lambda i: 1 - i))
        keep, send = weight_terms(core.reshape(1), prompt_hidden, grad, size)
        terms.append(halve(keep, send, index, size))
    own = jnp.concatenate(owns, axis=-1)
    far = jnp.concatenate(fars, axis=-1)
    far = jnp.where(core == 0, far, far[::-1])
    hidden_grad = hidden_grads(half.reshape(1), own, far, w_key, w_value, far_a, far_b)
    return (
        *prev,
        hidden_grad,
        jnp.concatenate([t[:, :HD] for t in terms], axis=-1),
        jnp.concatenate([t[:, HD:] for t in terms], axis=-1),
    )


def solution(mesh):
    placed = (
        P("dp", None),
        P(None, "mp"),
        P(None, "mp"),
        P("dp", "mp"),
        P("dp", "mp"),
        P("dp", "mp"),
        P("dp", "mp"),
        P("dp"),
        P("dp"),
    )
    return jax.shard_map(
        body,
        mesh=mesh,
        in_specs=placed,
        out_specs=(P("dp", "mp"),) * 7,
        check_vma=False,
    )
```

time: 450 us -> 178 us (0.40); the launches traced: 445 us -> 178 us
  matrix products: 159 us -> 0 us
  waiting for transfers between devices: 174 us -> 71.3 us
  Pallas kernels: 0 us -> 65.3 us
  local copies, waits for them, and re-layouts: 63.4 us -> 14.6 us
  between operations: 20.7 us -> 1 us
  other arithmetic: 18.4 us -> 6.71 us
  starting transfers between devices: 9.98 us -> 19 us
    dot_general x15 -> x0, matrix products: 139 us -> none  [the longest x2 40.6 us: attend(): jnp.einsum('gnqk,kgd->qgnd', score_grad, key_heads, preferred_element_typ...]
    unnamed x3 -> x0, waiting for transfers between devices: 118 us -> none
    pallas_call x0 -> x6, Pallas kernels: none -> 65.3 us  [the longest x2 40.2 us: attend(): pl.pallas_call(functools.partial(attend_kernel, heads), out_shape=[jax.Sh...]
    slice x19 -> x2, local copies, waits for them, and re-layouts: 21.2 us -> 0.05 us  [body(): t[:, HD:]]
    sub x2 -> x0, matrix products: 20.1 us -> none  [attend(): shifted = jnp.exp(scores - peak_score)]
    dot_general x1 -> x0, local copies, waits for them, and re-layouts: 16.1 us -> none  [body(): jnp.einsum('pd,spk->dsk', prompt_hidden, grads_bf, preferred_element_type...]
    ppermute x6 -> x24, waiting for transfers between devices: 55.4 us -> 71.3 us  [permute(): lax.ppermute(block, axis, [(i, target(i)) for i in range(lax.axis_size(ax...]
    convert_element_type x8 -> x6, local copies, waits for them, and re-layouts: 11.2 us -> 0.29 us  [halve(): lax.dynamic_index_in_dim(split, 1 - mine, 1, keepdims=False).astype(BF)]
  transfers between devices with their start and end apart: 8 -> 24, of which waited for: 4 -> 12; matrix products, arithmetic and copies ran while one was open for 25% -> 4% of each run, Pallas kernels for 0% -> 33%
where the time goes in v1:
time: 178 us
  waiting for transfers between devices  71.3 us (40%)
  Pallas kernels  65.3 us (37%)
  starting transfers between devices  19 us (11%)
  local copies, waits for them, and re-layouts  14.6 us (8%)
  other arithmetic  6.71 us (4%)
    ppermute x24, waiting for transfers between devices, permute(): lax.ppermute(block, axis, [(i, target(i)) for i in range(lax.axis_size(ax...  71.3 us
    pallas_call x2, Pallas kernels, attend(): pl.pallas_call(functools.partial(attend_kernel, heads), out_shape=[jax.Sh...  40.2 us
    ppermute x24, starting transfers between devices, permute(): lax.ppermute(block, axis, [(i, target(i)) for i in range(lax.axis_size(ax...  19 us
    unnamed x47, local copies, waits for them, and re-layouts  14.1 us
    pallas_call x2, Pallas kernels, weight_terms(): pl.pallas_call(weight_kernel, out_shape=[out, out], grid_spec=pltpu.Prefe...  12 us
    pallas_call x1, Pallas kernels, project(): pl.pallas_call(project_kernel, out_shape=[jax.ShapeDtypeStruct((2, rows,...  6.81 us
    pallas_call x1, Pallas kernels, hidden_grads(): pl.pallas_call(hidden_kernel, out_shape=jax.ShapeDtypeStruct((rows, cols)...  6.28 us
  transfers between devices with their start and end apart: 24, of which 12 were waited for; matrix products, arithmetic and copies ran while one was open for 4% of the time, Pallas kernels for 33%

profile of v1, /device:TPU:0, one launch (start us, length us, event | category | flops | bytes accessed | tf_op | source)
XLA Modules:
  0.0 177.9 jit_solution(10337623727604159250)
XLA Ops:
  0.6 2.5 %copy-done = bf16[512,5120]{1,0:T(8,128)(2,1)S(1)} copy-done((bf16[512,5120]{1,0:T(8,128)(2,1)S(1)}, bf16[512,5120]{1,0:T(8,128)(2,1)}, u32[]{:S(2)}) %copy-start) | copy-done | bytes 5242904
  3.1 1.7 copy-done.1
  4.9 1.7 copy-done.3
  6.6 6.8 %project.1 = (bf16[2,512,128]{2,1,0:T(8,128)(2,1)}, bf16[2,512,128]{2,1,0:T(8,128)(2,1)S(1)}) custom-call(bf16[512,5120]{1,0:T(8,128)(2,1)S(1)} %copy-done, bf16[5120,256]{1,0:T(8,128)(2,1)S(1)} %copy-done.1, bf16[5120,256]{1,0:T(8,128)(2,1)S(1)} %copy-done.3), custom_call_target="tpu_custom_call" | custom-call | flops 2684354560 | bytes 10485760 | tf_op jit(solution)/shard_map/project/pallas_call | solution.py:59
  13.4 2.9 %collective-permute-start.4 = (bf16[2,512,128]{2,1,0:T(8,128)(2,1)}, bf16[2,512,128]{2,1,0:T(8,128)(2,1)}, u32[]{:S(2)}, u32[]{:S(2)}) collective-permute-start(bf16[2,512,128]{2,1,0:T(8,128)(2,1)} %get-tuple-element.24.rest_0_), channel_id=1, source_target_pairs={{0,4},{2,6},{4,8},{6,10},{8,12},{10,14},{12,16},{14,18},{16,20},{1... | collective-permute-start | bytes 786440 | tf_op jit(solution)/shard_map/ppermute | solution.py:27
  16.4 1.5 collective-permute-start.1
  17.9 8.9 %collective-permute-done.4.rest_2_ = bf16[2,512,128]{2,1,0:T(8,128)(2,1)} collective-permute-done((bf16[2,512,128]{2,1,0:T(8,128)(2,1)}, bf16[2,512,128]{2,1,0:T(8,128)(2,1)}, u32[]{:S(2)}, u32[]{:S(2)}) %collective-permute-start.4) | collective-permute-done | bytes 262176 | tf_op jit(solution)/shard_map/ppermute | solution.py:27
  26.9 0.5 collective-permute-start
  27.4 5.0 %collective-permute-done.1.rest_2_ = bf16[2,512,128]{2,1,0:T(8,128)(2,1)S(1)} collective-permute-done((bf16[2,512,128]{2,1,0:T(8,128)(2,1)S(1)}, bf16[2,512,128]{2,1,0:T(8,128)(2,1)S(1)}, u32[]{:S(2)}, u32[]{:S(2)}) %collective-permute-start.1) | collective-permute-done | bytes 262176 | tf_op jit(solution)/shard_map/ppermute | solution.py:27
  32.4 1.6 copy-done.12
  34.1 20.7 %attend_0.1 = (bf16[512,2048]{1,0:T(8,128)(2,1)}, bf16[512,2048]{1,0:T(8,128)(2,1)}, bf16[512,256]{1,0:T(8,128)(2,1)}, bf16[512,256]{1,0:T(8,128)(2,1)}, bf16[4,2,512,128]{3,2,1,0:T(8,128)(2,1)S(1)}) custom-call(s32[2]{0:T(128)S(1)} %and_select_fusion.sel_ref, s32[2]{0:T(128)S(1)} %copy-done.19, bf16[512,2048]{1,0:T(8,128)(2,1)S(1)} %copy-done.10, ...), custom_call_target="tpu_custom_call" | custom-call | flops 9663676416 | bytes 8388608 | tf_op jit(solution)/shard_map/attend_0/pallas_call | solution.py:179
  54.8 0.5 collective-permute-start.7
  55.3 1.9 %collective-permute-start.6 = (bf16[2,512,128]{2,1,0:T(8,128)(2,1)S(1)}, bf16[2,512,128]{2,1,0:T(8,128)(2,1)S(1)}, u32[]{:S(2)}, u32[]{:S(2)}) collective-permute-start(bf16[2,512,128]{2,1,0:T(8,128)(2,1)S(1)} %get-tuple-element.39), channel_id=1, source_target_pairs={{0,26},{2,0},{4,30},{6,4},{8,2},{10,8},{12,6},{14,12},{16,10},{18,... | collective-permute-start | bytes 786440 | tf_op jit(solution)/shard_map/ppermute | solution.py:27
  57.2 0.7 copy-done.17
  57.9 0.9 copy-done.16
  58.8 0.9 copy-done.18
  59.8 19.6 %attend_1.1 = (bf16[512,2048]{1,0:T(8,128)(2,1)}, bf16[512,2048]{1,0:T(8,128)(2,1)}, bf16[512,256]{1,0:T(8,128)(2,1)}, bf16[512,256]{1,0:T(8,128)(2,1)}, bf16[4,2,512,128]{3,2,1,0:T(8,128)(2,1)S(1)}) custom-call(s32[2]{0:T(128)S(1)} %and_select_fusion.sel_ref, ...), custom_call_target="tpu_custom_call", output_to_operand_aliasing={{0}: (10, {}), {1}: (11, {}), {2}: (12, {}), {3}: (13, {})} | custom-call | flops 9663676416 | bytes 8388608 | tf_op jit(solution)/shard_map/attend_1/pallas_call | solution.py:179
  79.4 0.1 collective-permute-start.10
  79.5 0.1 fusion.5
  79.6 2.2 %collective-permute-start.8 = (bf16[2,512,128]{2,1,0:T(8,128)(2,1)S(1)}, bf16[2,512,128]{2,1,0:T(8,128)(2,1)S(1)}, u32[]{:S(2)}, u32[]{:S(2)}) collective-permute-start(bf16[2,512,128]{2,1,0:T(8,128)(2,1)S(1)} %fusion.5), channel_id=1, source_target_pairs={{0,28},{2,30},{4,0},{6,2},{8,4},{10,6},{12,8},{14,10},{16,12},{18,... | collective-permute-start | bytes 786440 | tf_op jit(solution)/shard_map/ppermute | solution.py:27
  81.8 1.4 dynamic-slice_select_fusion
  83.2 1.5 collective-permute-start.14
  84.8 0.1 fusion.2
  84.8 0.4 collective-permute-start.11
  85.2 3.7 %collective-permute-done.8 = bf16[2,512,128]{2,1,0:T(8,128)(2,1)S(1)} collective-permute-done((bf16[2,512,128]{2,1,0:T(8,128)(2,1)S(1)}, bf16[2,512,128]{2,1,0:T(8,128)(2,1)S(1)}, u32[]{:S(2)}, u32[]{:S(2)}) %collective-permute-start.8) | collective-permute-done | bytes 262176 | tf_op jit(solution)/shard_map/ppermute | solution.py:27
  88.9 0.1 fusion.7.grad_ref
  89.0 6.0 %weight_terms.2 = (bf16[8,320,256]{2,1,0:T(8,128)(2,1)S(1)}, bf16[8,320,256]{2,1,0:T(8,128)(2,1)}) custom-call(s32[1]{0:T(128)} %bitcast.9.side_ref, bf16[512,5120]{1,0:T(8,128)(2,1)S(1)} %bitcast.59, bf16[2,512,128]{2,1,0:T(8,128)(2,1)S(1)} %fusion.7.grad_ref), custom_call_target="tpu_custom_call" | custom-call | flops 1342177280 | bytes 7864320 | tf_op jit(solution)/shard_map/weight_terms/pallas_call | solution.py:223
  95.0 1.1 copy-done.6
  96.1 0.2 collective-permute-done.11
  96.3 0.1 fusion.4.grad_ref
  96.4 6.0 %weight_terms.3 = (bf16[8,320,256]{2,1,0:T(8,128)(2,1)S(1)}, bf16[8,320,256]{2,1,0:T(8,128)(2,1)}) custom-call(s32[1]{0:T(128)} %bitcast.9.side_ref, bf16[512,5120]{1,0:T(8,128)(2,1)S(1)} %bitcast.59, bf16[2,512,128]{2,1,0:T(8,128)(2,1)S(1)} %fusion.4.grad_ref), custom_call_target="tpu_custom_call" | custom-call | flops 1342177280 | bytes 7864320 | tf_op jit(solution)/shard_map/weight_terms/pallas_call | solution.py:223
  102.4 1.1 copy-done.8
  103.5 0.4 collective-permute-start.20
  103.8 1.5 collective-permute-start.12
  105.4 0.5 collective-permute-start.13
  105.9 0.1 pad_maximum_fusion.own_ref
  105.9 9.3 %collective-permute-done.14.wa_ref = bf16[2560,256]{1,0:T(8,128)(2,1)} collective-permute-done((bf16[2560,256]{1,0:T(8,128)(2,1)}, bf16[2560,256]{1,0:T(8,128)(2,1)}, u32[]{:S(2)}, u32[]{:S(2)}) %collective-permute-start.14) | collective-permute-done | bytes 1310752 | tf_op jit(solution)/shard_map/ppermute | solution.py:27
  115.2 5.6 %collective-permute-done.12 = bf16[2,512,128]{2,1,0:T(8,128)(2,1)} collective-permute-done((bf16[2,512,128]{2,1,0:T(8,128)(2,1)S(1)}, bf16[2,512,128]{2,1,0:T(8,128)(2,1)}, u32[]{:S(2)}, u32[]{:S(2)}) %collective-permute-start.12) | collective-permute-done | bytes 262176 | tf_op jit(solution)/shard_map/ppermute | solution.py:27
  120.8 1.0 constant_dynamic-update-slice_fusion.1
  121.8 3.6 %collective-permute-done.13 = bf16[2,512,128]{2,1,0:T(8,128)(2,1)S(1)} collective-permute-done((bf16[2,512,128]{2,1,0:T(8,128)(2,1)S(1)}, bf16[2,512,128]{2,1,0:T(8,128)(2,1)S(1)}, u32[]{:S(2)}, u32[]{:S(2)}) %collective-permute-start.13) | collective-permute-done | bytes 262176 | tf_op jit(solution)/shard_map/ppermute | solution.py:27
  125.4 0.1 constant_dynamic-update-slice_fusion
  125.5 1.6 convert_add_fusion.1
  127.1 0.1 fusion.1
  127.2 0.5 collective-permute-start.17
  127.7 0.7 copy-done.9
  128.4 1.8 convert_add_fusion
  130.2 0.1 fusion
  130.3 0.9 collective-permute-start.21
  131.2 0.1 reverse_select_fusion.far_ref
  131.3 6.3 %hidden_grads.1 = bf16[512,2560]{1,0:T(8,128)(2,1)} custom-call(s32[1]{0:T(128)} %bitcast.half_ref, bf16[2,512,256]{2,1,0:T(8,128)(2,1)S(1)} %pad_maximum_fusion.own_ref, bf16[2,512,256]{2,1,0:T(8,128)(2,1)S(1)} %reverse_select_fusion.far_ref, bf16[5120,256]{1,0:T(8,128)(2,1)S(1)} %copy-done.2, bf16[5120,256]{1,0:T(8,128)(2,1)S(1)} %copy-done.5, ...), custom_call_target="tpu_custom_call" | custom-call | flops 2684354560 | bytes 7864320 | tf_op jit(solution)/shard_map/hidden_grads/pallas_call | solution.py:274
  137.6 7.3 %collective-permute-done.17 = bf16[4,320,256]{2,1,0:T(8,128)(2,1)S(1)} collective-permute-done((bf16[4,320,256]{2,1,0:T(8,128)(2,1)S(1)}, bf16[4,320,256]{2,1,0:T(8,128)(2,1)S(1)}, u32[]{:S(2)}, u32[]{:S(2)}) %collective-permute-start.17) | collective-permute-done | bytes 655392 | tf_op jit(solution)/shard_map/ppermute | solution.py:27
  144.9 0.1 bitcast_add_fusion.1
  145.1 1.7 collective-permute-start.18
  146.8 10.4 %collective-permute-done.21 = bf16[4,320,256]{2,1,0:T(8,128)(2,1)S(1)} collective-permute-done((bf16[4,320,256]{2,1,0:T(8,128)(2,1)S(1)}, bf16[4,320,256]{2,1,0:T(8,128)(2,1)S(1)}, u32[]{:S(2)}, u32[]{:S(2)}) %collective-permute-start.21) | collective-permute-done | bytes 655392 | tf_op jit(solution)/shard_map/ppermute | solution.py:27
  157.1 0.2 bitcast_add_fusion
  157.3 1.9 %collective-permute-start.22 = (bf16[2,320,256]{2,1,0:T(8,128)(2,1)S(1)}, bf16[2,320,256]{2,1,0:T(8,128)(2,1)S(1)}, u32[]{:S(2)}, u32[]{:S(2)}) collective-permute-start(bf16[2,320,256]{2,1,0:T(8,128)(2,1)S(1)} %fusion.9), channel_id=1, source_target_pairs={{0,8},{2,10},{4,12},{6,14},{8,0},{10,2},{12,4},{14,6},{16,24},{18,... | collective-permute-start | bytes 983048 | tf_op jit(solution)/shard_map/ppermute | solution.py:27
  159.2 0.1 bitcast_add_fusion.3
  159.3 0.1 collective-permute-start.19
  159.4 9.7 %collective-permute-done.22 = bf16[2,320,256]{2,1,0:T(8,128)(2,1)S(1)} collective-permute-done((bf16[2,320,256]{2,1,0:T(8,128)(2,1)S(1)}, bf16[2,320,256]{2,1,0:T(8,128)(2,1)S(1)}, u32[]{:S(2)}, u32[]{:S(2)}) %collective-permute-start.22) | collective-permute-done | bytes 327712 | tf_op jit(solution)/shard_map/ppermute | solution.py:27
  169.0 0.1 bitcast_add_fusion.2
  169.1 0.1 collective-permute-start.23
  169.2 0.9 collective-permute-done.19
  170.2 6.8 %collective-permute-done.23 = bf16[1,320,256]{2,1,0:T(8,128)(2,1)S(1)} collective-permute-done((bf16[1,320,256]{2,1,0:T(8,128)(2,1)S(1)}, bf16[1,320,256]{2,1,0:T(8,128)(2,1)S(1)}, u32[]{:S(2)}, u32[]{:S(2)}) %collective-permute-start.23) | collective-permute-done | bytes 163872 | tf_op jit(solution)/shard_map/ppermute | solution.py:27
  177.0 0.9 pad_maximum_fusion.1
  (66 shorter events, 0.5 us)
Async XLA Ops:
  0.6 2.5 %copy-start = (bf16[512,5120]{1,0:T(8,128)(2,1)S(1)}, bf16[512,5120]{1,0:T(8,128)(2,1)}, u32[]{:S(2)}) copy-start(bf16[512,5120]{1,0:T(8,128)(2,1)} %h_ref.5) | copy-start | bytes 15728644
  3.1 1.7 copy-start.1
  4.9 1.7 copy-start.3
  6.6 20.8 %copy-start.20 = (s32[2]{0:T(128)S(1)}, s32[2]{0:T(128)}, u32[]{:S(2)}) copy-start(s32[2]{0:T(128)} %param.16) | copy-start | bytes 28
  6.6 25.8 %copy-start.10 = (bf16[512,2048]{1,0:T(8,128)(2,1)S(1)}, bf16[512,2048]{1,0:T(8,128)(2,1)}, u32[]{:S(2)}) copy-start(bf16[512,2048]{1,0:T(8,128)(2,1)} %q_ref.3) | copy-start | bytes 6291460
  6.6 25.8 %copy-start.13 = (bf16[512,256]{1,0:T(8,128)(2,1)S(1)}, bf16[512,256]{1,0:T(8,128)(2,1)}, u32[]{:S(2)}) copy-start(bf16[512,256]{1,0:T(8,128)(2,1)} %rest_4_.3) | copy-start | bytes 786436
  6.6 25.8 %copy-start.14 = (bf16[512,256]{1,0:T(8,128)(2,1)S(1)}, bf16[512,256]{1,0:T(8,128)(2,1)}, u32[]{:S(2)}) copy-start(bf16[512,256]{1,0:T(8,128)(2,1)} %rest_5_.3) | copy-start | bytes 786436
  6.6 25.8 %copy-start.19 = (s32[2]{0:T(128)S(1)}, s32[2]{0:T(128)}, u32[]{:S(2)}) copy-start(s32[2]{0:T(128)} %len_ref.3) | copy-start | bytes 28
  13.4 13.4 %collective-permute-start.4 = (bf16[2,512,128]{2,1,0:T(8,128)(2,1)}, bf16[2,512,128]{2,1,0:T(8,128)(2,1)}, u32[]{:S(2)}, u32[]{:S(2)}) collective-permute-start(bf16[2,512,128]{2,1,0:T(8,128)(2,1)} %get-tuple-element.24.rest_0_), channel_id=1, source_target_pairs={{0,4},{2,6},{4,8},{6,10},{8,12},{10,14},{12,16},{14,18},{16,20},{1... | collective-permute-start | bytes 786440 | tf_op jit(solution)/shard_map/ppermute | solution.py:27
  16.4 16.0 %collective-permute-start.1 = (bf16[2,512,128]{2,1,0:T(8,128)(2,1)S(1)}, bf16[2,512,128]{2,1,0:T(8,128)(2,1)S(1)}, u32[]{:S(2)}, u32[]{:S(2)}) collective-permute-start(bf16[2,512,128]{2,1,0:T(8,128)(2,1)S(1)} %get-tuple-element.23.rest_0_), channel_id=1, source_target_pairs={{0,4},{2,6},{4,8},{6,10},{8,12},{10,14},{12,16},{14,18},{16,20},{1... | collective-permute-start | bytes 786440 | tf_op jit(solution)/shard_map/ppermute | solution.py:27
  17.9 14.5 %collective-permute-start.3 = (bf16[2,512,128]{2,1,0:T(8,128)(2,1)}, bf16[2,512,128]{2,1,0:T(8,128)(2,1)}, u32[]{:S(2)}, u32[]{:S(2)}) collective-permute-start(bf16[2,512,128]{2,1,0:T(8,128)(2,1)} %get-tuple-element.24.rest_0_), channel_id=1, source_target_pairs={{0,2},{2,8},{4,6},{6,12},{8,10},{10,16},{12,14},{14,20},{16,18},{1... | collective-permute-start | bytes 786440 | tf_op jit(solution)/shard_map/ppermute | solution.py:27
  26.9 5.5 %collective-permute-start.5 = (bf16[2,512,128]{2,1,0:T(8,128)(2,1)}, bf16[2,512,128]{2,1,0:T(8,128)(2,1)}, u32[]{:S(2)}, u32[]{:S(2)}) collective-permute-start(bf16[2,512,128]{2,1,0:T(8,128)(2,1)} %collective-permute-done.4.rest_2_), channel_id=1, source_target_pairs={{0,2},{2,0},{4,6},{6,4},{8,10},{10,8},{12,14},{14,12},{16,18},{18,... | collective-permute-start | bytes 786440 | tf_op jit(solution)/shard_map/ppermute | solution.py:27
  26.9 30.3 %collective-permute-start = (bf16[2,512,128]{2,1,0:T(8,128)(2,1)S(1)}, bf16[2,512,128]{2,1,0:T(8,128)(2,1)S(1)}, u32[]{:S(2)}, u32[]{:S(2)}) collective-permute-start(bf16[2,512,128]{2,1,0:T(8,128)(2,1)S(1)} %get-tuple-element.23.rest_0_), channel_id=1, source_target_pairs={{0,2},{2,8},{4,6},{6,12},{8,10},{10,16},{12,14},{14,20},{16,18},{1... | collective-permute-start | bytes 786440 | tf_op jit(solution)/shard_map/ppermute | solution.py:27
  27.4 30.5 %copy-start.11 = (bf16[512,2048]{1,0:T(8,128)(2,1)S(1)}, bf16[512,2048]{1,0:T(8,128)(2,1)}, u32[]{:S(2)}) copy-start(bf16[512,2048]{1,0:T(8,128)(2,1)} %q_ref.3) | copy-start | bytes 6291460
  32.4 22.4 %copy-start.15 = (bf16[2,512,128]{2,1,0:T(8,128)(2,1)}, bf16[2,512,128]{2,1,0:T(8,128)(2,1)S(1)}, u32[]{:S(2)}) copy-start(bf16[2,512,128]{2,1,0:T(8,128)(2,1)S(1)} %collective-permute-done.1.rest_2_) | copy-start | bytes 786436
  32.4 25.5 %collective-permute-start.2 = (bf16[2,512,128]{2,1,0:T(8,128)(2,1)S(1)}, bf16[2,512,128]{2,1,0:T(8,128)(2,1)S(1)}, u32[]{:S(2)}, u32[]{:S(2)}) collective-permute-start(bf16[2,512,128]{2,1,0:T(8,128)(2,1)S(1)} %collective-permute-done.1.rest_2_), channel_id=1, source_target_pairs={{0,2},{2,0},{4,6},{6,4},{8,10},{10,8},{12,14},{14,12},{16,18},{18,... | collective-permute-start | bytes 786440 | tf_op jit(solution)/shard_map/ppermute | solution.py:27
  32.4 1.6 copy-start.12
  54.7 34.3 %slice-start = ((s8[5242880]{0:T(1024)(128)(4,1)}), s8[4194304]{0:T(1024)(128)(4,1)S(1)}, s32[]{:S(2)}) async-start(s8[5242880]{0:T(1024)(128)(4,1)} %bitcast.58), calls=%async_computation | async-start | bytes 8388608
  54.8 24.7 %collective-permute-start.7 = (bf16[2,512,128]{2,1,0:T(8,128)(2,1)S(1)}, bf16[2,512,128]{2,1,0:T(8,128)(2,1)S(1)}, u32[]{:S(2)}, u32[]{:S(2)}) collective-permute-start(bf16[2,512,128]{2,1,0:T(8,128)(2,1)S(1)} %get-tuple-element.40), channel_id=1, source_target_pairs={{0,2},{2,0},{4,6},{6,4},{8,10},{10,8},{12,14},{14,12},{16,18},{18,... | collective-permute-start | bytes 786440 | tf_op jit(solution)/shard_map/ppermute | solution.py:27
  55.3 29.9 %collective-permute-start.6 = (bf16[2,512,128]{2,1,0:T(8,128)(2,1)S(1)}, bf16[2,512,128]{2,1,0:T(8,128)(2,1)S(1)}, u32[]{:S(2)}, u32[]{:S(2)}) collective-permute-start(bf16[2,512,128]{2,1,0:T(8,128)(2,1)S(1)} %get-tuple-element.39), channel_id=1, source_target_pairs={{0,26},{2,0},{4,30},{6,4},{8,2},{10,8},{12,6},{14,12},{16,10},{18,... | collective-permute-start | bytes 786440 | tf_op jit(solution)/shard_map/ppermute | solution.py:27
  57.2 0.7 copy-start.17
  57.9 1.0 copy-start.16
  58.8 0.9 copy-start.18
  59.8 22.0 %copy-start.2 = (bf16[5120,256]{1,0:T(8,128)(2,1)S(1)}, bf16[5120,256]{1,0:T(8,128)(2,1)}, u32[]{:S(2)}) copy-start(bf16[5120,256]{1,0:T(8,128)(2,1)} %wk_ref.3) | copy-start | bytes 7864324
  59.8 22.0 %copy-start.4 = (bf16[5120,256]{1,0:T(8,128)(2,1)S(1)}, bf16[5120,256]{1,0:T(8,128)(2,1)}, u32[]{:S(2)}) copy-start(bf16[5120,256]{1,0:T(8,128)(2,1)} %wv_ref.3) | copy-start | bytes 7864324
  59.8 29.2 %slice-start.1 = ((s8[5242880]{0:T(1024)(128)(4,1)}), s8[1048576]{0:T(1024)(128)(4,1)S(1)}, s32[]{:S(2)}) async-start(s8[5242880]{0:T(1024)(128)(4,1)} %bitcast.58), calls=%async_computation.1 | async-start | bytes 2097152
  79.4 5.3 %collective-permute-start.10 = (bf16[2,512,128]{2,1,0:T(8,128)(2,1)S(1)}, bf16[2,512,128]{2,1,0:T(8,128)(2,1)S(1)}, u32[]{:S(2)}, u32[]{:S(2)}) collective-permute-start(bf16[2,512,128]{2,1,0:T(8,128)(2,1)S(1)} %get-tuple-element.42), channel_id=1, source_target_pairs={{0,2},{2,0},{4,6},{6,4},{8,10},{10,8},{12,14},{14,12},{16,18},{18,... | collective-permute-start | bytes 786440 | tf_op jit(solution)/shard_map/ppermute | solution.py:27
  79.6 9.3 %collective-permute-start.8 = (bf16[2,512,128]{2,1,0:T(8,128)(2,1)S(1)}, bf16[2,512,128]{2,1,0:T(8,128)(2,1)S(1)}, u32[]{:S(2)}, u32[]{:S(2)}) collective-permute-start(bf16[2,512,128]{2,1,0:T(8,128)(2,1)S(1)} %fusion.5), channel_id=1, source_target_pairs={{0,28},{2,30},{4,0},{6,2},{8,4},{10,6},{12,8},{14,10},{16,12},{18,... | collective-permute-start | bytes 786440 | tf_op jit(solution)/shard_map/ppermute | solution.py:27
  83.2 32.0 %collective-permute-start.14 = (bf16[2560,256]{1,0:T(8,128)(2,1)}, bf16[2560,256]{1,0:T(8,128)(2,1)}, u32[]{:S(2)}, u32[]{:S(2)}) collective-permute-start(bf16[2560,256]{1,0:T(8,128)(2,1)} %dynamic-slice_select_fusion), channel_id=1, source_target_pairs={{0,1},{1,0},{2,3},{3,2},{4,5},{5,4},{6,7},{7,6},{8,9},{9,8},{10,11... | collective-permute-start | bytes 3932168 | tf_op jit(solution)/shard_map/ppermute | solution.py:27
  84.7 11.4 %collective-permute-start.9 = (bf16[2,512,128]{2,1,0:T(8,128)(2,1)S(1)}, bf16[2,512,128]{2,1,0:T(8,128)(2,1)S(1)}, u32[]{:S(2)}, u32[]{:S(2)}) collective-permute-start(bf16[2,512,128]{2,1,0:T(8,128)(2,1)S(1)} %get-tuple-element.41), channel_id=1, source_target_pairs={{0,26},{2,0},{4,30},{6,4},{8,2},{10,8},{12,6},{14,12},{16,10},{18,... | collective-permute-start | bytes 786440 | tf_op jit(solution)/shard_map/ppermute | solution.py:27
  84.8 11.4 %collective-permute-start.11 = (bf16[2,512,128]{2,1,0:T(8,128)(2,1)S(1)}, bf16[2,512,128]{2,1,0:T(8,128)(2,1)S(1)}, u32[]{:S(2)}, u32[]{:S(2)}) collective-permute-start(bf16[2,512,128]{2,1,0:T(8,128)(2,1)S(1)} %fusion.2), channel_id=1, source_target_pairs={{0,28},{2,30},{4,0},{6,2},{8,4},{10,6},{12,8},{14,10},{16,12},{18,... | collective-permute-start | bytes 786440 | tf_op jit(solution)/shard_map/ppermute | solution.py:27
  95.0 1.1 copy-start.6
  96.1 29.4 %collective-permute-start.16 = (bf16[8,320,256]{2,1,0:T(8,128)(2,1)}, bf16[8,320,256]{2,1,0:T(8,128)(2,1)}, u32[]{:S(2)}, u32[]{:S(2)}) collective-permute-start(bf16[8,320,256]{2,1,0:T(8,128)(2,1)} %get-tuple-element.36), channel_id=1, source_target_pairs={{0,2},{2,0},{4,6},{6,4},{8,10},{10,8},{12,14},{14,12},{16,18},{18,... | collective-permute-start | bytes 3932168 | tf_op jit(solution)/shard_map/ppermute | solution.py:27
  102.3 1.1 copy-start.8
  103.5 24.2 %collective-permute-start.20 = (bf16[8,320,256]{2,1,0:T(8,128)(2,1)}, bf16[8,320,256]{2,1,0:T(8,128)(2,1)}, u32[]{:S(2)}, u32[]{:S(2)}) collective-permute-start(bf16[8,320,256]{2,1,0:T(8,128)(2,1)} %get-tuple-element.38), channel_id=1, source_target_pairs={{0,2},{2,0},{4,6},{6,4},{8,10},{10,8},{12,14},{14,12},{16,18},{18,... | collective-permute-start | bytes 3932168 | tf_op jit(solution)/shard_map/ppermute | solution.py:27
  103.8 17.0 %collective-permute-start.12 = (bf16[2,512,128]{2,1,0:T(8,128)(2,1)S(1)}, bf16[2,512,128]{2,1,0:T(8,128)(2,1)}, u32[]{:S(2)}, u32[]{:S(2)}) collective-permute-start(bf16[2,512,128]{2,1,0:T(8,128)(2,1)S(1)} %fusion.7.grad_ref), channel_id=1, source_target_pairs={{0,1},{1,0},{2,3},{3,2},{4,5},{5,4},{6,7},{7,6},{8,9},{9,8},{10,11... | collective-permute-start | bytes 786440 | tf_op jit(solution)/shard_map/ppermute | solution.py:27
  105.4 20.0 %collective-permute-start.13 = (bf16[2,512,128]{2,1,0:T(8,128)(2,1)S(1)}, bf16[2,512,128]{2,1,0:T(8,128)(2,1)S(1)}, u32[]{:S(2)}, u32[]{:S(2)}) collective-permute-start(bf16[2,512,128]{2,1,0:T(8,128)(2,1)S(1)} %fusion.4.grad_ref), channel_id=1, source_target_pairs={{0,1},{1,0},{2,3},{3,2},{4,5},{5,4},{6,7},{7,6},{8,9},{9,8},{10,11... | collective-permute-start | bytes 786440 | tf_op jit(solution)/shard_map/ppermute | solution.py:27
  105.8 19.6 %copy-start.7 = (bf16[8,320,256]{2,1,0:T(8,128)(2,1)S(1)}, bf16[8,320,256]{2,1,0:T(8,128)(2,1)}, u32[]{:S(2)}) copy-start(bf16[8,320,256]{2,1,0:T(8,128)(2,1)} %copy-done.6) | copy-start | bytes 3932164
  115.2 16.1 %collective-permute-start.15 = (bf16[2560,256]{1,0:T(8,128)(2,1)}, bf16[2560,256]{1,0:T(8,128)(2,1)S(1)}, u32[]{:S(2)}, u32[]{:S(2)}) collective-permute-start(bf16[2560,256]{1,0:T(8,128)(2,1)} %collective-permute-done.14.wa_ref), channel_id=1, source_target_pairs={{0,2},{2,0},{4,6},{6,4},{8,10},{10,8},{12,14},{14,12},{16,18},{18,... | collective-permute-start | bytes 3932168 | tf_op jit(solution)/shard_map/ppermute | solution.py:27
  127.1 1.3 copy-start.9
  127.2 17.7 %collective-permute-start.17 = (bf16[4,320,256]{2,1,0:T(8,128)(2,1)S(1)}, bf16[4,320,256]{2,1,0:T(8,128)(2,1)S(1)}, u32[]{:S(2)}, u32[]{:S(2)}) collective-permute-start(bf16[4,320,256]{2,1,0:T(8,128)(2,1)S(1)} %fusion.1), channel_id=1, source_target_pairs={{0,4},{2,6},{4,0},{6,2},{8,12},{10,14},{12,8},{14,10},{16,20},{18,... | collective-permute-start | bytes 1966088 | tf_op jit(solution)/shard_map/ppermute | solution.py:27
  128.4 2.9 %copy-start.5 = (bf16[5120,256]{1,0:T(8,128)(2,1)S(1)}, bf16[5120,256]{1,0:T(8,128)(2,1)}, u32[]{:S(2)}) copy-start(bf16[5120,256]{1,0:T(8,128)(2,1)} %wv_ref.3) | copy-start | bytes 7864324
  130.3 26.9 %collective-permute-start.21 = (bf16[4,320,256]{2,1,0:T(8,128)(2,1)S(1)}, bf16[4,320,256]{2,1,0:T(8,128)(2,1)S(1)}, u32[]{:S(2)}, u32[]{:S(2)}) collective-permute-start(bf16[4,320,256]{2,1,0:T(8,128)(2,1)S(1)} %fusion), channel_id=1, source_target_pairs={{0,4},{2,6},{4,0},{6,2},{8,12},{10,14},{12,8},{14,10},{16,20},{18,... | collective-permute-start | bytes 1966088 | tf_op jit(solution)/shard_map/ppermute | solution.py:27
  145.1 14.1 %collective-permute-start.18 = (bf16[2,320,256]{2,1,0:T(8,128)(2,1)S(1)}, bf16[2,320,256]{2,1,0:T(8,128)(2,1)S(1)}, u32[]{:S(2)}, u32[]{:S(2)}) collective-permute-start(bf16[2,320,256]{2,1,0:T(8,128)(2,1)S(1)} %fusion.8), channel_id=1, source_target_pairs={{0,8},{2,10},{4,12},{6,14},{8,0},{10,2},{12,4},{14,6},{16,24},{18,... | collective-permute-start | bytes 983048 | tf_op jit(solution)/shard_map/ppermute | solution.py:27
  157.3 11.7 %collective-permute-start.22 = (bf16[2,320,256]{2,1,0:T(8,128)(2,1)S(1)}, bf16[2,320,256]{2,1,0:T(8,128)(2,1)S(1)}, u32[]{:S(2)}, u32[]{:S(2)}) collective-permute-start(bf16[2,320,256]{2,1,0:T(8,128)(2,1)S(1)} %fusion.9), channel_id=1, source_target_pairs={{0,8},{2,10},{4,12},{6,14},{8,0},{10,2},{12,4},{14,6},{16,24},{18,... | collective-permute-start | bytes 983048 | tf_op jit(solution)/shard_map/ppermute | solution.py:27
  159.3 10.8 %collective-permute-start.19 = (bf16[1,320,256]{2,1,0:T(8,128)(2,1)S(1)}, bf16[1,320,256]{2,1,0:T(8,128)(2,1)S(1)}, u32[]{:S(2)}, u32[]{:S(2)}) collective-permute-start(bf16[1,320,256]{2,1,0:T(8,128)(2,1)S(1)} %dynamic-slice_convert_fusion.2), channel_id=1, source_target_pairs={{0,16},{2,18},{4,20},{6,22},{8,24},{10,26},{12,28},{14,30},{16,0},... | collective-permute-start | bytes 491528 | tf_op jit(solution)/shard_map/ppermute | solution.py:27
  169.1 7.8 %collective-permute-start.23 = (bf16[1,320,256]{2,1,0:T(8,128)(2,1)S(1)}, bf16[1,320,256]{2,1,0:T(8,128)(2,1)S(1)}, u32[]{:S(2)}, u32[]{:S(2)}) collective-permute-start(bf16[1,320,256]{2,1,0:T(8,128)(2,1)S(1)} %dynamic-slice_convert_fusion.1), channel_id=1, source_target_pairs={{0,16},{2,18},{4,20},{6,22},{8,24},{10,26},{12,28},{14,30},{16,0},... | collective-permute-start | bytes 491528 | tf_op jit(solution)/shard_map/ppermute | solution.py:27

commit v2 on v1

v2 whole, which is shorter than its diff:
```python
import functools
import math

import jax
import jax.numpy as jnp
from jax import lax
from jax.experimental import pallas as pl
from jax.experimental.pallas import tpu as pltpu
from jax.sharding import PartitionSpec as P

HD = 128
REACH = 4
ONES = 16
LOG2E = 1.4426950408889634
BF = jnp.bfloat16
F32 = jnp.float32
NT = (((1,), (1,)), ((), ()))
NN = (((1,), (0,)), ((), ()))
TN = (((0,), (0,)), ((), ()))
MIB = 1024 * 1024
VMEM = 32 * MIB
WHOLE = 58 * MIB
RESIDENT = pl.BlockSpec(memory_space=pltpu.VMEM)


def mm(a, b, dims=NN):
    return lax.dot_general(a, b, dims, preferred_element_type=F32)


def permute(block, axis, target, name):
    with jax.named_scope(name):
        return lax.ppermute(block, axis, [(i, target(i)) for i in range(lax.axis_size(axis))])


def after(values, *others):
    return lax.optimization_barrier((values, others))[0]


def project_kernel(groups, at_ref, h_ref, wk_ref, wv_ref, *rest):
    outs, (keep_ref, send_ref, mine_ref), rest = rest[:groups], rest[groups : groups + 3], rest[groups + 3 :]
    h_s, wk_s, wv_s, turned, in_sems, out_sems, mine_sems = rest
    steps, rows, tile = h_s.shape
    width = wk_s.shape[2]
    chunk = keep_ref.shape[1]
    pairs = tile // (2 * chunk)
    half, core = at_ref[0], at_ref[1]
    copies = []
    for j in range(steps):
        at = pl.ds(j * tile, tile)
        copies.append(
            [
                pltpu.make_async_copy(h_ref.at[:, at], h_s.at[j], in_sems.at[j, 0]),
                pltpu.make_async_copy(wk_ref.at[at], wk_s.at[j], in_sems.at[j, 1]),
                pltpu.make_async_copy(wv_ref.at[at], wv_s.at[j], in_sems.at[j, 2]),
            ]
        )
        for copy in copies[-1]:
            copy.start()
    key = value = jnp.zeros((rows, width), F32)
    leaving = []
    for j in range(steps):
        for copy in copies[j]:
            copy.wait()
        key += mm(h_s[j], wk_s[j])
        value += mm(h_s[j], wv_s[j])
        turned[j] = h_s[j].T
        for p in range(pairs):
            for which, out in ((core, keep_ref), (1 - core, send_ref)):
                at = pl.ds(pl.multiple_of((2 * p + which) * chunk, chunk), chunk)
                there = out.at[j * pairs + p]
                sem = out_sems.at[j, p, 0 if out is keep_ref else 1]
                leaving.append(pltpu.make_async_copy(turned.at[j, at], there, sem))
                leaving[-1].start()
    for j in range(steps // 2):
        there = mine_ref.at[pl.ds(j * tile, tile)]
        away = (1 - half) * (steps // 2) + j

        @pl.when(core == 0)
        def _():
            pltpu.make_async_copy(wk_s.at[away], there, mine_sems.at[j]).start()

        @pl.when(core != 0)
        def _():
            pltpu.make_async_copy(wv_s.at[away], there, mine_sems.at[j]).start()

        leaving.append(pltpu.make_async_copy(wk_s.at[away], there, mine_sems.at[j]))
    for g, out in enumerate(outs):
        out[0] = key[:, g * HD : (g + 1) * HD].astype(BF)
        out[1] = value[:, g * HD : (g + 1) * HD].astype(BF)
    for copy in leaving:
        copy.wait()


def project(at, hidden, w_key, w_value, parts):
    rows, depth = hidden.shape
    width = w_key.shape[1]
    steps = 4
    tile = depth // steps
    chunk = depth // parts
    groups = width // HD
    far = pl.BlockSpec(memory_space=pltpu.HBM)
    turned = jax.ShapeDtypeStruct((parts // 2, chunk, rows), BF)
    return pl.pallas_call(
        functools.partial(project_kernel, groups),
        out_shape=[jax.ShapeDtypeStruct((2, rows, HD), BF)] * groups
        + [turned, turned, jax.ShapeDtypeStruct((depth // 2, width), BF)],
        in_specs=[pl.BlockSpec(memory_space=pltpu.SMEM)] + [far] * 3,
        out_specs=[RESIDENT] * groups + [far] * 3,
        scratch_shapes=[
            pltpu.VMEM((steps, rows, tile), BF),
            pltpu.VMEM((steps, tile, width), BF),
            pltpu.VMEM((steps, tile, width), BF),
            pltpu.VMEM((steps, tile, rows), BF),
            pltpu.SemaphoreType.DMA((steps, 3)),
            pltpu.SemaphoreType.DMA((steps, tile // (2 * chunk), 2)),
            pltpu.SemaphoreType.DMA((steps // 2,)),
        ],
        compiler_params=pltpu.CompilerParams(vmem_limit_bytes=WHOLE),
        cost_estimate=pl.CostEstimate(
            flops=4 * rows * depth * width,
            bytes_accessed=4 * depth * (rows + width),
            transcendentals=0,
        ),
        name="project",
    )(at, hidden, w_key, w_value)


def attend_kernel(heads, sel_ref, len_ref, q_ref, do_ref, *rest):
    kv_refs, (rk_ref, rv_ref), rest = rest[:REACH], rest[REACH : REACH + 2], rest[REACH + 2 :]
    (o_ref, dq_ref, rdk_ref, rdv_ref, *part_refs) = rest[-13 - REACH : -9]
    (prompt_s, sems, k_s, v_s, kt_s, vt_s, dk_s, dv_s, first_s) = rest[-9:]
    r = pl.program_id(0)
    plen = kv_refs[0].shape[1]
    rlen = q_ref.shape[0]

    @pl.when(r == 0)
    def _():
        for slot in range(prompt_s.shape[0]):
            for j, ref in enumerate(kv_refs):

                @pl.when(sel_ref[slot] == j)
                def _():
                    pltpu.make_async_copy(ref, prompt_s.at[slot], sems.at[slot]).start()

    pltpu.make_async_copy(kv_refs[0], prompt_s.at[r], sems.at[r]).wait()
    k_s[:plen] = prompt_s[r, 0]
    v_s[:plen] = prompt_s[r, 1]
    k_s[plen:] = rk_ref[...]
    v_s[plen:] = rv_ref[...]
    kt_s[...] = k_s[...].T
    vt_s[:HD] = v_s[...].T
    vt_s[HD:] = jnp.ones((ONES, vt_s.shape[1]), BF)
    scale = HD**-0.5
    c = scale * LOG2E
    live = lax.broadcasted_iota(jnp.int32, (1, rlen), 1) < len_ref[r]
    livef = live.astype(F32)
    key_pos = lax.broadcasted_iota(jnp.int32, (rlen, rlen), 0)
    allowed = key_pos <= lax.broadcasted_iota(jnp.int32, (rlen, rlen), 1)
    span = range(heads)
    cols = [pl.ds(h * HD, HD) for h in span]
    scores = [mm(k_s[...], q_ref[:, cols[h]], NT) for h in span]
    grown, rounded = [], []
    for h in span:
        sp = scores[h][:plen]
        sr = jnp.where(allowed, scores[h][plen:], -jnp.inf)
        m = jnp.maximum(jnp.max(sp, axis=0, keepdims=True), jnp.max(sr, axis=0, keepdims=True))
        e = jnp.concatenate([jnp.exp2((sp - m) * c), jnp.exp2((sr - m) * c)], axis=0)
        grown.append(e)
        rounded.append(e.astype(BF))
    outs, douts = [], []
    for h in span:
        both = mm(vt_s[...], rounded[h])
        inv = livef / both[HD : HD + 1]
        ot = both[:HD] * inv
        outs.append(ot)
        o_ref[:, cols[h]] = ot.T.astype(BF)
        douts.append((do_ref[:, cols[h]].T.astype(F32) * inv).astype(BF))
    dss = []
    for h in span:
        delta = jnp.sum(douts[h].astype(F32) * outs[h], axis=0, keepdims=True)
        dss.append((grown[h] * (mm(v_s[...], douts[h]) - delta)).astype(BF))
    for h in span:
        dq_ref[:, cols[h]] = (mm(kt_s[...], dss[h]) * scale).T.astype(BF)
    dv_s[...] = mm(jnp.concatenate(rounded, axis=1), jnp.concatenate(douts, axis=1), NT)
    dk_s[...] = mm(
        jnp.concatenate(dss, axis=1), jnp.concatenate([q_ref[:, cols[h]] for h in span], axis=0)
    )
    rdk_ref[...] = (dk_s[plen:] * scale).astype(BF)
    rdv_ref[...] = dv_s[plen:].astype(BF)

    @pl.when(r == 0)
    def _():
        first_s[0] = dk_s[:plen]
        first_s[1] = dv_s[:plen]

    @pl.when(r == 1)
    def _():
        one, two = sel_ref[0], sel_ref[1]
        for j, part_ref in enumerate(part_refs):

            @pl.when((one != j) & (two != j))
            def _():
                part_ref[...] = jnp.zeros(part_ref.shape, BF)

            @pl.when((one == j) & (two != j))
            def _():
                part_ref[0] = (first_s[0] * scale).astype(BF)
                part_ref[1] = first_s[1].astype(BF)

            @pl.when((one != j) & (two == j))
            def _():
                part_ref[0] = (dk_s[:plen] * scale).astype(BF)
                part_ref[1] = dv_s[:plen].astype(BF)

            @pl.when((one == j) & (two == j))
            def _():
                part_ref[0] = ((first_s[0] + dk_s[:plen]) * scale).astype(BF)
                part_ref[1] = (first_s[1] + dv_s[:plen]).astype(BF)


def attend(g, sel, lengths, q, dout, kvs, rk, rv, prev):
    rows, width = q.shape
    slots = sel.shape[0]
    rlen = rows // slots
    gw = width // (rk.shape[1] // HD)
    heads = gw // HD
    plen = kvs[0].shape[1]
    klen = plen + rlen
    wide = pl.BlockSpec((rlen, gw), lambda r, *_: (r, g))
    narrow = pl.BlockSpec((rlen, HD), lambda r, *_: (r, g))
    ins = [q, dout, *kvs, rk, rv]
    in_specs = [wide, wide] + [pl.BlockSpec(memory_space=pltpu.HBM)] * REACH + [narrow, narrow]
    aliases = {}
    if prev is not None:
        aliases = {2 + len(ins) + i: i for i in range(4)}
        ins += list(prev)
        in_specs += [pl.BlockSpec(memory_space=pl.ANY)] * 4
    return pl.pallas_call(
        functools.partial(attend_kernel, heads),
        out_shape=[jax.ShapeDtypeStruct(q.shape, BF)] * 2
        + [jax.ShapeDtypeStruct(rk.shape, BF)] * 2
        + [jax.ShapeDtypeStruct((2, plen, HD), BF)] * REACH,
        grid_spec=pltpu.PrefetchScalarGridSpec(
            num_scalar_prefetch=2,
            grid=(slots,),
            in_specs=in_specs,
            out_specs=[wide, wide, narrow, narrow]
            + [pl.BlockSpec((2, plen, HD), lambda r, *_: (0, 0, 0))] * REACH,
            scratch_shapes=[
                pltpu.VMEM((slots, 2, plen, HD), BF),
                pltpu.SemaphoreType.DMA((slots,)),
            ]
            + [pltpu.VMEM((klen, HD), BF)] * 2
            + [pltpu.VMEM((HD, klen), BF), pltpu.VMEM((HD + ONES, klen), BF)]
            + [pltpu.VMEM((klen, HD), F32)] * 2
            + [pltpu.VMEM((2, plen, HD), F32)],
        ),
        input_output_aliases=aliases,
        compiler_params=pltpu.CompilerParams(vmem_limit_bytes=WHOLE),
        cost_estimate=pl.CostEstimate(
            flops=slots * heads * 24 * rlen * klen * HD,
            bytes_accessed=8 * MIB,
            transcendentals=slots * heads * rlen * klen,
        ),
        name=f"attend_{g}",
    )(sel, lengths, *ins)


def weight_kernel(index_ref, near_ref, far_ref, own_ref, pair_ref, *rest):
    count = near_ref.shape[0] // 2
    arrived, outs = (rest[0], rest[1:]) if len(rest) > 1 else (None, rest)
    own, pair = own_ref[...], pair_ref[...]
    for i in range(count):
        at = i ^ index_ref[1]
        chunk = 2 * at + index_ref[0]
        total = mm(near_ref[chunk], own) + mm(far_ref[chunk], pair)
        if arrived is not None:
            total += arrived[at].astype(F32)
        if len(outs) == 2:
            outs[i % 2][i // 2] = total.astype(BF)
        else:
            outs[0][at] = total.astype(BF)


def weight_terms(index, near, far, own, pair, arrived):
    count, chunk, rows = near.shape
    count //= 2
    ins = [near, far, own, pair]
    if arrived is not None:
        ins.append(arrived)
    if arrived is not None and count == REACH:
        out_shape = [jax.ShapeDtypeStruct((count // 2, chunk, 2 * HD), BF)] * 2
        out_specs = [RESIDENT] * 2
    else:
        out_shape = jax.ShapeDtypeStruct((count, chunk, 2 * HD), BF)
        out_specs = RESIDENT
    return pl.pallas_call(
        weight_kernel,
        out_shape=out_shape,
        in_specs=[pl.BlockSpec(memory_space=pltpu.SMEM)] + [RESIDENT] * len(ins),
        out_specs=out_specs,
        compiler_params=pltpu.CompilerParams(vmem_limit_bytes=VMEM),
        cost_estimate=pl.CostEstimate(
            flops=8 * rows * count * chunk * HD,
            bytes_accessed=4 * count * chunk * (rows + 2 * HD),
            transcendentals=0,
        ),
        name="weight_keep" if arrived is not None else "weight_send",
    )(index, *ins)


def halve(held, index, bit):
    count = held.shape[0]
    while count > 1:
        mine = (index // bit) % 2
        split = held.reshape(count // 2, 2, *held.shape[1:])
        out = lax.dynamic_index_in_dim(split, 1 - mine, 1, keepdims=False).astype(BF)
        stay = lax.dynamic_index_in_dim(split, mine, 1, keepdims=False).astype(F32)
        held = stay + permute(out, "dp", lambda i: i ^ bit, "terms_halved").astype(F32)
        count //= 2
        bit *= 2
    return held[0]


def place_index(index):
    return (index // 2) % 2, index // 4, jnp.zeros_like(index)


def send_terms(index, near, far, own, pair):
    bit, _, zero = place_index(index)
    return weight_terms(jnp.stack([1 - bit, zero]), near, far, own, pair, None)


def keep_terms(index, near, far, own, pair, arrived):
    bit, place, zero = place_index(index)
    if near.shape[0] // 2 != REACH:
        held = weight_terms(jnp.stack([bit, zero]), near, far, own, pair, arrived)
        return [halve(held, index, 4)]
    kept, sent = weight_terms(jnp.stack([bit, place]), near, far, own, pair, arrived)
    return [kept, permute(sent, "dp", lambda i: i ^ 4, "terms_z1")]


def cross_terms(held):
    if len(held) == 1:
        return held
    kept, sent = held
    two = (kept[1].astype(F32) + sent[1].astype(F32)).astype(BF)
    return [kept[0], sent[0], permute(two, "dp", lambda i: i ^ 8, "terms_z2")]


def hidden_kernel(groups, at_ref, *rest):
    owns, fars, rest = rest[:groups], rest[groups : 2 * groups], rest[2 * groups :]
    (wk_ref, wv_ref, wa_ref, wb_ref, out_ref, grads) = rest
    cols = wa_ref.shape[0]
    step = pl.program_id(0)
    tile = out_ref.shape[1]

    @pl.when(step == 0)
    def _():
        first = at_ref[1]
        for g in range(groups):
            at = pl.ds(g * HD, HD)
            for j in range(2):
                grads[j, :, at] = owns[g][:, j * HD : (j + 1) * HD]
                away = pl.multiple_of(jnp.where(first == 0, j, 1 - j) * HD, HD)
                grads[2 + j, :, at] = fars[g][:, pl.ds(away, HD)]

    near = pl.ds(pl.multiple_of(at_ref[0] * cols + step * tile, tile), tile)
    away = pl.ds(pl.multiple_of(step * tile, tile), tile)
    total = mm(grads[0], wk_ref[near, :], NT) + mm(grads[1], wv_ref[near, :], NT)
    total += mm(grads[2], wa_ref[away, :], NT) + mm(grads[3], wb_ref[away, :], NT)
    out_ref[...] = total.astype(BF)


def hidden_grads(at, owns, fars, w_key, w_value, far_a, far_b):
    groups = len(owns)
    rows = owns[0].shape[0]
    cols, width = far_a.shape
    tile = 512
    return pl.pallas_call(
        functools.partial(hidden_kernel, groups),
        out_shape=jax.ShapeDtypeStruct((rows, cols), BF),
        grid_spec=pltpu.PrefetchScalarGridSpec(
            num_scalar_prefetch=1,
            grid=(cols // tile,),
            in_specs=[RESIDENT] * (2 * groups + 4),
            out_specs=pl.BlockSpec((rows, tile), lambda i, at: (0, i)),
            scratch_shapes=[pltpu.VMEM((4, rows, width), BF)],
        ),
        compiler_params=pltpu.CompilerParams(vmem_limit_bytes=VMEM),
        cost_estimate=pl.CostEstimate(
            flops=8 * rows * cols * width,
            bytes_accessed=2 * cols * (rows + 4 * width),
            transcendentals=0,
        ),
        name="hidden_grads",
    )(at, *owns, *fars, w_key, w_value, far_a, far_b)


def total_grad(own, shares):
    total = own.astype(F32)
    for share in shares:
        total += share.astype(F32)
    return jnp.concatenate([total[0], total[1]], axis=-1).astype(BF)


def body(
    prompt_hidden,
    w_key,
    w_value,
    queries,
    resp_key,
    resp_value,
    cotangent,
    group_offset,
    resp_length,
):
    size = lax.axis_size("dp")
    index = lax.axis_index("dp")
    core = index % 2
    half = lax.axis_index("mp")
    groups = w_key.shape[1] // HD
    cols = w_key.shape[0] // 2

    def other(i):
        return (i + 1) % size if i % 2 == 0 else (i + 3) % size

    def back(i):
        return (i - 1) % size if i % 2 == 1 else (i - 3) % size

    def cross(i):
        return (i - 1) % size if i % 2 == 0 else (i - 3) % size

    sel = jnp.where((group_offset % 2 == 1) & (core == 0), 4 - group_offset, group_offset)

    at = jnp.stack([half, core])
    *pairs, near, turned, mine = project(at, prompt_hidden, w_key, w_value, size)
    two = permute(pairs[0], "dp", lambda i: (i + 2) % size, "pair_two")
    one = permute(pairs[0], "dp", other, "pair_other")
    received = [[pairs[0], one, two, permute(two, "dp", lambda i: i ^ 1, "pair_core")]]
    far_a = permute(mine, "mp", lambda i: 1 - i, "weights_y")
    far = permute(turned, "dp", lambda i: i ^ 1, "turned_core")
    later = after(pairs[1], two)
    received.append(
        [
            later,
            permute(later, "dp", other, "pair_other"),
            permute(later, "dp", lambda i: (i + 2) % size, "pair_two"),
            permute(later, "dp", lambda i: (i + (1 if i % 2 else 3)) % size, "pair_cross"),
        ]
    )

    *prev, mine_0, other_0, two_0, core_0 = attend(
        0, sel, resp_length, queries, cotangent, received[0], resp_key, resp_value, None
    )
    shares = [
        permute(other_0, "dp", back, "grad_other"),
        permute(two_0, "dp", lambda i: (i - 2) % size, "grad_two"),
        permute(core_0, "dp", cross, "grad_cross"),
    ]
    received[1], far, far_a, prev = after((received[1], far, far_a, prev), mine_0)
    *prev, mine_1, other_1, two_1, core_1 = attend(
        1, sel, resp_length, queries, cotangent, received[1], resp_key, resp_value, prev
    )
    far_b = permute(far_a, "dp", lambda i: i ^ 1, "weights_core")
    swapped = permute(core_1, "dp", lambda i: i ^ 1, "grad_core")
    shares_1 = [permute(other_1, "dp", back, "grad_other")]

    def along_x(i):
        return i ^ 2

    own = [total_grad(after(mine_0, mine_1), shares)]
    pair = [permute(own[0], "dp", lambda i: i ^ 1, "own_core")]
    two = after((two_1.astype(F32) + swapped.astype(F32)).astype(BF), own[0])
    shares_1.append(permute(two, "dp", lambda i: (i - 2) % size, "grad_two"))
    sent = [send_terms(index, near, far, after(own[0], two), pair[0])]
    arrived = [permute(sent[0], "dp", along_x, "terms_x")]

    own.append(total_grad(after(mine_1, sent[0]), shares_1))
    pair.append(permute(own[1], "dp", lambda i: i ^ 1, "own_core"))
    sent.append(send_terms(index, near, far, own[1], pair[1]))
    arrived.append(permute(sent[1], "dp", along_x, "terms_x"))
    away = [permute(grad, "mp", lambda i: 1 - i, "own_y") for grad in own]

    held = [keep_terms(index, near, far, own[0], pair[0], after(arrived[0], sent[1]))]
    hidden_grad = hidden_grads(
        at, after(own, held[0][0]), away, w_key, w_value, far_a, far_b
    )
    terms = [cross_terms(after(held[0], hidden_grad))]
    held.append(keep_terms(index, near, far, own[1], pair[1], after(arrived[1], terms[0][:2][-1])))
    terms.append(cross_terms(held[1]))
    weight_grads = [sum(t.astype(F32) for t in term) for term in terms]
    return (
        *prev,
        hidden_grad,
        jnp.concatenate([t[:, :HD] for t in weight_grads], axis=-1),
        jnp.concatenate([t[:, HD:] for t in weight_grads], axis=-1),
    )


def solution(mesh):
    placed = (
        P("dp", None),
        P(None, "mp"),
        P(None, "mp"),
        P("dp", "mp"),
        P("dp", "mp"),
        P("dp", "mp"),
        P("dp", "mp"),
        P("dp"),
        P("dp"),
    )
    return jax.shard_map(
        body,
        mesh=mesh,
        in_specs=placed,
        out_specs=(P("dp", "mp"),) * 7,
        check_vma=False,
    )
```

time: 178 us -> 129 us (0.72)
  waiting for transfers between devices: 71.3 us -> 39.6 us
  Pallas kernels: 65.3 us -> 53.7 us
  local copies, waits for them, and re-layouts: 14.6 us -> 5.78 us
  starting transfers between devices: 19 us -> 23.7 us
  other arithmetic: 6.71 us -> 4.73 us
    ppermute x24 -> x25, waiting for transfers between devices: 71.3 us -> 39.6 us  [permute(): lax.ppermute(block, axis, [(i, target(i)) for i in range(lax.axis_size(ax...]
    pallas_call x2, Pallas kernels: 40.2 us -> 30.4 us  [attend(): pl.pallas_call(functools.partial(attend_kernel, heads), out_shape=[jax.Sh...]
    unnamed x47 -> x34, local copies, waits for them, and re-layouts: 14.1 us -> 5.69 us
    ppermute x24 -> x25, starting transfers between devices: 19 us -> 23.7 us  [permute(): lax.ppermute(block, axis, [(i, target(i)) for i in range(lax.axis_size(ax...]
    add x6 -> x2, other arithmetic: 3.81 us -> 0.11 us  [body(): weight_grads = [sum((t.astype(F32) for t in term)) for term in terms]]
    another operation x0 -> x5, other arithmetic: none -> 2.02 us
    pallas_call x4 -> x6, Pallas kernels: 25.1 us -> 23.3 us  [the longest x1 8.22 us: project(): pl.pallas_call(functools.partial(project_kernel, groups), out_shape=[jax....]
  transfers between devices with their start and end apart: 24 -> 25, of which waited for: 12 -> 9; matrix products, arithmetic and copies ran while one was open for 4% -> 3% of each run, Pallas kernels for 33% -> 35%
where the time goes in v2:
time: 129 us; the launch traced here: 128 us
  Pallas kernels  53.7 us (42%)
  waiting for transfers between devices  39.6 us (31%)
  starting transfers between devices  23.7 us (18%)
  local copies, waits for them, and re-layouts  5.78 us (4%)
  other arithmetic  4.73 us (4%)
    ppermute x25, waiting for transfers between devices, permute(): lax.ppermute(block, axis, [(i, target(i)) for i in range(lax.axis_size(ax...  39.6 us
    pallas_call x2, Pallas kernels, attend(): pl.pallas_call(functools.partial(attend_kernel, heads), out_shape=[jax.Sh...  30.4 us
    ppermute x25, starting transfers between devices, permute(): lax.ppermute(block, axis, [(i, target(i)) for i in range(lax.axis_size(ax...  23.7 us
    pallas_call x1, Pallas kernels, project(): pl.pallas_call(functools.partial(project_kernel, groups), out_shape=[jax....  8.22 us
    pallas_call x4, Pallas kernels, weight_terms(): pl.pallas_call(weight_kernel, out_shape=out_shape, in_specs=[pl.BlockSpec...  7.79 us
    pallas_call x1, Pallas kernels, hidden_grads(): pl.pallas_call(functools.partial(hidden_kernel, groups), out_shape=jax.Sh...  7.27 us
    unnamed x34, local copies, waits for them, and re-layouts  5.69 us
  transfers between devices with their start and end apart: 25, of which 9 were waited for; matrix products, arithmetic and copies ran while one was open for 3% of the time, Pallas kernels for 35%

profile of v2, /device:TPU:0, one launch (start us, length us, event | category | flops | bytes accessed | tf_op | source)
XLA Modules:
  0.0 128.5 jit_solution(4649053870650047016)
XLA Ops:
  0.6 0.6 pad_add_fusion.at_ref
  1.2 8.2 %project.1 = (bf16[2,512,128]{2,1,0:T(8,128)(2,1)}, bf16[2,512,128]{2,1,0:T(8,128)(2,1)}, bf16[8,320,512]{2,1,0:T(8,128)(2,1)}, bf16[8,320,512]{2,1,0:T(8,128)(2,1)}, bf16[2560,256]{1,0:T(8,128)(2,1)}) custom-call(s32[2]{0:T(128)} %pad_add_fusion.at_ref, bf16[512,5120]{1,0:T(8,128)(2,1)} %h_ref.1, bf16[5120,256]{1,0:T(8,128)(2,1)} %rest_4_.5, ...), custom_call_target="tpu_custom_call" | custom-call | flops 2684354560 | bytes 15728640 | tf_op jit(solution)/shard_map/project/pallas_call | solution.py:103
  9.5 0.5 collective-permute-start.4
  10.0 2.6 %collective-permute-start = (bf16[2,512,128]{2,1,0:T(8,128)(2,1)}, bf16[2,512,128]{2,1,0:T(8,128)(2,1)S(1)}, u32[]{:S(2)}, u32[]{:S(2)}) collective-permute-start(bf16[2,512,128]{2,1,0:T(8,128)(2,1)} %get-tuple-element.54.rest_0_), channel_id=1, source_target_pairs={{0,4},{2,6},{4,8},{6,10},{8,12},{10,14},{12,16},{14,18},{16,20},{1... | collective-permute-start | bytes 786440 | tf_op jit(solution)/shard_map/pair_two/ppermute | solution.py:32
  12.5 1.5 %collective-permute-start.5 = (bf16[2560,256]{1,0:T(8,128)(2,1)}, bf16[2560,256]{1,0:T(8,128)(2,1)}, u32[]{:S(2)}, u32[]{:S(2)}) collective-permute-start(bf16[2560,256]{1,0:T(8,128)(2,1)} %get-tuple-element.57), channel_id=1, source_target_pairs={{0,1},{1,0},{2,3},{3,2},{4,5},{5,4},{6,7},{7,6},{8,9},{9,8},{10,11... | collective-permute-start | bytes 3932168 | tf_op jit(solution)/shard_map/weights_y/ppermute | solution.py:32
  14.1 0.0 collective-permute-start.6
  14.1 8.9 %collective-permute-done.rest_2_ = bf16[2,512,128]{2,1,0:T(8,128)(2,1)S(1)} collective-permute-done((bf16[2,512,128]{2,1,0:T(8,128)(2,1)}, bf16[2,512,128]{2,1,0:T(8,128)(2,1)S(1)}, u32[]{:S(2)}, u32[]{:S(2)}) %collective-permute-start) | collective-permute-done | bytes 262176 | tf_op jit(solution)/shard_map/pair_two/ppermute | solution.py:32
  23.0 0.5 and_select_fusion.sel_ref
  23.5 0.0 collective-permute-start.3
  23.5 0.0 collective-permute-done.6.rest_1_
  23.5 2.6 %collective-permute-start.2 = (bf16[2,512,128]{2,1,0:T(8,128)(2,1)}, bf16[2,512,128]{2,1,0:T(8,128)(2,1)S(1)}, u32[]{:S(2)}, u32[]{:S(2)}) collective-permute-start(bf16[2,512,128]{2,1,0:T(8,128)(2,1)} %get-tuple-element.63.rest_0_), channel_id=1, source_target_pairs={{0,4},{2,6},{4,8},{6,10},{8,12},{10,14},{12,16},{14,18},{16,20},{1... | collective-permute-start | bytes 786440 | tf_op jit(solution)/shard_map/pair_two/ppermute | solution.py:32
  26.1 0.0 collective-permute-done.7.rest_3_
  26.1 0.7 copy-done.15
  26.8 15.1 %attend_0.1 = (bf16[512,2048]{1,0:T(8,128)(2,1)}, bf16[512,2048]{1,0:T(8,128)(2,1)}, bf16[512,256]{1,0:T(8,128)(2,1)}, bf16[512,256]{1,0:T(8,128)(2,1)}, bf16[2,...) custom-call(s32[2]{0:T(128)} %and_select_fusion.sel_ref, ...), custom_call_target="tpu_custom_call" | custom-call | flops 9663676416 | bytes 8388608 | tf_op jit(solution)/shard_map/attend_0/pallas_call | solution.py:238
  41.9 0.0 collective-permute-done.3.rest_3_
  41.9 2.9 %collective-permute-start.8 = (bf16[2,512,128]{2,1,0:T(8,128)(2,1)}, bf16[2,512,128]{2,1,0:T(8,128)(2,1)S(1)}, u32[]{:S(2)}, u32[]{:S(2)}) collective-permute-start(bf16[2,512,128]{2,1,0:T(8,128)(2,1)} %get-tuple-element.77), channel_id=1, source_target_pairs={{0,26},{2,0},{4,30},{6,4},{8,2},{10,8},{12,6},{14,12},{16,10},{18,... | collective-permute-start | bytes 786440 | tf_op jit(solution)/shard_map/grad_other/ppermute | solution.py:32
  44.9 0.0 collective-permute-done.2.rest_2_
  44.9 0.5 collective-permute-start.9
  45.4 0.8 collective-permute-start.10
  46.1 0.0 collective-permute-done.5.rest_6_
  46.1 0.0 collective-permute-done.4.far_ref
  46.2 1.5 %copy-done.1 = bf16[8,320,512]{2,1,0:T(8,128)(2,1)} copy-done((bf16[8,320,512]{2,1,0:T(8,128)(2,1)}, bf16[8,320,512]{2,1,0:T(8,128)(2,1)S(1)}, u32[]{:S(2)}) %copy-start.1) | copy-done | bytes 2621464
  47.6 15.3 %attend_1.1 = (bf16[512,2048]{1,0:T(8,128)(2,1)}, bf16[512,2048]{1,0:T(8,128)(2,1)}, bf16[512,256]{1,0:T(8,128)(2,1)}, bf16[512,256]{1,0:T(8,128)(2,1)}, bf16[2,...) custom-call(s32[2]{0:T(128)} %and_select_fusion.sel_ref, ...), custom_call_target="tpu_custom_call", output_to_operand_aliasing={{0}: (10, {}), {1}: (11, {}), {2}: (12, {}), {3}: (13, {})} | custom-call | flops 9663676416 | bytes 8388608 | tf_op jit(solution)/shard_map/attend_1/pallas_call | solution.py:238
  62.9 0.0 copy-start
  62.9 1.4 %collective-permute-start.11 = (bf16[2,512,128]{2,1,0:T(8,128)(2,1)}, bf16[2,512,128]{2,1,0:T(8,128)(2,1)S(1)}, u32[]{:S(2)}, u32[]{:S(2)}) collective-permute-start(bf16[2,512,128]{2,1,0:T(8,128)(2,1)} %get-tuple-element.83), channel_id=1, source_target_pairs={{0,2},{2,0},{4,6},{6,4},{8,10},{10,8},{12,14},{14,12},{16,18},{18,... | collective-permute-start | bytes 786440 | tf_op jit(solution)/shard_map/grad_core/ppermute | solution.py:32
  64.3 0.0 collective-permute-done.8
  64.3 0.0 collective-permute-done.9
  64.3 0.1 add_convert_fusion.2
  64.5 0.6 collective-permute-start.12
  65.1 0.6 collective-permute-done.11
  65.7 1.0 add_convert_fusion.1
  66.7 0.4 collective-permute-start.14
  67.1 0.2 collective-permute-start.19
  67.3 0.1 pad_add_fusion.1.index_ref
  67.4 0.0 collective-permute-done.12.pair_ref
  67.4 1.7 %copy-done.2 = bf16[8,320,512]{2,1,0:T(8,128)(2,1)S(1)} copy-done((bf16[8,320,512]{2,1,0:T(8,128)(2,1)S(1)}, bf16[8,320,512]{2,1,0:T(8,128)(2,1)}, u32[]{:S(2)}) %copy-start.2) | copy-done | bytes 2621464
  69.1 2.2 %weight_send.2 = bf16[4,320,256]{2,1,0:T(8,128)(2,1)} custom-call(s32[2]{0:T(128)S(1)} %pad_add_fusion.1.index_ref, bf16[8,320,512]{2,1,0:T(8,128)(2,1)S(1)} %copy-done, bf16[8,320,512]{2,1,0:T(8,128)(2,1)S(1)} %copy-done.2, bf16[512,256]{1,0:T(8,128)(2,1)S(1)} %pad_maximum_fusion.2.own_ref.rest_0_, bf16[512,256]{1,0:T(8,128)(2,1)S(1)} %collective-permute-done.12.pair_ref), custom_call_target="tpu_custom_call" | custom-call | flops 671088640 | bytes 3932160 | tf_op jit(solution)/shard_map/weight_send/pallas_call | solution.py:297
  71.4 1.5 %collective-permute-start.15 = (bf16[4,320,256]{2,1,0:T(8,128)(2,1)}, bf16[4,320,256]{2,1,0:T(8,128)(2,1)}, u32[]{:S(2)}, u32[]{:S(2)}) collective-permute-start(bf16[4,320,256]{2,1,0:T(8,128)(2,1)} %weight_send.2), channel_id=1, source_target_pairs={{0,4},{2,6},{4,0},{6,2},{8,12},{10,14},{12,8},{14,10},{16,20},{18,... | collective-permute-start | bytes 1966088 | tf_op jit(solution)/shard_map/terms_x/ppermute | solution.py:32
  72.9 3.1 %collective-permute-done.14 = bf16[2,512,128]{2,1,0:T(8,128)(2,1)} collective-permute-done((bf16[2,512,128]{2,1,0:T(8,128)(2,1)S(1)}, bf16[2,512,128]{2,1,0:T(8,128)(2,1)}, u32[]{:S(2)}, u32[]{:S(2)}) %collective-permute-start.14) | collective-permute-done | bytes 262176 | tf_op jit(solution)/shard_map/grad_two/ppermute | solution.py:32
  76.0 1.1 add_convert_fusion
  77.2 0.1 collective-permute-start.16
  77.3 1.7 %collective-permute-start.17 = (bf16[512,256]{1,0:T(8,128)(2,1)S(1)}, bf16[512,256]{1,0:T(8,128)(2,1)S(1)}, u32[]{:S(2)}, u32[]{:S(2)}) collective-permute-start(bf16[512,256]{1,0:T(8,128)(2,1)S(1)} %pad_maximum_fusion.2.own_ref.rest_0_), channel_id=1, source_target_pairs={{0,1},{1,0},{2,3},{3,2},{4,5},{5,4},{6,7},{7,6},{8,9},{9,8},{10,11... | collective-permute-start | bytes 786440 | tf_op jit(solution)/shard_map/own_y/ppermute | solution.py:32
  79.0 0.4 collective-permute-start.18
  79.4 1.7 %copy-done.3 = bf16[8,320,512]{2,1,0:T(8,128)(2,1)S(1)} copy-done((bf16[8,320,512]{2,1,0:T(8,128)(2,1)S(1)}, bf16[8,320,512]{2,1,0:T(8,128)(2,1)}, u32[]{:S(2)}) %copy-start.3) | copy-done | bytes 2621464
  81.1 1.8 %weight_send.3 = bf16[4,320,256]{2,1,0:T(8,128)(2,1)S(1)} custom-call(s32[2]{0:T(128)S(1)} %pad_add_fusion.1.index_ref, bf16[8,320,512]{2,1,0:T(8,128)(2,1)S(1)} %copy-done, bf16[8,320,512]{2,1,0:T(8,128)(2,1)S(1)} %copy-done.3, bf16[512,256]{1,0:T(8,128)(2,1)S(1)} %pad_maximum_fusion.3.own_ref.rest_1_, bf16[512,256]{1,0:T(8,128)(2,1)} %collective-permute-done.16.pair_ref), custom_call_target="tpu_custom_call" | custom-call | flops 671088640 | bytes 3932160 | tf_op jit(solution)/shard_map/weight_send/pallas_call | solution.py:297
  82.9 1.9 %collective-permute-start.22 = (bf16[4,320,256]{2,1,0:T(8,128)(2,1)S(1)}, bf16[4,320,256]{2,1,0:T(8,128)(2,1)S(1)}, u32[]{:S(2)}, u32[]{:S(2)}) collective-permute-start(bf16[4,320,256]{2,1,0:T(8,128)(2,1)S(1)} %weight_send.3), channel_id=1, source_target_pairs={{0,4},{2,6},{4,0},{6,2},{8,12},{10,14},{12,8},{14,10},{16,20},{18,... | collective-permute-start | bytes 1966088 | tf_op jit(solution)/shard_map/terms_x/ppermute | solution.py:32
  84.9 0.1 pad_add_fusion.2.index_ref
  84.9 5.1 %collective-permute-done.15.rest_0_ = bf16[4,320,256]{2,1,0:T(8,128)(2,1)} collective-permute-done((bf16[4,320,256]{2,1,0:T(8,128)(2,1)}, bf16[4,320,256]{2,1,0:T(8,128)(2,1)}, u32[]{:S(2)}, u32[]{:S(2)}) %collective-permute-start.15) | collective-permute-done | bytes 655392 | tf_op jit(solution)/shard_map/terms_x/ppermute | solution.py:32
  90.0 1.9 %weight_keep.2 = (bf16[2,320,256]{2,1,0:T(8,128)(2,1)S(1)}, bf16[2,320,256]{2,1,0:T(8,128)(2,1)S(1)}) custom-call(s32[2]{0:T(128)S(1)} %pad_add_fusion.2.index_ref, bf16[8,320,512]{2,1,0:T(8,128)(2,1)S(1)} %copy-done, bf16[8,320,512]{2,1,0:T(8,128)(2,1)S(1)} %copy-done.3, bf16[512,256]{1,0:T(8,128)(2,1)S(1)} %pad_maximum_fusion.2.own_ref.rest_0_, ...), custom_call_target="tpu_custom_call" | custom-call | flops 671088640 | bytes 3932160 | tf_op jit(solution)/shard_map/weight_keep/pallas_call | solution.py:297
  92.0 1.1 collective-permute-start.20
  93.1 0.0 collective-permute-done.19.rest_7_
  93.1 7.3 %hidden_grads.1 = bf16[512,2560]{1,0:T(8,128)(2,1)} custom-call(s32[2]{0:T(128)S(1)} %copy-done.7, bf16[512,256]{1,0:T(8,128)(2,1)S(1)} %pad_maximum_fusion.2.own_ref.rest_0_, bf16[512,256]{1,0:T(8,128)(2,1)S(1)} %pad_maximum_fusion.3.own_ref.rest_1_, bf16[512,256]{1,0:T(8,128)(2,1)S(1)} %collective-permute-done.17.rest_2_, ...), custom_call_target="tpu_custom_call" | custom-call | flops 2684354560 | bytes 7864320 | tf_op jit(solution)/shard_map/hidden_grads/pallas_call | solution.py:380
  100.4 0.6 collective-permute-done.20
  101.0 1.1 collective-permute-start.21
  102.2 1.2 collective-permute-done.22.rest_0_
  103.4 1.8 %weight_keep.3 = (bf16[2,320,256]{2,1,0:T(8,128)(2,1)S(1)}, bf16[2,320,256]{2,1,0:T(8,128)(2,1)S(1)}) custom-call(s32[2]{0:T(128)S(1)} %pad_add_fusion.2.index_ref, bf16[8,320,512]{2,1,0:T(8,128)(2,1)S(1)} %copy-done, bf16[8,320,512]{2,1,0:T(8,128)(2,1)S(1)} %copy-done.4, bf16[512,256]{1,0:T(8,128)(2,1)S(1)} %pad_maximum_fusion.3.own_ref.rest_1_, ...), custom_call_target="tpu_custom_call" | custom-call | flops 671088640 | bytes 3932160 | tf_op jit(solution)/shard_map/weight_keep/pallas_call | solution.py:297
  105.2 1.1 collective-permute-start.23
  106.4 3.8 %collective-permute-done.21 = bf16[320,256]{1,0:T(8,128)(2,1)S(1)} collective-permute-done((bf16[320,256]{1,0:T(8,128)(2,1)S(1)}, bf16[320,256]{1,0:T(8,128)(2,1)S(1)}, u32[]{:S(2)}, u32[]{:S(2)}) %collective-permute-start.21) | collective-permute-done | bytes 163872 | tf_op jit(solution)/shard_map/terms_z2/ppermute | solution.py:32
  110.2 0.1 fusion
  110.3 6.7 %collective-permute-done.23 = bf16[2,320,256]{2,1,0:T(8,128)(2,1)S(1)} collective-permute-done((bf16[2,320,256]{2,1,0:T(8,128)(2,1)S(1)}, bf16[2,320,256]{2,1,0:T(8,128)(2,1)S(1)}, u32[]{:S(2)}, u32[]{:S(2)}) %collective-permute-start.23) | collective-permute-done | bytes 327712 | tf_op jit(solution)/shard_map/terms_z1/ppermute | solution.py:32
  117.0 0.8 collective-permute-start.24
  117.9 9.6 %collective-permute-done.24 = bf16[320,256]{1,0:T(8,128)(2,1)S(1)} collective-permute-done((bf16[320,256]{1,0:T(8,128)(2,1)S(1)}, bf16[320,256]{1,0:T(8,128)(2,1)S(1)}, u32[]{:S(2)}, u32[]{:S(2)}) %collective-permute-start.24) | collective-permute-done | bytes 163872 | tf_op jit(solution)/shard_map/terms_z2/ppermute | solution.py:32
  127.5 0.1 bitcast_add_fusion
  127.6 0.9 pad_maximum_fusion
  (46 shorter events, 0.3 us)
Async XLA Ops:
  1.2 21.7 %copy-start.16 = (s32[2]{0:T(128)S(1)}, s32[2]{0:T(128)}, u32[]{:S(2)}) copy-start(s32[2]{0:T(128)} %param.16) | copy-start | bytes 28
  9.5 36.7 %collective-permute-start.4 = (bf16[8,320,512]{2,1,0:T(8,128)(2,1)}, bf16[8,320,512]{2,1,0:T(8,128)(2,1)S(1)}, u32[]{:S(2)}, u32[]{:S(2)}) collective-permute-start(bf16[8,320,512]{2,1,0:T(8,128)(2,1)} %get-tuple-element.56), channel_id=1, source_target_pairs={{0,2},{2,0},{4,6},{6,4},{8,10},{10,8},{12,14},{14,12},{16,18},{18,... | collective-permute-start | bytes 7864328 | tf_op jit(solution)/shard_map/turned_core/ppermute | solution.py:32
  10.0 13.0 %collective-permute-start = (bf16[2,512,128]{2,1,0:T(8,128)(2,1)}, bf16[2,512,128]{2,1,0:T(8,128)(2,1)S(1)}, u32[]{:S(2)}, u32[]{:S(2)}) collective-permute-start(bf16[2,512,128]{2,1,0:T(8,128)(2,1)} %get-tuple-element.54.rest_0_), channel_id=1, source_target_pairs={{0,4},{2,6},{4,8},{6,10},{8,12},{10,14},{12,16},{14,18},{16,20},{1... | collective-permute-start | bytes 786440 | tf_op jit(solution)/shard_map/pair_two/ppermute | solution.py:32
  12.5 33.6 %collective-permute-start.5 = (bf16[2560,256]{1,0:T(8,128)(2,1)}, bf16[2560,256]{1,0:T(8,128)(2,1)}, u32[]{:S(2)}, u32[]{:S(2)}) collective-permute-start(bf16[2560,256]{1,0:T(8,128)(2,1)} %get-tuple-element.57), channel_id=1, source_target_pairs={{0,1},{1,0},{2,3},{3,2},{4,5},{5,4},{6,7},{7,6},{8,9},{9,8},{10,11... | collective-permute-start | bytes 3932168 | tf_op jit(solution)/shard_map/weights_y/ppermute | solution.py:32
  14.1 9.5 %collective-permute-start.6 = (bf16[2,512,128]{2,1,0:T(8,128)(2,1)}, bf16[2,512,128]{2,1,0:T(8,128)(2,1)S(1)}, u32[]{:S(2)}, u32[]{:S(2)}) collective-permute-start(bf16[2,512,128]{2,1,0:T(8,128)(2,1)} %get-tuple-element.54.rest_0_), channel_id=1, source_target_pairs={{0,2},{2,8},{4,6},{6,12},{8,10},{10,16},{12,14},{14,20},{16,18},{1... | collective-permute-start | bytes 786440 | tf_op jit(solution)/shard_map/pair_other/ppermute | solution.py:32
  22.9 3.1 %copy-start.13 = (bf16[2,512,128]{2,1,0:T(8,128)(2,1)}, bf16[2,512,128]{2,1,0:T(8,128)(2,1)S(1)}, u32[]{:S(2)}) copy-start(bf16[2,512,128]{2,1,0:T(8,128)(2,1)S(1)} %collective-permute-done.rest_2_) | copy-start | bytes 786436
  22.9 3.1 %collective-permute-start.7 = (bf16[2,512,128]{2,1,0:T(8,128)(2,1)S(1)}, bf16[2,512,128]{2,1,0:T(8,128)(2,1)S(1)}, u32[]{:S(2)}, u32[]{:S(2)}) collective-permute-start(bf16[2,512,128]{2,1,0:T(8,128)(2,1)S(1)} %collective-permute-done.rest_2_), channel_id=1, source_target_pairs={{0,2},{2,0},{4,6},{6,4},{8,10},{10,8},{12,14},{14,12},{16,18},{18,... | collective-permute-start | bytes 786440 | tf_op jit(solution)/shard_map/pair_core/ppermute | solution.py:32
  23.5 18.4 %collective-permute-start.3 = (bf16[2,512,128]{2,1,0:T(8,128)(2,1)}, bf16[2,512,128]{2,1,0:T(8,128)(2,1)S(1)}, u32[]{:S(2)}, u32[]{:S(2)}) collective-permute-start(bf16[2,512,128]{2,1,0:T(8,128)(2,1)} %get-tuple-element.63.rest_0_), channel_id=1, source_target_pairs={{0,6},{2,4},{4,10},{6,8},{8,14},{10,12},{12,18},{14,16},{16,22},{1... | collective-permute-start | bytes 786440 | tf_op jit(solution)/shard_map/pair_cross/ppermute | solution.py:32
  23.5 2.6 %copy-start.14 = (bf16[2,512,128]{2,1,0:T(8,128)(2,1)}, bf16[2,512,128]{2,1,0:T(8,128)(2,1)S(1)}, u32[]{:S(2)}) copy-start(bf16[2,512,128]{2,1,0:T(8,128)(2,1)S(1)} %collective-permute-done.6.rest_1_) | copy-start | bytes 786436
  23.5 21.4 %collective-permute-start.2 = (bf16[2,512,128]{2,1,0:T(8,128)(2,1)}, bf16[2,512,128]{2,1,0:T(8,128)(2,1)S(1)}, u32[]{:S(2)}, u32[]{:S(2)}) collective-permute-start(bf16[2,512,128]{2,1,0:T(8,128)(2,1)} %get-tuple-element.63.rest_0_), channel_id=1, source_target_pairs={{0,4},{2,6},{4,8},{6,10},{8,12},{10,14},{12,16},{14,18},{16,20},{1... | collective-permute-start | bytes 786440 | tf_op jit(solution)/shard_map/pair_two/ppermute | solution.py:32
  26.1 0.7 copy-start.15
  26.1 19.3 %collective-permute-start.1 = (bf16[2,512,128]{2,1,0:T(8,128)(2,1)}, bf16[2,512,128]{2,1,0:T(8,128)(2,1)S(1)}, u32[]{:S(2)}, u32[]{:S(2)}) collective-permute-start(bf16[2,512,128]{2,1,0:T(8,128)(2,1)} %get-tuple-element.63.rest_0_), channel_id=1, source_target_pairs={{0,2},{2,8},{4,6},{6,12},{8,10},{10,16},{12,14},{14,20},{16,18},{1... | collective-permute-start | bytes 786440 | tf_op jit(solution)/shard_map/pair_other/ppermute | solution.py:32
  41.9 5.7 %copy-start.10 = (bf16[2,512,128]{2,1,0:T(8,128)(2,1)}, bf16[2,512,128]{2,1,0:T(8,128)(2,1)S(1)}, u32[]{:S(2)}) copy-start(bf16[2,512,128]{2,1,0:T(8,128)(2,1)S(1)} %collective-permute-done.3.rest_3_) | copy-start | bytes 786436
  41.9 22.4 %collective-permute-start.8 = (bf16[2,512,128]{2,1,0:T(8,128)(2,1)}, bf16[2,512,128]{2,1,0:T(8,128)(2,1)S(1)}, u32[]{:S(2)}, u32[]{:S(2)}) collective-permute-start(bf16[2,512,128]{2,1,0:T(8,128)(2,1)} %get-tuple-element.77), channel_id=1, source_target_pairs={{0,26},{2,0},{4,30},{6,4},{8,2},{10,8},{12,6},{14,12},{16,10},{18,... | collective-permute-start | bytes 786440 | tf_op jit(solution)/shard_map/grad_other/ppermute | solution.py:32
  44.9 2.8 %copy-start.11 = (bf16[2,512,128]{2,1,0:T(8,128)(2,1)}, bf16[2,512,128]{2,1,0:T(8,128)(2,1)S(1)}, u32[]{:S(2)}) copy-start(bf16[2,512,128]{2,1,0:T(8,128)(2,1)S(1)} %collective-permute-done.2.rest_2_) | copy-start | bytes 786436
  44.9 19.4 %collective-permute-start.9 = (bf16[2,512,128]{2,1,0:T(8,128)(2,1)}, bf16[2,512,128]{2,1,0:T(8,128)(2,1)S(1)}, u32[]{:S(2)}, u32[]{:S(2)}) collective-permute-start(bf16[2,512,128]{2,1,0:T(8,128)(2,1)} %get-tuple-element.78), channel_id=1, source_target_pairs={{0,28},{2,30},{4,0},{6,2},{8,4},{10,6},{12,8},{14,10},{16,12},{18,... | collective-permute-start | bytes 786440 | tf_op jit(solution)/shard_map/grad_two/ppermute | solution.py:32
  45.4 2.3 %copy-start.12 = (bf16[2,512,128]{2,1,0:T(8,128)(2,1)}, bf16[2,512,128]{2,1,0:T(8,128)(2,1)S(1)}, u32[]{:S(2)}) copy-start(bf16[2,512,128]{2,1,0:T(8,128)(2,1)S(1)} %collective-permute-done.1.rest_1_) | copy-start | bytes 786436
  45.4 19.0 %collective-permute-start.10 = (bf16[2,512,128]{2,1,0:T(8,128)(2,1)}, bf16[2,512,128]{2,1,0:T(8,128)(2,1)S(1)}, u32[]{:S(2)}, u32[]{:S(2)}) collective-permute-start(bf16[2,512,128]{2,1,0:T(8,128)(2,1)} %get-tuple-element.79), channel_id=1, source_target_pairs={{0,30},{2,28},{4,2},{6,0},{8,6},{10,4},{12,10},{14,8},{16,14},{18,... | collective-permute-start | bytes 786440 | tf_op jit(solution)/shard_map/grad_cross/ppermute | solution.py:32
  46.1 1.5 %copy-start.1 = (bf16[8,320,512]{2,1,0:T(8,128)(2,1)}, bf16[8,320,512]{2,1,0:T(8,128)(2,1)S(1)}, u32[]{:S(2)}) copy-start(bf16[8,320,512]{2,1,0:T(8,128)(2,1)S(1)} %collective-permute-done.4.far_ref) | copy-start | bytes 7864324
  47.6 16.7 %copy-start.8 = (bf16[2,512,128]{2,1,0:T(8,128)(2,1)S(1)}, bf16[2,512,128]{2,1,0:T(8,128)(2,1)}, u32[]{:S(2)}) copy-start(bf16[2,512,128]{2,1,0:T(8,128)(2,1)} %get-tuple-element.76) | copy-start | bytes 786436
  62.9 4.5 %copy-start = (bf16[8,320,512]{2,1,0:T(8,128)(2,1)S(1)}, bf16[8,320,512]{2,1,0:T(8,128)(2,1)}, u32[]{:S(2)}) copy-start(bf16[8,320,512]{2,1,0:T(8,128)(2,1)} %get-tuple-element.80.near_ref) | copy-start | bytes 7864324
  62.9 2.7 %collective-permute-start.11 = (bf16[2,512,128]{2,1,0:T(8,128)(2,1)}, bf16[2,512,128]{2,1,0:T(8,128)(2,1)S(1)}, u32[]{:S(2)}, u32[]{:S(2)}) collective-permute-start(bf16[2,512,128]{2,1,0:T(8,128)(2,1)} %get-tuple-element.83), channel_id=1, source_target_pairs={{0,2},{2,0},{4,6},{6,4},{8,10},{10,8},{12,14},{14,12},{16,18},{18,... | collective-permute-start | bytes 786440 | tf_op jit(solution)/shard_map/grad_core/ppermute | solution.py:32
  64.3 8.6 %collective-permute-start.13 = (bf16[2,512,128]{2,1,0:T(8,128)(2,1)}, bf16[2,512,128]{2,1,0:T(8,128)(2,1)}, u32[]{:S(2)}, u32[]{:S(2)}) collective-permute-start(bf16[2,512,128]{2,1,0:T(8,128)(2,1)} %get-tuple-element.87), channel_id=1, source_target_pairs={{0,26},{2,0},{4,30},{6,4},{8,2},{10,8},{12,6},{14,12},{16,10},{18,... | collective-permute-start | bytes 786440 | tf_op jit(solution)/shard_map/grad_other/ppermute | solution.py:32
  64.5 2.9 %collective-permute-start.12 = (bf16[512,256]{1,0:T(8,128)(2,1)S(1)}, bf16[512,256]{1,0:T(8,128)(2,1)S(1)}, u32[]{:S(2)}, u32[]{:S(2)}) collective-permute-start(bf16[512,256]{1,0:T(8,128)(2,1)S(1)} %pad_maximum_fusion.2.own_ref.rest_0_), channel_id=1, source_target_pairs={{0,2},{2,0},{4,6},{6,4},{8,10},{10,8},{12,14},{14,12},{16,18},{18,... | collective-permute-start | bytes 786440 | tf_op jit(solution)/shard_map/own_core/ppermute | solution.py:32
  66.7 9.3 %collective-permute-start.14 = (bf16[2,512,128]{2,1,0:T(8,128)(2,1)S(1)}, bf16[2,512,128]{2,1,0:T(8,128)(2,1)}, u32[]{:S(2)}, u32[]{:S(2)}) collective-permute-start(bf16[2,512,128]{2,1,0:T(8,128)(2,1)S(1)} %add_convert_fusion.1), channel_id=1, source_target_pairs={{0,28},{2,30},{4,0},{6,2},{8,4},{10,6},{12,8},{14,10},{16,12},{18,... | collective-permute-start | bytes 786440 | tf_op jit(solution)/shard_map/grad_two/ppermute | solution.py:32
  67.1 26.0 %collective-permute-start.19 = (bf16[2560,256]{1,0:T(8,128)(2,1)}, bf16[2560,256]{1,0:T(8,128)(2,1)}, u32[]{:S(2)}, u32[]{:S(2)}) collective-permute-start(bf16[2560,256]{1,0:T(8,128)(2,1)} %collective-permute-done.5.rest_6_), channel_id=1, source_target_pairs={{0,2},{2,0},{4,6},{6,4},{8,10},{10,8},{12,14},{14,12},{16,18},{18,... | collective-permute-start | bytes 3932168 | tf_op jit(solution)/shard_map/weights_core/ppermute | solution.py:32
  67.4 1.7 %copy-start.2 = (bf16[8,320,512]{2,1,0:T(8,128)(2,1)S(1)}, bf16[8,320,512]{2,1,0:T(8,128)(2,1)}, u32[]{:S(2)}) copy-start(bf16[8,320,512]{2,1,0:T(8,128)(2,1)} %copy-done.1) | copy-start | bytes 7864324
  69.1 6.8 %copy-start.9 = (bf16[2,512,128]{2,1,0:T(8,128)(2,1)S(1)}, bf16[2,512,128]{2,1,0:T(8,128)(2,1)}, u32[]{:S(2)}) copy-start(bf16[2,512,128]{2,1,0:T(8,128)(2,1)} %get-tuple-element.86) | copy-start | bytes 786436
  71.4 18.6 %collective-permute-start.15 = (bf16[4,320,256]{2,1,0:T(8,128)(2,1)}, bf16[4,320,256]{2,1,0:T(8,128)(2,1)}, u32[]{:S(2)}, u32[]{:S(2)}) collective-permute-start(bf16[4,320,256]{2,1,0:T(8,128)(2,1)} %weight_send.2), channel_id=1, source_target_pairs={{0,4},{2,6},{4,0},{6,2},{8,12},{10,14},{12,8},{14,10},{16,20},{18,... | collective-permute-start | bytes 1966088 | tf_op jit(solution)/shard_map/terms_x/ppermute | solution.py:32
  77.2 2.2 %collective-permute-start.16 = (bf16[512,256]{1,0:T(8,128)(2,1)S(1)}, bf16[512,256]{1,0:T(8,128)(2,1)}, u32[]{:S(2)}, u32[]{:S(2)}) collective-permute-start(bf16[512,256]{1,0:T(8,128)(2,1)S(1)} %pad_maximum_fusion.3.own_ref.rest_1_), channel_id=1, source_target_pairs={{0,2},{2,0},{4,6},{6,4},{8,10},{10,8},{12,14},{14,12},{16,18},{18,... | collective-permute-start | bytes 786440 | tf_op jit(solution)/shard_map/own_core/ppermute | solution.py:32
  77.3 15.8 %collective-permute-start.17 = (bf16[512,256]{1,0:T(8,128)(2,1)S(1)}, bf16[512,256]{1,0:T(8,128)(2,1)S(1)}, u32[]{:S(2)}, u32[]{:S(2)}) collective-permute-start(bf16[512,256]{1,0:T(8,128)(2,1)S(1)} %pad_maximum_fusion.2.own_ref.rest_0_), channel_id=1, source_target_pairs={{0,1},{1,0},{2,3},{3,2},{4,5},{5,4},{6,7},{7,6},{8,9},{9,8},{10,11... | collective-permute-start | bytes 786440 | tf_op jit(solution)/shard_map/own_y/ppermute | solution.py:32
  79.0 14.1 %collective-permute-start.18 = (bf16[512,256]{1,0:T(8,128)(2,1)S(1)}, bf16[512,256]{1,0:T(8,128)(2,1)S(1)}, u32[]{:S(2)}, u32[]{:S(2)}) collective-permute-start(bf16[512,256]{1,0:T(8,128)(2,1)S(1)} %pad_maximum_fusion.3.own_ref.rest_1_), channel_id=1, source_target_pairs={{0,1},{1,0},{2,3},{3,2},{4,5},{5,4},{6,7},{7,6},{8,9},{9,8},{10,11... | collective-permute-start | bytes 786440 | tf_op jit(solution)/shard_map/own_y/ppermute | solution.py:32
  79.4 1.7 %copy-start.3 = (bf16[8,320,512]{2,1,0:T(8,128)(2,1)S(1)}, bf16[8,320,512]{2,1,0:T(8,128)(2,1)}, u32[]{:S(2)}) copy-start(bf16[8,320,512]{2,1,0:T(8,128)(2,1)} %copy-done.1) | copy-start | bytes 7864324
  82.9 20.5 %collective-permute-start.22 = (bf16[4,320,256]{2,1,0:T(8,128)(2,1)S(1)}, bf16[4,320,256]{2,1,0:T(8,128)(2,1)S(1)}, u32[]{:S(2)}, u32[]{:S(2)}) collective-permute-start(bf16[4,320,256]{2,1,0:T(8,128)(2,1)S(1)} %weight_send.3), channel_id=1, source_target_pairs={{0,4},{2,6},{4,0},{6,2},{8,12},{10,14},{12,8},{14,10},{16,20},{18,... | collective-permute-start | bytes 1966088 | tf_op jit(solution)/shard_map/terms_x/ppermute | solution.py:32
  84.9 8.2 %copy-start.5 = (bf16[5120,256]{1,0:T(8,128)(2,1)S(1)}, bf16[5120,256]{1,0:T(8,128)(2,1)}, u32[]{:S(2)}) copy-start(bf16[5120,256]{1,0:T(8,128)(2,1)} %rest_4_.5) | copy-start | bytes 7864324
  84.9 8.2 %copy-start.6 = (bf16[5120,256]{1,0:T(8,128)(2,1)S(1)}, bf16[5120,256]{1,0:T(8,128)(2,1)}, u32[]{:S(2)}) copy-start(bf16[5120,256]{1,0:T(8,128)(2,1)} %rest_5_.5) | copy-start | bytes 7864324
  84.9 8.2 %copy-start.7 = (s32[2]{0:T(128)S(1)}, s32[2]{0:T(128)}, u32[]{:S(2)}) copy-start(s32[2]{0:T(128)} %pad_add_fusion.at_ref) | copy-start | bytes 28
  92.0 9.0 %collective-permute-start.20 = (bf16[2,320,256]{2,1,0:T(8,128)(2,1)S(1)}, bf16[2,320,256]{2,1,0:T(8,128)(2,1)S(1)}, u32[]{:S(2)}, u32[]{:S(2)}) collective-permute-start(bf16[2,320,256]{2,1,0:T(8,128)(2,1)S(1)} %get-tuple-element.93), channel_id=1, source_target_pairs={{0,8},{2,10},{4,12},{6,14},{8,0},{10,2},{12,4},{14,6},{16,24},{18,... | collective-permute-start | bytes 983048 | tf_op jit(solution)/shard_map/terms_z1/ppermute | solution.py:32
  93.1 10.3 %copy-start.4 = (bf16[8,320,512]{2,1,0:T(8,128)(2,1)S(1)}, bf16[8,320,512]{2,1,0:T(8,128)(2,1)}, u32[]{:S(2)}) copy-start(bf16[8,320,512]{2,1,0:T(8,128)(2,1)} %copy-done.1) | copy-start | bytes 7864324
  101.0 9.2 %collective-permute-start.21 = (bf16[320,256]{1,0:T(8,128)(2,1)S(1)}, bf16[320,256]{1,0:T(8,128)(2,1)S(1)}, u32[]{:S(2)}, u32[]{:S(2)}) collective-permute-start(bf16[320,256]{1,0:T(8,128)(2,1)S(1)} %fusion.1), channel_id=1, source_target_pairs={{0,16},{2,18},{4,20},{6,22},{8,24},{10,26},{12,28},{14,30},{16,0},... | collective-permute-start | bytes 491528 | tf_op jit(solution)/shard_map/terms_z2/ppermute | solution.py:32
  105.2 11.7 %collective-permute-start.23 = (bf16[2,320,256]{2,1,0:T(8,128)(2,1)S(1)}, bf16[2,320,256]{2,1,0:T(8,128)(2,1)S(1)}, u32[]{:S(2)}, u32[]{:S(2)}) collective-permute-start(bf16[2,320,256]{2,1,0:T(8,128)(2,1)S(1)} %get-tuple-element.98), channel_id=1, source_target_pairs={{0,8},{2,10},{4,12},{6,14},{8,0},{10,2},{12,4},{14,6},{16,24},{18,... | collective-permute-start | bytes 983048 | tf_op jit(solution)/shard_map/terms_z1/ppermute | solution.py:32
  117.0 10.5 %collective-permute-start.24 = (bf16[320,256]{1,0:T(8,128)(2,1)S(1)}, bf16[320,256]{1,0:T(8,128)(2,1)S(1)}, u32[]{:S(2)}, u32[]{:S(2)}) collective-permute-start(bf16[320,256]{1,0:T(8,128)(2,1)S(1)} %fusion.2), channel_id=1, source_target_pairs={{0,16},{2,18},{4,20},{6,22},{8,24},{10,26},{12,28},{14,30},{16,0},... | collective-permute-start | bytes 491528 | tf_op jit(solution)/shard_map/terms_z2/ppermute | solution.py:32

commit v3 on v2

--- a/solution.py
+++ b/solution.py
@@ -18,8 +18,10 @@
 NN = (((1,), (0,)), ((), ()))
 TN = (((0,), (0,)), ((), ()))
 MIB = 1024 * 1024
-VMEM = 32 * MIB
+VMEM = 16 * MIB
+SMALL = 12 * MIB
 WHOLE = 58 * MIB
+ATTEND = 36 * MIB
 RESIDENT = pl.BlockSpec(memory_space=pltpu.VMEM)
 
 
@@ -125,7 +127,26 @@
     )(at, hidden, w_key, w_value)
 
 
-def attend_kernel(heads, sel_ref, len_ref, q_ref, do_ref, *rest):
+def attend_kernel(heads, loads, sel_ref, len_ref, q_ref, do_ref, *rest):
+    if loads:
+        sources, landed = rest[REACH + 2 : REACH + 2 + loads], rest[-10 - loads : -10]
+        load_sems = rest[-1]
+        rest = rest[: REACH + 2] + rest[REACH + 2 + loads : -10 - loads] + rest[-10:-1]
+        moves = [
+            pltpu.make_async_copy(src, dst, load_sems.at[i])
+            for i, (src, dst) in enumerate(zip(sources, landed))
+        ]
+
+        @pl.when(pl.program_id(0) == 0)
+        def _():
+            for move in moves:
+                move.start()
+
+        @pl.when(pl.program_id(0) == pl.num_programs(0) - 1)
+        def _():
+            for move in moves:
+                move.wait()
+
     kv_refs, (rk_ref, rv_ref), rest = rest[:REACH], rest[REACH : REACH + 2], rest[REACH + 2 :]
     (o_ref, dq_ref, rdk_ref, rdv_ref, *part_refs) = rest[-13 - REACH : -9]
     (prompt_s, sems, k_s, v_s, kt_s, vt_s, dk_s, dv_s, first_s) = rest[-9:]
@@ -218,7 +239,7 @@
                 part_ref[1] = (first_s[1] + dv_s[:plen]).astype(BF)
 
 
-def attend(g, sel, lengths, q, dout, kvs, rk, rv, prev):
+def attend(g, sel, lengths, q, dout, kvs, rk, rv, prev, loads=()):
     rows, width = q.shape
     slots = sel.shape[0]
     rlen = rows // slots
@@ -230,22 +251,26 @@
     narrow = pl.BlockSpec((rlen, HD), lambda r, *_: (r, g))
     ins = [q, dout, *kvs, rk, rv]
     in_specs = [wide, wide] + [pl.BlockSpec(memory_space=pltpu.HBM)] * REACH + [narrow, narrow]
+    ins += list(loads)
+    in_specs += [pl.BlockSpec(memory_space=pltpu.HBM)] * len(loads)
     aliases = {}
     if prev is not None:
         aliases = {2 + len(ins) + i: i for i in range(4)}
         ins += list(prev)
         in_specs += [pl.BlockSpec(memory_space=pl.ANY)] * 4
     return pl.pallas_call(
-        functools.partial(attend_kernel, heads),
+        functools.partial(attend_kernel, heads, len(loads)),
         out_shape=[jax.ShapeDtypeStruct(q.shape, BF)] * 2
         + [jax.ShapeDtypeStruct(rk.shape, BF)] * 2
-        + [jax.ShapeDtypeStruct((2, plen, HD), BF)] * REACH,
+        + [jax.ShapeDtypeStruct((2, plen, HD), BF)] * REACH
+        + [jax.ShapeDtypeStruct(x.shape, x.dtype) for x in loads],
         grid_spec=pltpu.PrefetchScalarGridSpec(
             num_scalar_prefetch=2,
             grid=(slots,),
             in_specs=in_specs,
             out_specs=[wide, wide, narrow, narrow]
-            + [pl.BlockSpec((2, plen, HD), lambda r, *_: (0, 0, 0))] * REACH,
+            + [pl.BlockSpec((2, plen, HD), lambda r, *_: (0, 0, 0))] * REACH
+            + [RESIDENT] * len(loads),
             scratch_shapes=[
                 pltpu.VMEM((slots, 2, plen, HD), BF),
                 pltpu.SemaphoreType.DMA((slots,)),
@@ -253,10 +278,11 @@
             + [pltpu.VMEM((klen, HD), BF)] * 2
             + [pltpu.VMEM((HD, klen), BF), pltpu.VMEM((HD + ONES, klen), BF)]
             + [pltpu.VMEM((klen, HD), F32)] * 2
-            + [pltpu.VMEM((2, plen, HD), F32)],
+            + [pltpu.VMEM((2, plen, HD), F32)]
+            + [pltpu.SemaphoreType.DMA((len(loads),))] * bool(loads),
         ),
         input_output_aliases=aliases,
-        compiler_params=pltpu.CompilerParams(vmem_limit_bytes=WHOLE),
+        compiler_params=pltpu.CompilerParams(vmem_limit_bytes=ATTEND),
         cost_estimate=pl.CostEstimate(
             flops=slots * heads * 24 * rlen * klen * HD,
             bytes_accessed=8 * MIB,
@@ -266,110 +292,84 @@
     )(sel, lengths, *ins)
 
 
-def weight_kernel(index_ref, near_ref, far_ref, own_ref, pair_ref, *rest):
-    count = near_ref.shape[0] // 2
-    arrived, outs = (rest[0], rest[1:]) if len(rest) > 1 else (None, rest)
-    own, pair = own_ref[...], pair_ref[...]
+def weight_kernel(first, at_ref, near_ref, far_ref, own_ref, pair_ref, *rest):
+    count = at_ref.shape[0]
+    arrived, outs = (rest[0], rest[1:]) if rest[0].shape[0] == count and len(rest) > 1 else (None, rest)
+    width = outs[0].shape[2]
+    own = own_ref[:, first : first + width]
+    pair = pair_ref[:, first : first + width]
+    each = outs[0].shape[0]
     for i in range(count):
-        at = i ^ index_ref[1]
-        chunk = 2 * at + index_ref[0]
+        chunk = at_ref[i]
         total = mm(near_ref[chunk], own) + mm(far_ref[chunk], pair)
         if arrived is not None:
-            total += arrived[at].astype(F32)
-        if len(outs) == 2:
-            outs[i % 2][i // 2] = total.astype(BF)
-        else:
-            outs[0][at] = total.astype(BF)
-
-
-def weight_terms(index, near, far, own, pair, arrived):
-    count, chunk, rows = near.shape
-    count //= 2
-    ins = [near, far, own, pair]
-    if arrived is not None:
-        ins.append(arrived)
-    if arrived is not None and count == REACH:
-        out_shape = [jax.ShapeDtypeStruct((count // 2, chunk, 2 * HD), BF)] * 2
-        out_specs = [RESIDENT] * 2
-    else:
-        out_shape = jax.ShapeDtypeStruct((count, chunk, 2 * HD), BF)
-        out_specs = RESIDENT
+            total += arrived[i].astype(F32)
+        outs[i // each][i % each] = total.astype(BF)
+
+
+def weight_terms(at, near, far, grads, columns, arrived=None, parts=1):
+    own, pair = grads
+    chunk, rows = near.shape[1:]
+    count = at.shape[0]
+    first, width = columns
+    ins = [near, far, own, pair] + ([] if arrived is None else [arrived])
     return pl.pallas_call(
-        weight_kernel,
-        out_shape=out_shape,
+        functools.partial(weight_kernel, first),
+        out_shape=[jax.ShapeDtypeStruct((count // parts, chunk, width), BF)] * parts,
         in_specs=[pl.BlockSpec(memory_space=pltpu.SMEM)] + [RESIDENT] * len(ins),
-        out_specs=out_specs,
-        compiler_params=pltpu.CompilerParams(vmem_limit_bytes=VMEM),
+        out_specs=[RESIDENT] * parts,
+        compiler_params=pltpu.CompilerParams(vmem_limit_bytes=SMALL),
         cost_estimate=pl.CostEstimate(
-            flops=8 * rows * count * chunk * HD,
-            bytes_accessed=4 * count * chunk * (rows + 2 * HD),
+            flops=4 * rows * count * chunk * width,
+            bytes_accessed=4 * count * chunk * (rows + width),
             transcendentals=0,
         ),
-        name="weight_keep" if arrived is not None else "weight_send",
-    )(index, *ins)
-
-
-def halve(held, index, bit):
-    count = held.shape[0]
-    while count > 1:
-        mine = (index // bit) % 2
-        split = held.reshape(count // 2, 2, *held.shape[1:])
-        out = lax.dynamic_index_in_dim(split, 1 - mine, 1, keepdims=False).astype(BF)
-        stay = lax.dynamic_index_in_dim(split, mine, 1, keepdims=False).astype(F32)
-        held = stay + permute(out, "dp", lambda i: i ^ bit, "terms_halved").astype(F32)
-        count //= 2
-        bit *= 2
-    return held[0]
-
-
-def place_index(index):
-    return (index // 2) % 2, index // 4, jnp.zeros_like(index)
-
-
-def send_terms(index, near, far, own, pair):
-    bit, _, zero = place_index(index)
-    return weight_terms(jnp.stack([1 - bit, zero]), near, far, own, pair, None)
-
-
-def keep_terms(index, near, far, own, pair, arrived):
-    bit, place, zero = place_index(index)
-    if near.shape[0] // 2 != REACH:
-        held = weight_terms(jnp.stack([bit, zero]), near, far, own, pair, arrived)
-        return [halve(held, index, 4)]
-    kept, sent = weight_terms(jnp.stack([bit, place]), near, far, own, pair, arrived)
-    return [kept, permute(sent, "dp", lambda i: i ^ 4, "terms_z1")]
-
-
-def cross_terms(held):
-    if len(held) == 1:
-        return held
-    kept, sent = held
-    two = (kept[1].astype(F32) + sent[1].astype(F32)).astype(BF)
-    return [kept[0], sent[0], permute(two, "dp", lambda i: i ^ 8, "terms_z2")]
+        name="weight_terms",
+    )(at, *ins)
+
+
+def add(one, two):
+    return one.astype(F32) + two.astype(F32)
 
 
 def hidden_kernel(groups, at_ref, *rest):
     owns, fars, rest = rest[:groups], rest[groups : 2 * groups], rest[2 * groups :]
-    (wk_ref, wv_ref, wa_ref, wb_ref, out_ref, grads) = rest
+    (wk_ref, wv_ref, wa_ref, wb_ref, out_ref, grads, weights, done, in_sems, out_sems) = rest
     cols = wa_ref.shape[0]
-    step = pl.program_id(0)
-    tile = out_ref.shape[1]
-
-    @pl.when(step == 0)
-    def _():
-        first = at_ref[1]
-        for g in range(groups):
-            at = pl.ds(g * HD, HD)
-            for j in range(2):
-                grads[j, :, at] = owns[g][:, j * HD : (j + 1) * HD]
-                away = pl.multiple_of(jnp.where(first == 0, j, 1 - j) * HD, HD)
-                grads[2 + j, :, at] = fars[g][:, pl.ds(away, HD)]
-
-    near = pl.ds(pl.multiple_of(at_ref[0] * cols + step * tile, tile), tile)
-    away = pl.ds(pl.multiple_of(step * tile, tile), tile)
-    total = mm(grads[0], wk_ref[near, :], NT) + mm(grads[1], wv_ref[near, :], NT)
-    total += mm(grads[2], wa_ref[away, :], NT) + mm(grads[3], wb_ref[away, :], NT)
-    out_ref[...] = total.astype(BF)
+    steps, tile = weights.shape[1:3]
+    copies = []
+    for step in range(steps):
+        near = pl.ds(pl.multiple_of(at_ref[0] * cols + step * tile, tile), tile)
+        away = pl.ds(step * tile, tile)
+        sources = (wk_ref.at[near], wv_ref.at[near], wa_ref.at[away], wb_ref.at[away])
+        copies.append(
+            [
+                pltpu.make_async_copy(source, weights.at[j, step], in_sems.at[j, step])
+                for j, source in enumerate(sources)
+            ]
+        )
+        for copy in copies[-1]:
+            copy.start()
+    first = at_ref[1]
+    for g in range(groups):
+        at = pl.ds(g * HD, HD)
+        for j in range(2):
+            grads[j, :, at] = owns[g][:, j * HD : (j + 1) * HD]
+            away = pl.multiple_of(jnp.where(first == 0, j, 1 - j) * HD, HD)
+            grads[2 + j, :, at] = fars[g][:, pl.ds(away, HD)]
+    leaving = []
+    for step in range(steps):
+        for copy in copies[step]:
+            copy.wait()
+        total = mm(grads[0], weights[0, step], NT)
+        for j in range(1, 4):
+            total += mm(grads[j], weights[j, step], NT)
+        done[step] = total.astype(BF)
+        there = out_ref.at[:, pl.ds(step * tile, tile)]
+        leaving.append(pltpu.make_async_copy(done.at[step], there, out_sems.at[step]))
+        leaving[-1].start()
+    for copy in leaving:
+        copy.wait()
 
 
 def hidden_grads(at, owns, fars, w_key, w_value, far_a, far_b):
@@ -377,16 +377,22 @@
     rows = owns[0].shape[0]
     cols, width = far_a.shape
     tile = 512
+    steps = cols // tile
+    far = pl.BlockSpec(memory_space=pltpu.HBM)
     return pl.pallas_call(
         functools.partial(hidden_kernel, groups),
         out_shape=jax.ShapeDtypeStruct((rows, cols), BF),
-        grid_spec=pltpu.PrefetchScalarGridSpec(
-            num_scalar_prefetch=1,
-            grid=(cols // tile,),
-            in_specs=[RESIDENT] * (2 * groups + 4),
-            out_specs=pl.BlockSpec((rows, tile), lambda i, at: (0, i)),
-            scratch_shapes=[pltpu.VMEM((4, rows, width), BF)],
-        ),
+        in_specs=[pl.BlockSpec(memory_space=pltpu.SMEM)]
+        + [RESIDENT] * (2 * groups)
+        + [far] * 4,
+        out_specs=far,
+        scratch_shapes=[
+            pltpu.VMEM((4, rows, width), BF),
+            pltpu.VMEM((4, steps, tile, width), BF),
+            pltpu.VMEM((steps, rows, tile), BF),
+            pltpu.SemaphoreType.DMA((4, steps)),
+            pltpu.SemaphoreType.DMA((steps,)),
+        ],
         compiler_params=pltpu.CompilerParams(vmem_limit_bytes=VMEM),
         cost_estimate=pl.CostEstimate(
             flops=8 * rows * cols * width,
@@ -459,42 +465,114 @@
         permute(core_0, "dp", cross, "grad_cross"),
     ]
     received[1], far, far_a, prev = after((received[1], far, far_a, prev), mine_0)
-    *prev, mine_1, other_1, two_1, core_1 = attend(
-        1, sel, resp_length, queries, cotangent, received[1], resp_key, resp_value, prev
+    *prev, mine_1, other_1, two_1, core_1, near, far = attend(
+        1,
+        sel,
+        resp_length,
+        queries,
+        cotangent,
+        received[1],
+        resp_key,
+        resp_value,
+        prev,
+        (near, far),
     )
     far_b = permute(far_a, "dp", lambda i: i ^ 1, "weights_core")
     swapped = permute(core_1, "dp", lambda i: i ^ 1, "grad_core")
     shares_1 = [permute(other_1, "dp", back, "grad_other")]
-
-    def along_x(i):
-        return i ^ 2
 
     own = [total_grad(after(mine_0, mine_1), shares)]
     pair = [permute(own[0], "dp", lambda i: i ^ 1, "own_core")]
     two = after((two_1.astype(F32) + swapped.astype(F32)).astype(BF), own[0])
     shares_1.append(permute(two, "dp", lambda i: (i - 2) % size, "grad_two"))
-    sent = [send_terms(index, near, far, after(own[0], two), pair[0])]
-    arrived = [permute(sent[0], "dp", along_x, "terms_x")]
-
-    own.append(total_grad(after(mine_1, sent[0]), shares_1))
+
+    bit, place = (index // 2) % 2, index // 4
+    count = near.shape[0]
+
+    def places(shifts, flips):
+        return jnp.stack([2 * (place ^ i) + (bit ^ x) for i in shifts for x in flips])
+
+    def along(block, bits, name):
+        return permute(block, "dp", lambda i: i ^ bits, name)
+
+    def far_sum(kept, rest, bits):
+        while rest:
+            sent = jnp.stack([rest[0]] + rest[1:][1::2])
+            got = along(sent.astype(BF), bits, "terms_z")
+            kept = add(kept, got[0])
+            rest = [add(r, g) for r, g in zip(rest[1:][0::2], got[1:])]
+            bits *= 2
+        return kept
+
+    whole = (0, 2 * HD)
+    every = range(count // 2)
+    if count // 2 != REACH:
+        owns = own + [total_grad(mine_1, shares_1)]
+        weight_grads = []
+        for grad in owns:
+            grads = (grad, permute(grad, "dp", lambda i: i ^ 1, "own_core"))
+            (sent,) = weight_terms(places(every, [1]), near, far, grads, whole)
+            got = along(sent, 2, "terms_x")
+            (held,) = weight_terms(places(every, [0]), near, far, grads, whole, got)
+            weight_grads.append(far_sum(held[0], list(held[1:]), 4))
+        away = [permute(grad, "mp", lambda i: 1 - i, "own_y") for grad in owns]
+        hidden_grad = hidden_grads(at, owns, away, w_key, w_value, far_a, far_b)
+        keys = [t[:, :HD] for t in weight_grads]
+        values = [t[:, HD:] for t in weight_grads]
+        return (
+            *prev,
+            hidden_grad,
+            jnp.concatenate(keys, axis=-1),
+            jnp.concatenate(values, axis=-1),
+        )
+
+    key, value = (0, HD), (HD, HD)
+    near_first, near_then = [0, 2], [1, 3]
+    every = near_first + near_then
+    grads_0 = (after(own[0], two), pair[0])
+    (sent_0,) = weight_terms(places(every, [1]), near, far, grads_0, whole)
+    got_0 = along(sent_0, 2, "terms_x")
+    away = [permute(after(own[0], sent_0), "mp", lambda i: 1 - i, "own_y")]
+    own.append(total_grad(after(mine_1, sent_0, away[0]), shares_1))
     pair.append(permute(own[1], "dp", lambda i: i ^ 1, "own_core"))
-    sent.append(send_terms(index, near, far, own[1], pair[1]))
-    arrived.append(permute(sent[1], "dp", along_x, "terms_x"))
-    away = [permute(grad, "mp", lambda i: 1 - i, "own_y") for grad in own]
-
-    held = [keep_terms(index, near, far, own[0], pair[0], after(arrived[0], sent[1]))]
+    grads_1 = (own[1], pair[1])
+    (sent_v,) = weight_terms(places([1, 3], [0, 1]), near, far, grads_1, value)
+    got_v = along(sent_v, 4, "terms_z1")
+    (sent_k,) = weight_terms(places(every, [1]), near, far, (after(own[1], sent_v), pair[1]), key)
+    got_k = along(sent_k, 2, "terms_x")
+
+    held_0, sent_0 = weight_terms(
+        places(every, [0]), near, far, grads_0, whole,
+        after(got_0, sent_k), 2,
+    )
+    got_0 = along(sent_0, 4, "terms_z1")
+    away.append(permute(after(own[1], held_0), "mp", lambda i: 1 - i, "own_y"))
+    held_v, sent_v = weight_terms(
+        places(near_first, [0, 1]), near, far, grads_1, value, after(got_v, held_0), 2
+    )
+    got_v = along(sent_v, 8, "terms_z2")
+    held_k, sent_k = weight_terms(
+        places(every, [0]), near, far, grads_1, key, after(got_k, held_v, away[1]), 2
+    )
+    got_k = along(sent_k, 4, "terms_z1")
+    two_0 = add(held_0[1], after(got_0, held_k)[1]).astype(BF)
+    last_0 = along(two_0, 8, "terms_z2")
+    two_v = add(held_v[1], after(got_v, two_0)[1]).astype(BF)
+    last_v = along(two_v, 2, "terms_x")
+    two_k = add(held_k[1], after(got_k, two_v)[1]).astype(BF)
+    last_k = along(two_k, 8, "terms_z2")
     hidden_grad = hidden_grads(
-        at, after(own, held[0][0]), away, w_key, w_value, far_a, far_b
-    )
-    terms = [cross_terms(after(held[0], hidden_grad))]
-    held.append(keep_terms(index, near, far, own[1], pair[1], after(arrived[1], terms[0][:2][-1])))
-    terms.append(cross_terms(held[1]))
-    weight_grads = [sum(t.astype(F32) for t in term) for term in terms]
+        at, after(own, two_0, two_v, two_k), away, w_key, w_value, far_a, far_b
+    )
+    last_0, last_v, last_k = after((last_0, last_v, last_k), hidden_grad)
+    total_0 = add(add(held_0[0], got_0[0]), last_0)
+    total_v = add(add(held_v[0], got_v[0]), last_v)
+    total_k = add(add(held_k[0], got_k[0]), last_k)
     return (
         *prev,
         hidden_grad,
-        jnp.concatenate([t[:, :HD] for t in weight_grads], axis=-1),
-        jnp.concatenate([t[:, HD:] for t in weight_grads], axis=-1),
+        jnp.concatenate([total_0[:, :HD], total_k], axis=-1),
+        jnp.concatenate([total_0[:, HD:], total_v], axis=-1),
     )
 
 

time: 129 us -> 122 us (0.946)
  waiting for transfers between devices: 39.6 us -> 32.3 us
  starting transfers between devices: 23.7 us -> 27.3 us
  Pallas kernels: 53.7 us -> 50.7 us
  other arithmetic: 4.73 us -> 3.08 us
  local copies, waits for them, and re-layouts: 5.78 us -> 7.39 us
    ppermute x25 -> x28, waiting for transfers between devices: 39.6 us -> 32.3 us  [permute(): lax.ppermute(block, axis, [(i, target(i)) for i in range(lax.axis_size(ax...]
    ppermute x25 -> x28, starting transfers between devices: 23.7 us -> 27.3 us  [permute(): lax.ppermute(block, axis, [(i, target(i)) for i in range(lax.axis_size(ax...]
    pallas_call x6 -> x8, Pallas kernels: 38.2 us -> 36.2 us  [the longest x2 26.5 us: attend(): pl.pallas_call(functools.partial(attend_kernel, heads, len(loads)), out_s...]
    unnamed x34 -> x48, local copies, waits for them, and re-layouts: 5.69 us -> 7.33 us
  transfers between devices with their start and end apart: 25 -> 28, of which waited for: 9 -> 11; matrix products, arithmetic and copies ran while one was open for 3% -> 1% of each run, Pallas kernels for 35% -> 33%
where the time goes in v3:
time: 122 us
  Pallas kernels  50.7 us (42%)
  waiting for transfers between devices  32.3 us (26%)
  starting transfers between devices  27.3 us (22%)
  local copies, waits for them, and re-layouts  7.39 us (6%)
  other arithmetic  3.08 us (3%)
    ppermute x28, waiting for transfers between devices, permute(): lax.ppermute(block, axis, [(i, target(i)) for i in range(lax.axis_size(ax...  32.3 us
    ppermute x28, starting transfers between devices, permute(): lax.ppermute(block, axis, [(i, target(i)) for i in range(lax.axis_size(ax...  27.3 us
    pallas_call x2, Pallas kernels, attend(): pl.pallas_call(functools.partial(attend_kernel, heads, len(loads)), out_s...  26.5 us
    pallas_call x6, Pallas kernels, weight_terms(): pl.pallas_call(functools.partial(weight_kernel, first), out_shape=[jax.Sh...  9.7 us
    pallas_call x1, Pallas kernels, project(): pl.pallas_call(functools.partial(project_kernel, groups), out_shape=[jax....  8.21 us
    unnamed x48, local copies, waits for them, and re-layouts  7.33 us
    pallas_call x1, Pallas kernels, hidden_grads(): pl.pallas_call(functools.partial(hidden_kernel, groups), out_shape=jax.Sh...  6.29 us
  transfers between devices with their start and end apart: 28, of which 11 were waited for; matrix products, arithmetic and copies ran while one was open for 1% of the time, Pallas kernels for 33%

profile of v3, /device:TPU:0, one launch (start us, length us, event | category | flops | bytes accessed | tf_op | source)
XLA Modules:
  0.0 121.9 jit_solution(11344781971746363527)
XLA Ops:
  0.6 0.7 pad_add_fusion.at_ref
  1.3 8.2 %project.1 = (bf16[2,512,128]{2,1,0:T(8,128)(2,1)}, bf16[2,512,128]{2,1,0:T(8,128)(2,1)}, bf16[8,320,512]{2,1,0:T(8,128)(2,1)}, bf16[8,320,512]{2,1,0:T(8,128)(2,1)}, bf16[2560,256]{1,0:T(8,128)(2,1)}) custom-call(s32[2]{0:T(128)} %pad_add_fusion.at_ref, bf16[512,5120]{1,0:T(8,128)(2,1)} %h_ref.1, bf16[5120,256]{1,0:T(8,128)(2,1)} %rest_4_.5, ...), custom_call_target="tpu_custom_call" | custom-call | flops 2684354560 | bytes 15728640 | tf_op jit(solution)/shard_map/project/pallas_call | solution.py:105
  9.5 0.5 collective-permute-start.4
  10.0 2.5 %collective-permute-start = (bf16[2,512,128]{2,1,0:T(8,128)(2,1)}, bf16[2,512,128]{2,1,0:T(8,128)(2,1)}, u32[]{:S(2)}, u32[]{:S(2)}) collective-permute-start(bf16[2,512,128]{2,1,0:T(8,128)(2,1)} %get-tuple-element.66.rest_0_), channel_id=1, source_target_pairs={{0,4},{2,6},{4,8},{6,10},{8,12},{10,14},{12,16},{14,18},{16,20},{1... | collective-permute-start | bytes 786440 | tf_op jit(solution)/shard_map/pair_two/ppermute | solution.py:34
  12.6 1.5 %collective-permute-start.5 = (bf16[2560,256]{1,0:T(8,128)(2,1)}, bf16[2560,256]{1,0:T(8,128)(2,1)S(1)}, u32[]{:S(2)}, u32[]{:S(2)}) collective-permute-start(bf16[2560,256]{1,0:T(8,128)(2,1)} %get-tuple-element.69), channel_id=1, source_target_pairs={{0,1},{1,0},{2,3},{3,2},{4,5},{5,4},{6,7},{7,6},{8,9},{9,8},{10,11... | collective-permute-start | bytes 3932168 | tf_op jit(solution)/shard_map/weights_y/ppermute | solution.py:34
  14.1 9.0 %collective-permute-done.rest_2_ = bf16[2,512,128]{2,1,0:T(8,128)(2,1)} collective-permute-done((bf16[2,512,128]{2,1,0:T(8,128)(2,1)}, bf16[2,512,128]{2,1,0:T(8,128)(2,1)}, u32[]{:S(2)}, u32[]{:S(2)}) %collective-permute-start) | collective-permute-done | bytes 262176 | tf_op jit(solution)/shard_map/pair_two/ppermute | solution.py:34
  23.1 0.0 copy-start.11
  23.1 0.0 copy-start.13
  23.2 0.1 collective-permute-start.3
  23.2 3.0 %collective-permute-start.2 = (bf16[2,512,128]{2,1,0:T(8,128)(2,1)}, bf16[2,512,128]{2,1,0:T(8,128)(2,1)S(1)}, u32[]{:S(2)}, u32[]{:S(2)}) collective-permute-start(bf16[2,512,128]{2,1,0:T(8,128)(2,1)} %get-tuple-element.75.rest_0_), channel_id=1, source_target_pairs={{0,4},{2,6},{4,8},{6,10},{8,12},{10,14},{12,16},{14,18},{16,20},{1... | collective-permute-start | bytes 786440 | tf_op jit(solution)/shard_map/pair_two/ppermute | solution.py:34
  26.3 1.6 %copy-done.14 = bf16[512,2048]{1,0:T(8,128)(2,1)S(1)} copy-done((bf16[512,2048]{1,0:T(8,128)(2,1)S(1)}, bf16[512,2048]{1,0:T(8,128)(2,1)}, u32[]{:S(2)}) %copy-start.14) | copy-done | bytes 2097176
  27.9 0.9 copy-done.16
  28.8 0.9 copy-done.18
  29.8 0.9 copy-done.21
  30.7 13.6 %attend_0.1 = (bf16[512,2048]{1,0:T(8,128)(2,1)}, bf16[512,2048]{1,0:T(8,128)(2,1)}, bf16[512,256]{1,0:T(8,128)(2,1)}, bf16[512,256]{1,0:T(8,128)(2,1)}, bf16[2,...) custom-call(s32[2]{0:T(128)S(1)} %and_select_fusion.sel_ref, ...), custom_call_target="tpu_custom_call" | custom-call | flops 9663676416 | bytes 8388608 | tf_op jit(solution)/shard_map/attend_0/pallas_call | solution.py:261
  44.3 3.6 %collective-permute-start.8 = (bf16[2,512,128]{2,1,0:T(8,128)(2,1)S(1)}, bf16[2,512,128]{2,1,0:T(8,128)(2,1)S(1)}, u32[]{:S(2)}, u32[]{:S(2)}) collective-permute-start(bf16[2,512,128]{2,1,0:T(8,128)(2,1)S(1)} %get-tuple-element.91), channel_id=1, source_target_pairs={{0,26},{2,0},{4,30},{6,4},{8,2},{10,8},{12,6},{14,12},{16,10},{18,... | collective-permute-start | bytes 786440 | tf_op jit(solution)/shard_map/grad_other/ppermute | solution.py:34
  47.9 1.3 %collective-permute-start.10 = (bf16[2,512,128]{2,1,0:T(8,128)(2,1)S(1)}, bf16[2,512,128]{2,1,0:T(8,128)(2,1)S(1)}, u32[]{:S(2)}, u32[]{:S(2)}) collective-permute-start(bf16[2,512,128]{2,1,0:T(8,128)(2,1)S(1)} %get-tuple-element.93), channel_id=1, source_target_pairs={{0,30},{2,28},{4,2},{6,0},{8,6},{10,4},{12,10},{14,8},{16,14},{18,... | collective-permute-start | bytes 786440 | tf_op jit(solution)/shard_map/grad_cross/ppermute | solution.py:34
  49.2 1.1 copy-done.4
  50.3 12.9 %attend_1.1 = (bf16[512,2048]{1,0:T(8,128)(2,1)}, bf16[512,2048]{1,0:T(8,128)(2,1)}, bf16[512,256]{1,0:T(8,128)(2,1)}, bf16[512,256]{1,0:T(8,128)(2,1)}, bf16[2,...) custom-call(s32[2]{0:T(128)S(1)} %and_select_fusion.sel_ref, ...), custom_call_target="tpu_custom_call", output_to_operand_aliasing={{0}: (12, {}), {1}: (13, {}), {2}: (14, {}), {3}: (15, {})} | custom-call | flops 9663676416 | bytes 8388608 | tf_op jit(solution)/shard_map/attend_1/pallas_call | solution.py:261
  63.3 1.0 collective-permute-start.11
  64.2 0.1 add_convert_fusion.2
  64.5 0.1 collective-permute-start.12
  64.6 0.1 add_add_fusion.at_ref
  64.6 0.8 collective-permute-done.11
  65.4 0.1 add_convert_fusion.1
  65.5 0.6 collective-permute-done.12.pair_ref
  66.1 2.2 %weight_terms.6 = bf16[4,320,256]{2,1,0:T(8,128)(2,1)} custom-call(s32[4]{0:T(128)S(1)} %add_add_fusion.at_ref, bf16[8,320,512]{2,1,0:T(8,128)(2,1)S(1)} %get-tuple-element.94.near_ref, bf16[8,320,512]{2,1,0:T(8,128)(2,1)S(1)} %get-tuple-element.95.far_ref, bf16[512,256]{1,0:T(8,128)(2,1)S(1)} %pad_maximum_fusion.2.own_ref.rest_0_, ...), custom_call_target="tpu_custom_call" | custom-call | flops 671088640 | bytes 3932160 | tf_op jit(solution)/shard_map/weight_terms/pallas_call | solution.py:316
  68.3 1.6 %collective-permute-start.13 = (bf16[512,256]{1,0:T(8,128)(2,1)S(1)}, bf16[512,256]{1,0:T(8,128)(2,1)S(1)}, u32[]{:S(2)}, u32[]{:S(2)}) collective-permute-start(bf16[512,256]{1,0:T(8,128)(2,1)S(1)} %pad_maximum_fusion.2.own_ref.rest_0_), channel_id=1, source_target_pairs={{0,1},{1,0},{2,3},{3,2},{4,5},{5,4},{6,7},{7,6},{8,9},{9,8},{10,11... | collective-permute-start | bytes 786440 | tf_op jit(solution)/shard_map/own_y/ppermute | solution.py:34
  69.9 1.4 %collective-permute-start.15 = (bf16[2,512,128]{2,1,0:T(8,128)(2,1)S(1)}, bf16[2,512,128]{2,1,0:T(8,128)(2,1)S(1)}, u32[]{:S(2)}, u32[]{:S(2)}) collective-permute-start(bf16[2,512,128]{2,1,0:T(8,128)(2,1)S(1)} %add_convert_fusion.1), channel_id=1, source_target_pairs={{0,28},{2,30},{4,0},{6,2},{8,4},{10,6},{12,8},{14,10},{16,12},{18,... | collective-permute-start | bytes 786440 | tf_op jit(solution)/shard_map/grad_two/ppermute | solution.py:34
  71.4 0.6 collective-permute-start.16
  71.9 4.7 %collective-permute-done.13.rest_2_ = bf16[512,256]{1,0:T(8,128)(2,1)S(1)} collective-permute-done((bf16[512,256]{1,0:T(8,128)(2,1)S(1)}, bf16[512,256]{1,0:T(8,128)(2,1)S(1)}, u32[]{:S(2)}, u32[]{:S(2)}) %collective-permute-start.13) | collective-permute-done | bytes 262176 | tf_op jit(solution)/shard_map/own_y/ppermute | solution.py:34
  76.6 2.8 %collective-permute-done.15 = bf16[2,512,128]{2,1,0:T(8,128)(2,1)S(1)} collective-permute-done((bf16[2,512,128]{2,1,0:T(8,128)(2,1)S(1)}, bf16[2,512,128]{2,1,0:T(8,128)(2,1)S(1)}, u32[]{:S(2)}, u32[]{:S(2)}) %collective-permute-start.15) | collective-permute-done | bytes 262176 | tf_op jit(solution)/shard_map/grad_two/ppermute | solution.py:34
  79.4 0.1 add_convert_fusion
  79.6 0.1 collective-permute-start.17
  79.7 0.5 collective-permute-start.24
  80.2 0.1 add_add_fusion.1.at_ref
  80.3 0.1 pad_add_fusion.1.at_ref
  80.3 0.9 collective-permute-done.17.pair_ref
  81.2 1.7 %copy-done.1 = bf16[8,320,512]{2,1,0:T(8,128)(2,1)S(1)} copy-done((bf16[8,320,512]{2,1,0:T(8,128)(2,1)S(1)}, bf16[8,320,512]{2,1,0:T(8,128)(2,1)}, u32[]{:S(2)}) %copy-start.1) | copy-done | bytes 2621464
  83.0 1.4 %weight_terms.7 = bf16[4,320,128]{2,1,0:T(8,128)(2,1)S(1)} custom-call(s32[4]{0:T(128)S(1)} %add_add_fusion.1.at_ref, bf16[8,320,512]{2,1,0:T(8,128)(2,1)S(1)} %get-tuple-element.94.near_ref, bf16[8,320,512]{2,1,0:T(8,128)(2,1)S(1)} %copy-done.1, bf16[512,256]{1,0:T(8,128)(2,1)S(1)} %pad_maximum_fusion.3.own_ref.rest_1_, ...), custom_call_target="tpu_custom_call" | custom-call | flops 335544320 | bytes 3276800 | tf_op jit(solution)/shard_map/weight_terms/pallas_call | solution.py:316
  84.3 1.3 %collective-permute-start.20 = (bf16[4,320,128]{2,1,0:T(8,128)(2,1)S(1)}, bf16[4,320,128]{2,1,0:T(8,128)(2,1)S(1)}, u32[]{:S(2)}, u32[]{:S(2)}) collective-permute-start(bf16[4,320,128]{2,1,0:T(8,128)(2,1)S(1)} %weight_terms.7), channel_id=1, source_target_pairs={{0,8},{2,10},{4,12},{6,14},{8,0},{10,2},{12,4},{14,6},{16,24},{18,... | collective-permute-start | bytes 983048 | tf_op jit(solution)/shard_map/terms_z1/ppermute | solution.py:34
  85.6 1.4 %weight_terms.8 = bf16[4,320,128]{2,1,0:T(8,128)(2,1)S(1)} custom-call(s32[4]{0:T(128)S(1)} %add_add_fusion.at_ref, bf16[8,320,512]{2,1,0:T(8,128)(2,1)S(1)} %get-tuple-element.94.near_ref, bf16[8,320,512]{2,1,0:T(8,128)(2,1)S(1)} %copy-done.1, bf16[512,256]{1,0:T(8,128)(2,1)S(1)} %pad_maximum_fusion.3.own_ref.rest_1_, ...), custom_call_target="tpu_custom_call" | custom-call | flops 335544320 | bytes 3276800 | tf_op jit(solution)/shard_map/weight_terms/pallas_call | solution.py:316
  87.0 2.3 %collective-permute-start.19 = (bf16[4,320,128]{2,1,0:T(8,128)(2,1)S(1)}, bf16[4,320,128]{2,1,0:T(8,128)(2,1)S(1)}, u32[]{:S(2)}, u32[]{:S(2)}) collective-permute-start(bf16[4,320,128]{2,1,0:T(8,128)(2,1)S(1)} %weight_terms.8), channel_id=1, source_target_pairs={{0,4},{2,6},{4,0},{6,2},{8,12},{10,14},{12,8},{14,10},{16,20},{18,... | collective-permute-start | bytes 983048 | tf_op jit(solution)/shard_map/terms_x/ppermute | solution.py:34
  89.3 3.9 %collective-permute-done.16.rest_0_ = bf16[4,320,256]{2,1,0:T(8,128)(2,1)} collective-permute-done((bf16[4,320,256]{2,1,0:T(8,128)(2,1)}, bf16[4,320,256]{2,1,0:T(8,128)(2,1)}, u32[]{:S(2)}, u32[]{:S(2)}) %collective-permute-start.16) | collective-permute-done | bytes 655392 | tf_op jit(solution)/shard_map/terms_x/ppermute | solution.py:34
  93.2 2.0 %weight_terms.9 = (bf16[2,320,256]{2,1,0:T(8,128)(2,1)S(1)}, bf16[2,320,256]{2,1,0:T(8,128)(2,1)S(1)}) custom-call(s32[4]{0:T(128)S(1)} %pad_add_fusion.1.at_ref, bf16[8,320,512]{2,1,0:T(8,128)(2,1)S(1)} %get-tuple-element.94.near_ref, bf16[8,320,512]{2,1,0:T(8,128)(2,1)S(1)} %copy-done.1, bf16[512,256]{1,0:T(8,128)(2,1)S(1)} %pad_maximum_fusion.2.own_ref.rest_0_, ...), custom_call_target="tpu_custom_call" | custom-call | flops 671088640 | bytes 3932160 | tf_op jit(solution)/shard_map/weight_terms/pallas_call | solution.py:316
  95.1 1.6 %collective-permute-start.18 = (bf16[2,320,256]{2,1,0:T(8,128)(2,1)S(1)}, bf16[2,320,256]{2,1,0:T(8,128)(2,1)S(1)}, u32[]{:S(2)}, u32[]{:S(2)}) collective-permute-start(bf16[2,320,256]{2,1,0:T(8,128)(2,1)S(1)} %get-tuple-element.106), channel_id=1, source_target_pairs={{0,8},{2,10},{4,12},{6,14},{8,0},{10,2},{12,4},{14,6},{16,24},{18,... | collective-permute-start | bytes 983048 | tf_op jit(solution)/shard_map/terms_z1/ppermute | solution.py:34
  96.7 0.4 collective-permute-start.21
  97.1 0.1 pad_add_fusion.2.at_ref
  97.2 1.4 %weight_terms.10 = (bf16[2,320,128]{2,1,0:T(8,128)(2,1)S(1)}, bf16[2,320,128]{2,1,0:T(8,128)(2,1)S(1)}) custom-call(s32[4]{0:T(128)S(1)} %pad_add_fusion.2.at_ref, bf16[8,320,512]{2,1,0:T(8,128)(2,1)S(1)} %get-tuple-element.94.near_ref, bf16[8,320,512]{2,1,0:T(8,128)(2,1)S(1)} %copy-done.1, bf16[512,256]{1,0:T(8,128)(2,1)S(1)} %pad_maximum_fusion.3.own_ref.rest_1_, ...), custom_call_target="tpu_custom_call" | custom-call | flops 335544320 | bytes 3276800 | tf_op jit(solution)/shard_map/weight_terms/pallas_call | solution.py:316
  98.6 0.1 collective-permute-start.22
  98.6 1.1 collective-permute-done.19.rest_0_
  99.7 3.9 %collective-permute-done.21.rest_3_ = bf16[512,256]{1,0:T(8,128)(2,1)S(1)} collective-permute-done((bf16[512,256]{1,0:T(8,128)(2,1)S(1)}, bf16[512,256]{1,0:T(8,128)(2,1)S(1)}, u32[]{:S(2)}, u32[]{:S(2)}) %collective-permute-start.21) | collective-permute-done | bytes 262176 | tf_op jit(solution)/shard_map/own_y/ppermute | solution.py:34
  103.6 1.4 %weight_terms.11 = (bf16[2,320,128]{2,1,0:T(8,128)(2,1)S(1)}, bf16[2,320,128]{2,1,0:T(8,128)(2,1)S(1)}) custom-call(s32[4]{0:T(128)S(1)} %pad_add_fusion.1.at_ref, bf16[8,320,512]{2,1,0:T(8,128)(2,1)S(1)} %get-tuple-element.94.near_ref, bf16[8,320,512]{2,1,0:T(8,128)(2,1)S(1)} %copy-done.1, bf16[512,256]{1,0:T(8,128)(2,1)S(1)} %pad_maximum_fusion.3.own_ref.rest_1_, ...), custom_call_target="tpu_custom_call" | custom-call | flops 335544320 | bytes 3276800 | tf_op jit(solution)/shard_map/weight_terms/pallas_call | solution.py:316
  105.0 1.0 collective-permute-start.23
  106.0 2.6 %collective-permute-done.18 = bf16[2,320,256]{2,1,0:T(8,128)(2,1)S(1)} collective-permute-done((bf16[2,320,256]{2,1,0:T(8,128)(2,1)S(1)}, bf16[2,320,256]{2,1,0:T(8,128)(2,1)S(1)}, u32[]{:S(2)}, u32[]{:S(2)}) %collective-permute-start.18) | collective-permute-done | bytes 327712 | tf_op jit(solution)/shard_map/terms_z1/ppermute | solution.py:34
  108.7 0.1 collective-permute-start.25
  108.8 2.1 %collective-permute-start.26 = (bf16[320,128]{1,0:T(8,128)(2,1)S(1)}, bf16[320,128]{1,0:T(8,128)(2,1)S(1)}, u32[]{:S(2)}, u32[]{:S(2)}) collective-permute-start(bf16[320,128]{1,0:T(8,128)(2,1)S(1)} %fusion.1), channel_id=1, source_target_pairs={{0,4},{2,6},{4,0},{6,2},{8,12},{10,14},{12,8},{14,10},{16,20},{18,... | collective-permute-start | bytes 245768 | tf_op jit(solution)/shard_map/terms_x/ppermute | solution.py:34
  110.9 2.1 %collective-permute-done.23 = bf16[2,320,128]{2,1,0:T(8,128)(2,1)S(1)} collective-permute-done((bf16[2,320,128]{2,1,0:T(8,128)(2,1)S(1)}, bf16[2,320,128]{2,1,0:T(8,128)(2,1)S(1)}, u32[]{:S(2)}, u32[]{:S(2)}) %collective-permute-start.23) | collective-permute-done | bytes 163872 | tf_op jit(solution)/shard_map/terms_z1/ppermute | solution.py:34
  113.0 0.9 collective-permute-start.27
  113.9 6.3 %hidden_grads.1 = bf16[512,2560]{1,0:T(8,128)(2,1)} custom-call(s32[2]{0:T(128)S(1)} %copy-done.10, bf16[512,256]{1,0:T(8,128)(2,1)S(1)} %pad_maximum_fusion.2.own_ref.rest_0_, bf16[512,256]{1,0:T(8,128)(2,1)S(1)} %pad_maximum_fusion.3.own_ref.rest_1_, bf16[512,256]{1,0:T(8,128)(2,1)S(1)} %copy-done.9, bf16[512,256]{1,0:T(8,128)(2,1)S(1)} %collective-permute-done.21.rest_3_, ...), custom_call_target="tpu_custom_call" | custom-call | flops 2684354560 | bytes 7864320 | tf_op jit(solution)/shard_map/hidden_grads/pallas_call | solution.py:382
  120.2 0.1 bitcast_add_fusion
  120.3 0.1 bitcast_add_fusion.1
  120.4 0.7 pad_maximum_fusion.1
  121.1 0.8 pad_maximum_fusion
  (71 shorter events, 0.4 us)
Async XLA Ops:
  1.3 21.8 %copy-start.23 = (s32[2]{0:T(128)S(1)}, s32[2]{0:T(128)}, u32[]{:S(2)}) copy-start(s32[2]{0:T(128)} %param.16) | copy-start | bytes 28
  1.3 24.9 %copy-start.12 = (bf16[512,2048]{1,0:T(8,128)(2,1)S(1)}, bf16[512,2048]{1,0:T(8,128)(2,1)}, u32[]{:S(2)}) copy-start(bf16[512,2048]{1,0:T(8,128)(2,1)} %q_ref.3) | copy-start | bytes 6291460
  1.3 24.9 %copy-start.22 = (s32[2]{0:T(128)S(1)}, s32[2]{0:T(128)}, u32[]{:S(2)}) copy-start(s32[2]{0:T(128)} %len_ref.3) | copy-start | bytes 28
  9.5 39.7 %collective-permute-start.4 = (bf16[8,320,512]{2,1,0:T(8,128)(2,1)}, bf16[8,320,512]{2,1,0:T(8,128)(2,1)}, u32[]{:S(2)}, u32[]{:S(2)}) collective-permute-start(bf16[8,320,512]{2,1,0:T(8,128)(2,1)} %get-tuple-element.68), channel_id=1, source_target_pairs={{0,2},{2,0},{4,6},{6,4},{8,10},{10,8},{12,14},{14,12},{16,18},{18,... | collective-permute-start | bytes 7864328 | tf_op jit(solution)/shard_map/turned_core/ppermute | solution.py:34
  10.0 13.1 %collective-permute-start = (bf16[2,512,128]{2,1,0:T(8,128)(2,1)}, bf16[2,512,128]{2,1,0:T(8,128)(2,1)}, u32[]{:S(2)}, u32[]{:S(2)}) collective-permute-start(bf16[2,512,128]{2,1,0:T(8,128)(2,1)} %get-tuple-element.66.rest_0_), channel_id=1, source_target_pairs={{0,4},{2,6},{4,8},{6,10},{8,12},{10,14},{12,16},{14,18},{16,20},{1... | collective-permute-start | bytes 786440 | tf_op jit(solution)/shard_map/pair_two/ppermute | solution.py:34
  12.6 36.6 %collective-permute-start.5 = (bf16[2560,256]{1,0:T(8,128)(2,1)}, bf16[2560,256]{1,0:T(8,128)(2,1)S(1)}, u32[]{:S(2)}, u32[]{:S(2)}) collective-permute-start(bf16[2560,256]{1,0:T(8,128)(2,1)} %get-tuple-element.69), channel_id=1, source_target_pairs={{0,1},{1,0},{2,3},{3,2},{4,5},{5,4},{6,7},{7,6},{8,9},{9,8},{10,11... | collective-permute-start | bytes 3932168 | tf_op jit(solution)/shard_map/weights_y/ppermute | solution.py:34
  14.1 9.1 %collective-permute-start.6 = (bf16[2,512,128]{2,1,0:T(8,128)(2,1)}, bf16[2,512,128]{2,1,0:T(8,128)(2,1)}, u32[]{:S(2)}, u32[]{:S(2)}) collective-permute-start(bf16[2,512,128]{2,1,0:T(8,128)(2,1)} %get-tuple-element.66.rest_0_), channel_id=1, source_target_pairs={{0,2},{2,8},{4,6},{6,12},{8,10},{10,16},{12,14},{14,20},{16,18},{1... | collective-permute-start | bytes 786440 | tf_op jit(solution)/shard_map/pair_other/ppermute | solution.py:34
  23.1 3.1 %collective-permute-start.7 = (bf16[2,512,128]{2,1,0:T(8,128)(2,1)}, bf16[2,512,128]{2,1,0:T(8,128)(2,1)}, u32[]{:S(2)}, u32[]{:S(2)}) collective-permute-start(bf16[2,512,128]{2,1,0:T(8,128)(2,1)} %collective-permute-done.rest_2_), channel_id=1, source_target_pairs={{0,2},{2,0},{4,6},{6,4},{8,10},{10,8},{12,14},{14,12},{16,18},{18,... | collective-permute-start | bytes 786440 | tf_op jit(solution)/shard_map/pair_core/ppermute | solution.py:34
  23.1 27.1 %copy-start.11 = (bf16[8,320,512]{2,1,0:T(8,128)(2,1)S(1)}, bf16[8,320,512]{2,1,0:T(8,128)(2,1)}, u32[]{:S(2)}) copy-start(bf16[8,320,512]{2,1,0:T(8,128)(2,1)} %get-tuple-element.79.rest_6_) | copy-start | bytes 7864324
  23.1 27.1 %copy-start.13 = (bf16[512,2048]{1,0:T(8,128)(2,1)S(1)}, bf16[512,2048]{1,0:T(8,128)(2,1)}, u32[]{:S(2)}) copy-start(bf16[512,2048]{1,0:T(8,128)(2,1)} %q_ref.3) | copy-start | bytes 6291460
  23.2 21.2 %collective-permute-start.3 = (bf16[2,512,128]{2,1,0:T(8,128)(2,1)}, bf16[2,512,128]{2,1,0:T(8,128)(2,1)S(1)}, u32[]{:S(2)}, u32[]{:S(2)}) collective-permute-start(bf16[2,512,128]{2,1,0:T(8,128)(2,1)} %get-tuple-element.75.rest_0_), channel_id=1, source_target_pairs={{0,6},{2,4},{4,10},{6,8},{8,14},{10,12},{12,18},{14,16},{16,22},{1... | collective-permute-start | bytes 786440 | tf_op jit(solution)/shard_map/pair_cross/ppermute | solution.py:34
  23.2 24.7 %collective-permute-start.2 = (bf16[2,512,128]{2,1,0:T(8,128)(2,1)}, bf16[2,512,128]{2,1,0:T(8,128)(2,1)S(1)}, u32[]{:S(2)}, u32[]{:S(2)}) collective-permute-start(bf16[2,512,128]{2,1,0:T(8,128)(2,1)} %get-tuple-element.75.rest_0_), channel_id=1, source_target_pairs={{0,4},{2,6},{4,8},{6,10},{8,12},{10,14},{12,16},{14,18},{16,20},{1... | collective-permute-start | bytes 786440 | tf_op jit(solution)/shard_map/pair_two/ppermute | solution.py:34
  26.2 21.7 %collective-permute-start.1 = (bf16[2,512,128]{2,1,0:T(8,128)(2,1)}, bf16[2,512,128]{2,1,0:T(8,128)(2,1)S(1)}, u32[]{:S(2)}, u32[]{:S(2)}) collective-permute-start(bf16[2,512,128]{2,1,0:T(8,128)(2,1)} %get-tuple-element.75.rest_0_), channel_id=1, source_target_pairs={{0,2},{2,8},{4,6},{6,12},{8,10},{10,16},{12,14},{14,20},{16,18},{1... | collective-permute-start | bytes 786440 | tf_op jit(solution)/shard_map/pair_other/ppermute | solution.py:34
  26.3 1.6 %copy-start.14 = (bf16[512,2048]{1,0:T(8,128)(2,1)S(1)}, bf16[512,2048]{1,0:T(8,128)(2,1)}, u32[]{:S(2)}) copy-start(bf16[512,2048]{1,0:T(8,128)(2,1)} %do_ref.3) | copy-start | bytes 6291460
  27.9 0.9 copy-start.16
  28.8 0.9 copy-start.18
  29.8 0.9 copy-start.21
  30.7 19.6 %copy-start.15 = (bf16[512,2048]{1,0:T(8,128)(2,1)S(1)}, bf16[512,2048]{1,0:T(8,128)(2,1)}, u32[]{:S(2)}) copy-start(bf16[512,2048]{1,0:T(8,128)(2,1)} %do_ref.3) | copy-start | bytes 6291460
  30.7 19.6 %copy-start.17 = (bf16[512,256]{1,0:T(8,128)(2,1)S(1)}, bf16[512,256]{1,0:T(8,128)(2,1)}, u32[]{:S(2)}) copy-start(bf16[512,256]{1,0:T(8,128)(2,1)} %rest_4_.4) | copy-start | bytes 786436
  30.7 19.6 %copy-start.19 = (bf16[512,256]{1,0:T(8,128)(2,1)S(1)}, bf16[512,256]{1,0:T(8,128)(2,1)}, u32[]{:S(2)}) copy-start(bf16[512,256]{1,0:T(8,128)(2,1)} %rest_5_.4) | copy-start | bytes 786436
  30.7 19.6 %copy-start.20 = (bf16[2,512,128]{2,1,0:T(8,128)(2,1)S(1)}, bf16[2,512,128]{2,1,0:T(8,128)(2,1)}, u32[]{:S(2)}) copy-start(bf16[2,512,128]{2,1,0:T(8,128)(2,1)} %get-tuple-element.75.rest_0_) | copy-start | bytes 786436
  44.3 19.9 %collective-permute-start.8 = (bf16[2,512,128]{2,1,0:T(8,128)(2,1)S(1)}, bf16[2,512,128]{2,1,0:T(8,128)(2,1)S(1)}, u32[]{:S(2)}, u32[]{:S(2)}) collective-permute-start(bf16[2,512,128]{2,1,0:T(8,128)(2,1)S(1)} %get-tuple-element.91), channel_id=1, source_target_pairs={{0,26},{2,0},{4,30},{6,4},{8,2},{10,8},{12,6},{14,12},{16,10},{18,... | collective-permute-start | bytes 786440 | tf_op jit(solution)/shard_map/grad_other/ppermute | solution.py:34
  47.9 16.3 %collective-permute-start.9 = (bf16[2,512,128]{2,1,0:T(8,128)(2,1)S(1)}, bf16[2,512,128]{2,1,0:T(8,128)(2,1)S(1)}, u32[]{:S(2)}, u32[]{:S(2)}) collective-permute-start(bf16[2,512,128]{2,1,0:T(8,128)(2,1)S(1)} %get-tuple-element.92), channel_id=1, source_target_pairs={{0,28},{2,30},{4,0},{6,2},{8,4},{10,6},{12,8},{14,10},{16,12},{18,... | collective-permute-start | bytes 786440 | tf_op jit(solution)/shard_map/grad_two/ppermute | solution.py:34
  47.9 16.3 %collective-permute-start.10 = (bf16[2,512,128]{2,1,0:T(8,128)(2,1)S(1)}, bf16[2,512,128]{2,1,0:T(8,128)(2,1)S(1)}, u32[]{:S(2)}, u32[]{:S(2)}) collective-permute-start(bf16[2,512,128]{2,1,0:T(8,128)(2,1)S(1)} %get-tuple-element.93), channel_id=1, source_target_pairs={{0,30},{2,28},{4,2},{6,0},{8,6},{10,4},{12,10},{14,8},{16,14},{18,... | collective-permute-start | bytes 786440 | tf_op jit(solution)/shard_map/grad_cross/ppermute | solution.py:34
  49.2 1.1 copy-start.4
  63.2 5.0 %copy-start = (bf16[8,320,512]{2,1,0:T(8,128)(2,1)}, bf16[8,320,512]{2,1,0:T(8,128)(2,1)S(1)}, u32[]{:S(2)}) copy-start(bf16[8,320,512]{2,1,0:T(8,128)(2,1)S(1)} %get-tuple-element.95.far_ref) | copy-start | bytes 7864324
  63.3 2.1 %collective-permute-start.11 = (bf16[2,512,128]{2,1,0:T(8,128)(2,1)S(1)}, bf16[2,512,128]{2,1,0:T(8,128)(2,1)S(1)}, u32[]{:S(2)}, u32[]{:S(2)}) collective-permute-start(bf16[2,512,128]{2,1,0:T(8,128)(2,1)S(1)} %get-tuple-element.97), channel_id=1, source_target_pairs={{0,2},{2,0},{4,6},{6,4},{8,10},{10,8},{12,14},{14,12},{16,18},{18,... | collective-permute-start | bytes 786440 | tf_op jit(solution)/shard_map/grad_core/ppermute | solution.py:34
  64.5 1.6 %collective-permute-start.12 = (bf16[512,256]{1,0:T(8,128)(2,1)S(1)}, bf16[512,256]{1,0:T(8,128)(2,1)S(1)}, u32[]{:S(2)}, u32[]{:S(2)}) collective-permute-start(bf16[512,256]{1,0:T(8,128)(2,1)S(1)} %pad_maximum_fusion.2.own_ref.rest_0_), channel_id=1, source_target_pairs={{0,2},{2,0},{4,6},{6,4},{8,10},{10,8},{12,14},{14,12},{16,18},{18,... | collective-permute-start | bytes 786440 | tf_op jit(solution)/shard_map/own_core/ppermute | solution.py:34
  66.1 2.2 %copy-start.6 = (bf16[512,256]{1,0:T(8,128)(2,1)}, bf16[512,256]{1,0:T(8,128)(2,1)S(1)}, u32[]{:S(2)}) copy-start(bf16[512,256]{1,0:T(8,128)(2,1)S(1)} %collective-permute-done.12.pair_ref) | copy-start | bytes 786436
  68.3 8.3 %collective-permute-start.13 = (bf16[512,256]{1,0:T(8,128)(2,1)S(1)}, bf16[512,256]{1,0:T(8,128)(2,1)S(1)}, u32[]{:S(2)}, u32[]{:S(2)}) collective-permute-start(bf16[512,256]{1,0:T(8,128)(2,1)S(1)} %pad_maximum_fusion.2.own_ref.rest_0_), channel_id=1, source_target_pairs={{0,1},{1,0},{2,3},{3,2},{4,5},{5,4},{6,7},{7,6},{8,9},{9,8},{10,11... | collective-permute-start | bytes 786440 | tf_op jit(solution)/shard_map/own_y/ppermute | solution.py:34
  69.9 6.7 %collective-permute-start.14 = (bf16[2,512,128]{2,1,0:T(8,128)(2,1)S(1)}, bf16[2,512,128]{2,1,0:T(8,128)(2,1)S(1)}, u32[]{:S(2)}, u32[]{:S(2)}) collective-permute-start(bf16[2,512,128]{2,1,0:T(8,128)(2,1)S(1)} %get-tuple-element.102), channel_id=1, source_target_pairs={{0,26},{2,0},{4,30},{6,4},{8,2},{10,8},{12,6},{14,12},{16,10},{18,... | collective-permute-start | bytes 786440 | tf_op jit(solution)/shard_map/grad_other/ppermute | solution.py:34
  69.9 9.5 %collective-permute-start.15 = (bf16[2,512,128]{2,1,0:T(8,128)(2,1)S(1)}, bf16[2,512,128]{2,1,0:T(8,128)(2,1)S(1)}, u32[]{:S(2)}, u32[]{:S(2)}) collective-permute-start(bf16[2,512,128]{2,1,0:T(8,128)(2,1)S(1)} %add_convert_fusion.1), channel_id=1, source_target_pairs={{0,28},{2,30},{4,0},{6,2},{8,4},{10,6},{12,8},{14,10},{16,12},{18,... | collective-permute-start | bytes 786440 | tf_op jit(solution)/shard_map/grad_two/ppermute | solution.py:34
  71.4 21.8 %collective-permute-start.16 = (bf16[4,320,256]{2,1,0:T(8,128)(2,1)}, bf16[4,320,256]{2,1,0:T(8,128)(2,1)}, u32[]{:S(2)}, u32[]{:S(2)}) collective-permute-start(bf16[4,320,256]{2,1,0:T(8,128)(2,1)} %weight_terms.6), channel_id=1, source_target_pairs={{0,4},{2,6},{4,0},{6,2},{8,12},{10,14},{12,8},{14,10},{16,20},{18,... | collective-permute-start | bytes 1966088 | tf_op jit(solution)/shard_map/terms_x/ppermute | solution.py:34
  76.6 2.9 %copy-start.8 = (bf16[512,256]{1,0:T(8,128)(2,1)}, bf16[512,256]{1,0:T(8,128)(2,1)S(1)}, u32[]{:S(2)}) copy-start(bf16[512,256]{1,0:T(8,128)(2,1)S(1)} %collective-permute-done.13.rest_2_) | copy-start | bytes 786436
  79.6 1.6 %collective-permute-start.17 = (bf16[512,256]{1,0:T(8,128)(2,1)S(1)}, bf16[512,256]{1,0:T(8,128)(2,1)S(1)}, u32[]{:S(2)}, u32[]{:S(2)}) collective-permute-start(bf16[512,256]{1,0:T(8,128)(2,1)S(1)} %pad_maximum_fusion.3.own_ref.rest_1_), channel_id=1, source_target_pairs={{0,2},{2,0},{4,6},{6,4},{8,10},{10,8},{12,14},{14,12},{16,18},{18,... | collective-permute-start | bytes 786440 | tf_op jit(solution)/shard_map/own_core/ppermute | solution.py:34
  79.7 34.2 %collective-permute-start.24 = (bf16[2560,256]{1,0:T(8,128)(2,1)}, bf16[2560,256]{1,0:T(8,128)(2,1)}, u32[]{:S(2)}, u32[]{:S(2)}) collective-permute-start(bf16[2560,256]{1,0:T(8,128)(2,1)} %copy-done.4), channel_id=1, source_target_pairs={{0,2},{2,0},{4,6},{6,4},{8,10},{10,8},{12,14},{14,12},{16,18},{18,... | collective-permute-start | bytes 3932168 | tf_op jit(solution)/shard_map/weights_core/ppermute | solution.py:34
  81.2 1.7 %copy-start.1 = (bf16[8,320,512]{2,1,0:T(8,128)(2,1)S(1)}, bf16[8,320,512]{2,1,0:T(8,128)(2,1)}, u32[]{:S(2)}) copy-start(bf16[8,320,512]{2,1,0:T(8,128)(2,1)} %copy-done) | copy-start | bytes 7864324
  84.3 8.8 %copy-start.7 = (bf16[512,256]{1,0:T(8,128)(2,1)S(1)}, bf16[512,256]{1,0:T(8,128)(2,1)}, u32[]{:S(2)}) copy-start(bf16[512,256]{1,0:T(8,128)(2,1)} %copy-done.6) | copy-start | bytes 786436
  84.3 12.8 %collective-permute-start.20 = (bf16[4,320,128]{2,1,0:T(8,128)(2,1)S(1)}, bf16[4,320,128]{2,1,0:T(8,128)(2,1)S(1)}, u32[]{:S(2)}, u32[]{:S(2)}) collective-permute-start(bf16[4,320,128]{2,1,0:T(8,128)(2,1)S(1)} %weight_terms.7), channel_id=1, source_target_pairs={{0,8},{2,10},{4,12},{6,14},{8,0},{10,2},{12,4},{14,6},{16,24},{18,... | collective-permute-start | bytes 983048 | tf_op jit(solution)/shard_map/terms_z1/ppermute | solution.py:34
  87.0 12.7 %collective-permute-start.19 = (bf16[4,320,128]{2,1,0:T(8,128)(2,1)S(1)}, bf16[4,320,128]{2,1,0:T(8,128)(2,1)S(1)}, u32[]{:S(2)}, u32[]{:S(2)}) collective-permute-start(bf16[4,320,128]{2,1,0:T(8,128)(2,1)S(1)} %weight_terms.8), channel_id=1, source_target_pairs={{0,4},{2,6},{4,0},{6,2},{8,12},{10,14},{12,8},{14,10},{16,20},{18,... | collective-permute-start | bytes 983048 | tf_op jit(solution)/shard_map/terms_x/ppermute | solution.py:34
  95.1 13.5 %collective-permute-start.18 = (bf16[2,320,256]{2,1,0:T(8,128)(2,1)S(1)}, bf16[2,320,256]{2,1,0:T(8,128)(2,1)S(1)}, u32[]{:S(2)}, u32[]{:S(2)}) collective-permute-start(bf16[2,320,256]{2,1,0:T(8,128)(2,1)S(1)} %get-tuple-element.106), channel_id=1, source_target_pairs={{0,8},{2,10},{4,12},{6,14},{8,0},{10,2},{12,4},{14,6},{16,24},{18,... | collective-permute-start | bytes 983048 | tf_op jit(solution)/shard_map/terms_z1/ppermute | solution.py:34
  96.7 6.9 %collective-permute-start.21 = (bf16[512,256]{1,0:T(8,128)(2,1)S(1)}, bf16[512,256]{1,0:T(8,128)(2,1)S(1)}, u32[]{:S(2)}, u32[]{:S(2)}) collective-permute-start(bf16[512,256]{1,0:T(8,128)(2,1)S(1)} %pad_maximum_fusion.3.own_ref.rest_1_), channel_id=1, source_target_pairs={{0,1},{1,0},{2,3},{3,2},{4,5},{5,4},{6,7},{7,6},{8,9},{9,8},{10,11... | collective-permute-start | bytes 786440 | tf_op jit(solution)/shard_map/own_y/ppermute | solution.py:34
  98.6 10.2 %collective-permute-start.22 = (bf16[2,320,128]{2,1,0:T(8,128)(2,1)S(1)}, bf16[2,320,128]{2,1,0:T(8,128)(2,1)S(1)}, u32[]{:S(2)}, u32[]{:S(2)}) collective-permute-start(bf16[2,320,128]{2,1,0:T(8,128)(2,1)S(1)} %get-tuple-element.113), channel_id=1, source_target_pairs={{0,16},{2,18},{4,20},{6,22},{8,24},{10,26},{12,28},{14,30},{16,0},... | collective-permute-start | bytes 491528 | tf_op jit(solution)/shard_map/terms_z2/ppermute | solution.py:34
  103.6 10.3 %copy-start.2 = (bf16[5120,256]{1,0:T(8,128)(2,1)S(1)}, bf16[5120,256]{1,0:T(8,128)(2,1)}, u32[]{:S(2)}) copy-start(bf16[5120,256]{1,0:T(8,128)(2,1)} %rest_4_.5) | copy-start | bytes 7864324
  103.6 10.3 %copy-start.3 = (bf16[5120,256]{1,0:T(8,128)(2,1)S(1)}, bf16[5120,256]{1,0:T(8,128)(2,1)}, u32[]{:S(2)}) copy-start(bf16[5120,256]{1,0:T(8,128)(2,1)} %rest_5_.5) | copy-start | bytes 7864324
  103.6 10.3 %copy-start.5 = (bf16[2560,256]{1,0:T(8,128)(2,1)S(1)}, bf16[2560,256]{1,0:T(8,128)(2,1)}, u32[]{:S(2)}) copy-start(bf16[2560,256]{1,0:T(8,128)(2,1)} %copy-done.4) | copy-start | bytes 3932164
  103.6 10.3 %copy-start.9 = (bf16[512,256]{1,0:T(8,128)(2,1)S(1)}, bf16[512,256]{1,0:T(8,128)(2,1)}, u32[]{:S(2)}) copy-start(bf16[512,256]{1,0:T(8,128)(2,1)} %copy-done.8) | copy-start | bytes 786436
  103.6 10.3 %copy-start.10 = (s32[2]{0:T(128)S(1)}, s32[2]{0:T(128)}, u32[]{:S(2)}) copy-start(s32[2]{0:T(128)} %pad_add_fusion.at_ref) | copy-start | bytes 28
  105.0 7.9 %collective-permute-start.23 = (bf16[2,320,128]{2,1,0:T(8,128)(2,1)S(1)}, bf16[2,320,128]{2,1,0:T(8,128)(2,1)S(1)}, u32[]{:S(2)}, u32[]{:S(2)}) collective-permute-start(bf16[2,320,128]{2,1,0:T(8,128)(2,1)S(1)} %get-tuple-element.115), channel_id=1, source_target_pairs={{0,8},{2,10},{4,12},{6,14},{8,0},{10,2},{12,4},{14,6},{16,24},{18,... | collective-permute-start | bytes 491528 | tf_op jit(solution)/shard_map/terms_z1/ppermute | solution.py:34
  108.7 11.5 %collective-permute-start.25 = (bf16[320,256]{1,0:T(8,128)(2,1)S(1)}, bf16[320,256]{1,0:T(8,128)(2,1)S(1)}, u32[]{:S(2)}, u32[]{:S(2)}) collective-permute-start(bf16[320,256]{1,0:T(8,128)(2,1)S(1)} %fusion), channel_id=1, source_target_pairs={{0,16},{2,18},{4,20},{6,22},{8,24},{10,26},{12,28},{14,30},{16,0},... | collective-permute-start | bytes 491528 | tf_op jit(solution)/shard_map/terms_z2/ppermute | solution.py:34
  108.8 11.4 %collective-permute-start.26 = (bf16[320,128]{1,0:T(8,128)(2,1)S(1)}, bf16[320,128]{1,0:T(8,128)(2,1)S(1)}, u32[]{:S(2)}, u32[]{:S(2)}) collective-permute-start(bf16[320,128]{1,0:T(8,128)(2,1)S(1)} %fusion.1), channel_id=1, source_target_pairs={{0,4},{2,6},{4,0},{6,2},{8,12},{10,14},{12,8},{14,10},{16,20},{18,... | collective-permute-start | bytes 245768 | tf_op jit(solution)/shard_map/terms_x/ppermute | solution.py:34
  113.0 7.3 %collective-permute-start.27 = (bf16[320,128]{1,0:T(8,128)(2,1)S(1)}, bf16[320,128]{1,0:T(8,128)(2,1)S(1)}, u32[]{:S(2)}, u32[]{:S(2)}) collective-permute-start(bf16[320,128]{1,0:T(8,128)(2,1)S(1)} %fusion.2), channel_id=1, source_target_pairs={{0,16},{2,18},{4,20},{6,22},{8,24},{10,26},{12,28},{14,30},{16,0},... | collective-permute-start | bytes 245768 | tf_op jit(solution)/shard_map/terms_z2/ppermute | solution.py:34

commit v4 on v3

--- a/solution.py
+++ b/solution.py
@@ -129,12 +129,12 @@
 
 def attend_kernel(heads, loads, sel_ref, len_ref, q_ref, do_ref, *rest):
     if loads:
-        sources, landed = rest[REACH + 2 : REACH + 2 + loads], rest[-10 - loads : -10]
+        sources, landed = rest[REACH + 2 : REACH + 2 + loads], rest[-11]
         load_sems = rest[-1]
-        rest = rest[: REACH + 2] + rest[REACH + 2 + loads : -10 - loads] + rest[-10:-1]
+        rest = rest[: REACH + 2] + rest[REACH + 2 + loads : -11] + rest[-10:-1]
         moves = [
-            pltpu.make_async_copy(src, dst, load_sems.at[i])
-            for i, (src, dst) in enumerate(zip(sources, landed))
+            pltpu.make_async_copy(src, landed.at[i], load_sems.at[i])
+            for i, src in enumerate(sources)
         ]
 
         @pl.when(pl.program_id(0) == 0)
@@ -263,14 +263,14 @@
         out_shape=[jax.ShapeDtypeStruct(q.shape, BF)] * 2
         + [jax.ShapeDtypeStruct(rk.shape, BF)] * 2
         + [jax.ShapeDtypeStruct((2, plen, HD), BF)] * REACH
-        + [jax.ShapeDtypeStruct(x.shape, x.dtype) for x in loads],
+        + [jax.ShapeDtypeStruct((len(loads), *x.shape), BF) for x in loads[:1]],
         grid_spec=pltpu.PrefetchScalarGridSpec(
             num_scalar_prefetch=2,
             grid=(slots,),
             in_specs=in_specs,
             out_specs=[wide, wide, narrow, narrow]
             + [pl.BlockSpec((2, plen, HD), lambda r, *_: (0, 0, 0))] * REACH
-            + [RESIDENT] * len(loads),
+            + [RESIDENT] * bool(loads),
             scratch_shapes=[
                 pltpu.VMEM((slots, 2, plen, HD), BF),
                 pltpu.SemaphoreType.DMA((slots,)),
@@ -282,7 +282,7 @@
             + [pltpu.SemaphoreType.DMA((len(loads),))] * bool(loads),
         ),
         input_output_aliases=aliases,
-        compiler_params=pltpu.CompilerParams(vmem_limit_bytes=ATTEND),
+        compiler_params=pltpu.CompilerParams(vmem_limit_bytes=(WHOLE - 6 * MIB) if loads else WHOLE),
         cost_estimate=pl.CostEstimate(
             flops=slots * heads * 24 * rlen * klen * HD,
             bytes_accessed=8 * MIB,
@@ -292,7 +292,7 @@
     )(sel, lengths, *ins)
 
 
-def weight_kernel(first, at_ref, near_ref, far_ref, own_ref, pair_ref, *rest):
+def weight_kernel(first, at_ref, both_ref, own_ref, pair_ref, *rest):
     count = at_ref.shape[0]
     arrived, outs = (rest[0], rest[1:]) if rest[0].shape[0] == count and len(rest) > 1 else (None, rest)
     width = outs[0].shape[2]
@@ -301,18 +301,18 @@
     each = outs[0].shape[0]
     for i in range(count):
         chunk = at_ref[i]
-        total = mm(near_ref[chunk], own) + mm(far_ref[chunk], pair)
+        total = mm(both_ref[0, chunk], own) + mm(both_ref[1, chunk], pair)
         if arrived is not None:
             total += arrived[i].astype(F32)
         outs[i // each][i % each] = total.astype(BF)
 
 
-def weight_terms(at, near, far, grads, columns, arrived=None, parts=1):
+def weight_terms(at, both, grads, columns, arrived=None, parts=1):
     own, pair = grads
-    chunk, rows = near.shape[1:]
+    chunk, rows = both.shape[2:]
     count = at.shape[0]
     first, width = columns
-    ins = [near, far, own, pair] + ([] if arrived is None else [arrived])
+    ins = [both, own, pair] + ([] if arrived is None else [arrived])
     return pl.pallas_call(
         functools.partial(weight_kernel, first),
         out_shape=[jax.ShapeDtypeStruct((count // parts, chunk, width), BF)] * parts,
@@ -443,7 +443,8 @@
     *pairs, near, turned, mine = project(at, prompt_hidden, w_key, w_value, size)
     two = permute(pairs[0], "dp", lambda i: (i + 2) % size, "pair_two")
     one = permute(pairs[0], "dp", other, "pair_other")
-    received = [[pairs[0], one, two, permute(two, "dp", lambda i: i ^ 1, "pair_core")]]
+    core_two = permute(after(two, sel), "dp", lambda i: i ^ 1, "pair_core")
+    received = [[pairs[0], one, two, core_two]]
     far_a = permute(mine, "mp", lambda i: 1 - i, "weights_y")
     far = permute(turned, "dp", lambda i: i ^ 1, "turned_core")
     later = after(pairs[1], two)
@@ -465,7 +466,7 @@
         permute(core_0, "dp", cross, "grad_cross"),
     ]
     received[1], far, far_a, prev = after((received[1], far, far_a, prev), mine_0)
-    *prev, mine_1, other_1, two_1, core_1, near, far = attend(
+    *prev, mine_1, other_1, two_1, core_1, both = attend(
         1,
         sel,
         resp_length,
@@ -487,7 +488,7 @@
     shares_1.append(permute(two, "dp", lambda i: (i - 2) % size, "grad_two"))
 
     bit, place = (index // 2) % 2, index // 4
-    count = near.shape[0]
+    count = both.shape[1]
 
     def places(shifts, flips):
         return jnp.stack([2 * (place ^ i) + (bit ^ x) for i in shifts for x in flips])
@@ -511,9 +512,9 @@
         weight_grads = []
         for grad in owns:
             grads = (grad, permute(grad, "dp", lambda i: i ^ 1, "own_core"))
-            (sent,) = weight_terms(places(every, [1]), near, far, grads, whole)
+            (sent,) = weight_terms(places(every, [1]), both, grads, whole)
             got = along(sent, 2, "terms_x")
-            (held,) = weight_terms(places(every, [0]), near, far, grads, whole, got)
+            (held,) = weight_terms(places(every, [0]), both, grads, whole, got)
             weight_grads.append(far_sum(held[0], list(held[1:]), 4))
         away = [permute(grad, "mp", lambda i: 1 - i, "own_y") for grad in owns]
         hidden_grad = hidden_grads(at, owns, away, w_key, w_value, far_a, far_b)
@@ -530,36 +531,36 @@
     near_first, near_then = [0, 2], [1, 3]
     every = near_first + near_then
     grads_0 = (after(own[0], two), pair[0])
-    (sent_0,) = weight_terms(places(every, [1]), near, far, grads_0, whole)
+    (sent_0,) = weight_terms(places(every, [1]), both, grads_0, whole)
     got_0 = along(sent_0, 2, "terms_x")
     away = [permute(after(own[0], sent_0), "mp", lambda i: 1 - i, "own_y")]
-    own.append(total_grad(after(mine_1, sent_0, away[0]), shares_1))
+    own.append(total_grad(after(mine_1, sent_0), shares_1))
     pair.append(permute(own[1], "dp", lambda i: i ^ 1, "own_core"))
     grads_1 = (own[1], pair[1])
-    (sent_v,) = weight_terms(places([1, 3], [0, 1]), near, far, grads_1, value)
+    (sent_v,) = weight_terms(places([1, 3], [0, 1]), both, grads_1, value)
     got_v = along(sent_v, 4, "terms_z1")
-    (sent_k,) = weight_terms(places(every, [1]), near, far, (after(own[1], sent_v), pair[1]), key)
+    (sent_k,) = weight_terms(places(every, [1]), both, (after(own[1], sent_v), pair[1]), key)
     got_k = along(sent_k, 2, "terms_x")
 
     held_0, sent_0 = weight_terms(
-        places(every, [0]), near, far, grads_0, whole,
-        after(got_0, sent_k), 2,
+        places(every, [0]), both, grads_0, whole,
+        after(got_0, sent_k, away[0]), 2,
     )
     got_0 = along(sent_0, 4, "terms_z1")
     away.append(permute(after(own[1], held_0), "mp", lambda i: 1 - i, "own_y"))
     held_v, sent_v = weight_terms(
-        places(near_first, [0, 1]), near, far, grads_1, value, after(got_v, held_0), 2
+        places(near_first, [0, 1]), both, grads_1, value, after(got_v, held_0), 2
     )
     got_v = along(sent_v, 8, "terms_z2")
     held_k, sent_k = weight_terms(
-        places(every, [0]), near, far, grads_1, key, after(got_k, held_v, away[1]), 2
+        places(every, [0]), both, grads_1, key, after(got_k, held_v, away[1]), 2
     )
     got_k = along(sent_k, 4, "terms_z1")
-    two_0 = add(held_0[1], after(got_0, held_k)[1]).astype(BF)
+    two_v = add(held_v[1], after(got_v, held_k)[1]).astype(BF)
+    last_v = along(two_v, 2, "terms_x")
+    two_0 = add(held_0[1], after(got_0, two_v)[1]).astype(BF)
     last_0 = along(two_0, 8, "terms_z2")
-    two_v = add(held_v[1], after(got_v, two_0)[1]).astype(BF)
-    last_v = along(two_v, 2, "terms_x")
-    two_k = add(held_k[1], after(got_k, two_v)[1]).astype(BF)
+    two_k = add(held_k[1], after(got_k, two_0)[1]).astype(BF)
     last_k = along(two_k, 8, "terms_z2")
     hidden_grad = hidden_grads(
         at, after(own, two_0, two_v, two_k), away, w_key, w_value, far_a, far_b

time: 122 us -> 123 us (level)
  waiting for transfers between devices: 32.3 us -> 19.4 us
  starting transfers between devices: 27.3 us -> 35.7 us
  Pallas kernels: 50.7 us -> 55.9 us
    ppermute x28, waiting for transfers between devices: 32.3 us -> 19.4 us  [permute(): lax.ppermute(block, axis, [(i, target(i)) for i in range(lax.axis_size(ax...]
    ppermute x28, starting transfers between devices: 27.3 us -> 35.7 us  [permute(): lax.ppermute(block, axis, [(i, target(i)) for i in range(lax.axis_size(ax...]
    pallas_call x2, Pallas kernels: 26.5 us -> 30.5 us  [attend(): pl.pallas_call(functools.partial(attend_kernel, heads, len(loads)), out_s...]
    unnamed x48 -> x34, local copies, waits for them, and re-layouts: 7.33 us -> 8.29 us
  transfers between devices with their start and end apart: 28 -> 28, of which waited for: 11 -> 9; matrix products, arithmetic and copies ran while one was open for 1% -> 1% of each run, Pallas kernels for 33% -> 39%
where the time goes in v4:
time: 123 us; the launch traced here: 124 us
  Pallas kernels  55.9 us (45%)
  starting transfers between devices  35.7 us (29%)
  waiting for transfers between devices  19.4 us (16%)
  local copies, waits for them, and re-layouts  8.35 us (7%)
  other arithmetic  3.52 us (3%)
    ppermute x28, starting transfers between devices, permute(): lax.ppermute(block, axis, [(i, target(i)) for i in range(lax.axis_size(ax...  35.7 us
    pallas_call x2, Pallas kernels, attend(): pl.pallas_call(functools.partial(attend_kernel, heads, len(loads)), out_s...  30.5 us
    ppermute x28, waiting for transfers between devices, permute(): lax.ppermute(block, axis, [(i, target(i)) for i in range(lax.axis_size(ax...  19.4 us
    pallas_call x6, Pallas kernels, weight_terms(): pl.pallas_call(functools.partial(weight_kernel, first), out_shape=[jax.Sh...  10.9 us
    unnamed x34, local copies, waits for them, and re-layouts  8.29 us
    pallas_call x1, Pallas kernels, project(): pl.pallas_call(functools.partial(project_kernel, groups), out_shape=[jax....  8.21 us
    pallas_call x1, Pallas kernels, hidden_grads(): pl.pallas_call(functools.partial(hidden_kernel, groups), out_shape=jax.Sh...  6.29 us
  transfers between devices with their start and end apart: 28, of which 9 were waited for; matrix products, arithmetic and copies ran while one was open for 1% of the time, Pallas kernels for 39%

profile of v4, /device:TPU:0, one launch (start us, length us, event | category | flops | bytes accessed | tf_op | source)
XLA Modules:
  0.0 123.8 jit_solution(5099975428862607275)
XLA Ops:
  0.6 0.6 pad_add_fusion.at_ref
  1.2 8.2 %project.1 = (bf16[2,512,128]{2,1,0:T(8,128)(2,1)}, bf16[2,512,128]{2,1,0:T(8,128)(2,1)}, bf16[8,320,512]{2,1,0:T(8,128)(2,1)}, bf16[8,320,512]{2,1,0:T(8,128)(2,1)}, bf16[2560,256]{1,0:T(8,128)(2,1)}) custom-call(s32[2]{0:T(128)} %pad_add_fusion.at_ref, bf16[512,5120]{1,0:T(8,128)(2,1)} %h_ref.1, bf16[5120,256]{1,0:T(8,128)(2,1)} %rest_4_.5, ...), custom_call_target="tpu_custom_call" | custom-call | flops 2684354560 | bytes 15728640 | tf_op jit(solution)/shard_map/project/pallas_call | solution.py:105
  9.5 0.5 collective-permute-start.4
  10.0 2.6 %collective-permute-start = (bf16[2,512,128]{2,1,0:T(8,128)(2,1)}, bf16[2,512,128]{2,1,0:T(8,128)(2,1)S(1)}, u32[]{:S(2)}, u32[]{:S(2)}) collective-permute-start(bf16[2,512,128]{2,1,0:T(8,128)(2,1)} %get-tuple-element.66.rest_0_), channel_id=1, source_target_pairs={{0,4},{2,6},{4,8},{6,10},{8,12},{10,14},{12,16},{14,18},{16,20},{1... | collective-permute-start | bytes 786440 | tf_op jit(solution)/shard_map/pair_two/ppermute | solution.py:34
  12.5 0.2 collective-permute-start.6
  12.7 1.5 %collective-permute-start.5 = (bf16[2560,256]{1,0:T(8,128)(2,1)}, bf16[2560,256]{1,0:T(8,128)(2,1)S(1)}, u32[]{:S(2)}, u32[]{:S(2)}) collective-permute-start(bf16[2560,256]{1,0:T(8,128)(2,1)} %get-tuple-element.69), channel_id=1, source_target_pairs={{0,1},{1,0},{2,3},{3,2},{4,5},{5,4},{6,7},{7,6},{8,9},{9,8},{10,11... | collective-permute-start | bytes 3932168 | tf_op jit(solution)/shard_map/weights_y/ppermute | solution.py:34
  14.2 0.5 and_select_fusion.sel_ref
  14.7 8.2 %collective-permute-done.rest_2_ = bf16[2,512,128]{2,1,0:T(8,128)(2,1)S(1)} collective-permute-done((bf16[2,512,128]{2,1,0:T(8,128)(2,1)}, bf16[2,512,128]{2,1,0:T(8,128)(2,1)S(1)}, u32[]{:S(2)}, u32[]{:S(2)}) %collective-permute-start) | collective-permute-done | bytes 262176 | tf_op jit(solution)/shard_map/pair_two/ppermute | solution.py:34
  22.9 0.0 collective-permute-start.7
  23.0 0.1 collective-permute-start.3
  23.0 3.0 %collective-permute-start.2 = (bf16[2,512,128]{2,1,0:T(8,128)(2,1)}, bf16[2,512,128]{2,1,0:T(8,128)(2,1)S(1)}, u32[]{:S(2)}, u32[]{:S(2)}) collective-permute-start(bf16[2,512,128]{2,1,0:T(8,128)(2,1)} %get-tuple-element.76.rest_0_), channel_id=1, source_target_pairs={{0,4},{2,6},{4,8},{6,10},{8,12},{10,14},{12,16},{14,18},{16,20},{1... | collective-permute-start | bytes 786440 | tf_op jit(solution)/shard_map/pair_two/ppermute | solution.py:34
  26.1 0.0 collective-permute-start.1
  26.1 0.7 copy-done.15
  26.8 15.1 %attend_0.1 = (bf16[512,2048]{1,0:T(8,128)(2,1)}, bf16[512,2048]{1,0:T(8,128)(2,1)}, bf16[512,256]{1,0:T(8,128)(2,1)}, bf16[512,256]{1,0:T(8,128)(2,1)}, bf16[2,...) custom-call(s32[2]{0:T(128)} %and_select_fusion.sel_ref, ...), custom_call_target="tpu_custom_call" | custom-call | flops 9663676416 | bytes 8388608 | tf_op jit(solution)/shard_map/attend_0/pallas_call | solution.py:261
  41.9 0.0 copy-start.12
  41.9 2.9 %collective-permute-start.8 = (bf16[2,512,128]{2,1,0:T(8,128)(2,1)}, bf16[2,512,128]{2,1,0:T(8,128)(2,1)S(1)}, u32[]{:S(2)}, u32[]{:S(2)}) collective-permute-start(bf16[2,512,128]{2,1,0:T(8,128)(2,1)} %get-tuple-element.92), channel_id=1, source_target_pairs={{0,26},{2,0},{4,30},{6,4},{8,2},{10,8},{12,6},{14,12},{16,10},{18,... | collective-permute-start | bytes 786440 | tf_op jit(solution)/shard_map/grad_other/ppermute | solution.py:34
  44.9 1.3 %collective-permute-start.10 = (bf16[2,512,128]{2,1,0:T(8,128)(2,1)}, bf16[2,512,128]{2,1,0:T(8,128)(2,1)S(1)}, u32[]{:S(2)}, u32[]{:S(2)}) collective-permute-start(bf16[2,512,128]{2,1,0:T(8,128)(2,1)} %get-tuple-element.94), channel_id=1, source_target_pairs={{0,30},{2,28},{4,2},{6,0},{8,6},{10,4},{12,10},{14,8},{16,14},{18,... | collective-permute-start | bytes 786440 | tf_op jit(solution)/shard_map/grad_cross/ppermute | solution.py:34
  46.2 15.4 %attend_1.1 = (bf16[512,2048]{1,0:T(8,128)(2,1)}, bf16[512,2048]{1,0:T(8,128)(2,1)}, bf16[512,256]{1,0:T(8,128)(2,1)}, bf16[512,256]{1,0:T(8,128)(2,1)}, bf16[2,...) custom-call(s32[2]{0:T(128)S(1)} %copy-done.10, ...), custom_call_target="tpu_custom_call", output_to_operand_aliasing={{0}: (12, {}), {1}: (13, {}), {2}: (14, {}), {3}: (15, {})} | custom-call | flops 9663676416 | bytes 8388608 | tf_op jit(solution)/shard_map/attend_1/pallas_call | solution.py:261
  61.6 0.9 collective-permute-start.11
  62.5 0.6 collective-permute-start.13
  63.1 0.1 add_convert_fusion.2
  63.3 0.1 collective-permute-start.12
  63.4 0.3 collective-permute-done.11
  63.6 0.1 add_convert_fusion.1
  63.7 3.6 %collective-permute-start.14 = (bf16[2,512,128]{2,1,0:T(8,128)(2,1)S(1)}, bf16[2,512,128]{2,1,0:T(8,128)(2,1)S(1)}, u32[]{:S(2)}, u32[]{:S(2)}) collective-permute-start(bf16[2,512,128]{2,1,0:T(8,128)(2,1)S(1)} %add_convert_fusion.1), channel_id=1, source_target_pairs={{0,28},{2,30},{4,0},{6,2},{8,4},{10,6},{12,8},{14,10},{16,12},{18,... | collective-permute-start | bytes 786440 | tf_op jit(solution)/shard_map/grad_two/ppermute | solution.py:34
  67.3 0.1 add_add_fusion.at_ref
  67.4 2.6 %copy-done = bf16[2,8,320,512]{3,2,1,0:T(8,128)(2,1)S(1)} copy-done((bf16[2,8,320,512]{3,2,1,0:T(8,128)(2,1)S(1)}, bf16[2,8,320,512]{3,2,1,0:T(8,128)(2,1)}, u32[]{:S(2)}) %copy-start) | copy-done | bytes 5242904
  70.0 2.2 %weight_terms.6 = bf16[4,320,256]{2,1,0:T(8,128)(2,1)} custom-call(s32[4]{0:T(128)S(1)} %add_add_fusion.at_ref, bf16[2,8,320,512]{3,2,1,0:T(8,128)(2,1)S(1)} %copy-done, bf16[512,256]{1,0:T(8,128)(2,1)S(1)} %pad_maximum_fusion.2.own_ref.rest_0_, bf16[512,256]{1,0:T(8,128)(2,1)S(1)} %collective-permute-done.12.pair_ref), custom_call_target="tpu_custom_call" | custom-call | flops 671088640 | bytes 3932160 | tf_op jit(solution)/shard_map/weight_terms/pallas_call | solution.py:316
  72.2 0.5 collective-permute-start.15
  72.7 1.0 collective-permute-done.14
  73.7 0.1 add_convert_fusion
  73.8 0.1 collective-permute-start.16
  73.9 0.5 collective-permute-start.24
  74.4 1.5 %collective-permute-start.17 = (bf16[512,256]{1,0:T(8,128)(2,1)S(1)}, bf16[512,256]{1,0:T(8,128)(2,1)}, u32[]{:S(2)}, u32[]{:S(2)}) collective-permute-start(bf16[512,256]{1,0:T(8,128)(2,1)S(1)} %pad_maximum_fusion.2.own_ref.rest_0_), channel_id=1, source_target_pairs={{0,1},{1,0},{2,3},{3,2},{4,5},{5,4},{6,7},{7,6},{8,9},{9,8},{10,11... | collective-permute-start | bytes 786440 | tf_op jit(solution)/shard_map/own_y/ppermute | solution.py:34
  75.9 0.1 add_add_fusion.1.at_ref
  76.0 2.5 %copy-done.1 = bf16[2,8,320,512]{3,2,1,0:T(8,128)(2,1)S(1)} copy-done((bf16[2,8,320,512]{3,2,1,0:T(8,128)(2,1)S(1)}, bf16[2,8,320,512]{3,2,1,0:T(8,128)(2,1)}, u32[]{:S(2)}) %copy-start.1) | copy-done | bytes 5242904
  78.5 2.1 %weight_terms.7 = bf16[4,320,128]{2,1,0:T(8,128)(2,1)} custom-call(s32[4]{0:T(128)S(1)} %add_add_fusion.1.at_ref, bf16[2,8,320,512]{3,2,1,0:T(8,128)(2,1)S(1)} %copy-done.1, bf16[512,256]{1,0:T(8,128)(2,1)S(1)} %pad_maximum_fusion.3.own_ref.rest_1_, bf16[512,256]{1,0:T(8,128)(2,1)S(1)} %collective-permute-done.16.pair_ref), custom_call_target="tpu_custom_call" | custom-call | flops 335544320 | bytes 3276800 | tf_op jit(solution)/shard_map/weight_terms/pallas_call | solution.py:316
  80.6 3.0 %collective-permute-start.19 = (bf16[4,320,128]{2,1,0:T(8,128)(2,1)}, bf16[4,320,128]{2,1,0:T(8,128)(2,1)}, u32[]{:S(2)}, u32[]{:S(2)}) collective-permute-start(bf16[4,320,128]{2,1,0:T(8,128)(2,1)} %weight_terms.7), channel_id=1, source_target_pairs={{0,8},{2,10},{4,12},{6,14},{8,0},{10,2},{12,4},{14,6},{16,24},{18,... | collective-permute-start | bytes 983048 | tf_op jit(solution)/shard_map/terms_z1/ppermute | solution.py:34
  83.7 0.1 pad_add_fusion.1.at_ref
  83.7 2.5 %copy-done.2 = bf16[2,8,320,512]{3,2,1,0:T(8,128)(2,1)S(1)} copy-done((bf16[2,8,320,512]{3,2,1,0:T(8,128)(2,1)S(1)}, bf16[2,8,320,512]{3,2,1,0:T(8,128)(2,1)}, u32[]{:S(2)}) %copy-start.2) | copy-done | bytes 5242904
  86.2 1.4 %weight_terms.8 = bf16[4,320,128]{2,1,0:T(8,128)(2,1)S(1)} custom-call(s32[4]{0:T(128)S(1)} %add_add_fusion.at_ref, bf16[2,8,320,512]{3,2,1,0:T(8,128)(2,1)S(1)} %copy-done.2, bf16[512,256]{1,0:T(8,128)(2,1)S(1)} %pad_maximum_fusion.3.own_ref.rest_1_, bf16[512,256]{1,0:T(8,128)(2,1)S(1)} %collective-permute-done.16.pair_ref), custom_call_target="tpu_custom_call" | custom-call | flops 335544320 | bytes 3276800 | tf_op jit(solution)/shard_map/weight_terms/pallas_call | solution.py:316
  87.6 3.1 %collective-permute-start.21 = (bf16[4,320,128]{2,1,0:T(8,128)(2,1)S(1)}, bf16[4,320,128]{2,1,0:T(8,128)(2,1)S(1)}, u32[]{:S(2)}, u32[]{:S(2)}) collective-permute-start(bf16[4,320,128]{2,1,0:T(8,128)(2,1)S(1)} %weight_terms.8), channel_id=1, source_target_pairs={{0,4},{2,6},{4,0},{6,2},{8,12},{10,14},{12,8},{14,10},{16,20},{18,... | collective-permute-start | bytes 983048 | tf_op jit(solution)/shard_map/terms_x/ppermute | solution.py:34
  90.7 1.9 %weight_terms.9 = (bf16[2,320,256]{2,1,0:T(8,128)(2,1)S(1)}, bf16[2,320,256]{2,1,0:T(8,128)(2,1)S(1)}) custom-call(s32[4]{0:T(128)S(1)} %pad_add_fusion.1.at_ref, bf16[2,8,320,512]{3,2,1,0:T(8,128)(2,1)S(1)} %copy-done.2, bf16[512,256]{1,0:T(8,128)(2,1)S(1)} %pad_maximum_fusion.2.own_ref.rest_0_, bf16[512,256]{1,0:T(8,128)(2,1)S(1)} %copy-done.6, ...), custom_call_target="tpu_custom_call" | custom-call | flops 671088640 | bytes 3932160 | tf_op jit(solution)/shard_map/weight_terms/pallas_call | solution.py:316
  92.7 1.0 collective-permute-start.22
  93.7 0.1 pad_add_fusion.2.at_ref
  93.8 1.8 %weight_terms.10 = (bf16[2,320,128]{2,1,0:T(8,128)(2,1)S(1)}, bf16[2,320,128]{2,1,0:T(8,128)(2,1)S(1)}) custom-call(s32[4]{0:T(128)S(1)} %pad_add_fusion.2.at_ref, bf16[2,8,320,512]{3,2,1,0:T(8,128)(2,1)S(1)} %copy-done.2, bf16[512,256]{1,0:T(8,128)(2,1)S(1)} %pad_maximum_fusion.3.own_ref.rest_1_, bf16[512,256]{1,0:T(8,128)(2,1)S(1)} %collective-permute-done.16.pair_ref, ...), custom_call_target="tpu_custom_call" | custom-call | flops 335544320 | bytes 3276800 | tf_op jit(solution)/shard_map/weight_terms/pallas_call | solution.py:316
  95.6 1.7 %collective-permute-start.20 = (bf16[2,320,128]{2,1,0:T(8,128)(2,1)S(1)}, bf16[2,320,128]{2,1,0:T(8,128)(2,1)S(1)}, u32[]{:S(2)}, u32[]{:S(2)}) collective-permute-start(bf16[2,320,128]{2,1,0:T(8,128)(2,1)S(1)} %get-tuple-element.109), channel_id=1, source_target_pairs={{0,16},{2,18},{4,20},{6,22},{8,24},{10,26},{12,28},{14,30},{16,0},... | collective-permute-start | bytes 491528 | tf_op jit(solution)/shard_map/terms_z2/ppermute | solution.py:34
  97.3 0.1 collective-permute-start.18
  97.4 0.7 collective-permute-done.21.rest_0_
  98.1 2.1 %collective-permute-done.22.rest_3_ = bf16[512,256]{1,0:T(8,128)(2,1)S(1)} collective-permute-done((bf16[512,256]{1,0:T(8,128)(2,1)S(1)}, bf16[512,256]{1,0:T(8,128)(2,1)S(1)}, u32[]{:S(2)}, u32[]{:S(2)}) %collective-permute-start.22) | collective-permute-done | bytes 262176 | tf_op jit(solution)/shard_map/own_y/ppermute | solution.py:34
  100.2 1.4 %weight_terms.11 = (bf16[2,320,128]{2,1,0:T(8,128)(2,1)S(1)}, bf16[2,320,128]{2,1,0:T(8,128)(2,1)S(1)}) custom-call(s32[4]{0:T(128)S(1)} %pad_add_fusion.1.at_ref, bf16[2,8,320,512]{3,2,1,0:T(8,128)(2,1)S(1)} %copy-done.2, bf16[512,256]{1,0:T(8,128)(2,1)S(1)} %pad_maximum_fusion.3.own_ref.rest_1_, bf16[512,256]{1,0:T(8,128)(2,1)S(1)} %collective-permute-done.16.pair_ref, ...), custom_call_target="tpu_custom_call" | custom-call | flops 335544320 | bytes 3276800 | tf_op jit(solution)/shard_map/weight_terms/pallas_call | solution.py:316
  101.6 1.4 %collective-permute-start.23 = (bf16[2,320,128]{2,1,0:T(8,128)(2,1)S(1)}, bf16[2,320,128]{2,1,0:T(8,128)(2,1)S(1)}, u32[]{:S(2)}, u32[]{:S(2)}) collective-permute-start(bf16[2,320,128]{2,1,0:T(8,128)(2,1)S(1)} %get-tuple-element.115), channel_id=1, source_target_pairs={{0,8},{2,10},{4,12},{6,14},{8,0},{10,2},{12,4},{14,6},{16,24},{18,... | collective-permute-start | bytes 491528 | tf_op jit(solution)/shard_map/terms_z1/ppermute | solution.py:34
  103.0 2.6 %collective-permute-done.20 = bf16[2,320,128]{2,1,0:T(8,128)(2,1)S(1)} collective-permute-done((bf16[2,320,128]{2,1,0:T(8,128)(2,1)S(1)}, bf16[2,320,128]{2,1,0:T(8,128)(2,1)S(1)}, u32[]{:S(2)}, u32[]{:S(2)}) %collective-permute-start.20) | collective-permute-done | bytes 163872 | tf_op jit(solution)/shard_map/terms_z2/ppermute | solution.py:34
  105.7 2.5 %collective-permute-start.26 = (bf16[320,128]{1,0:T(8,128)(2,1)S(1)}, bf16[320,128]{1,0:T(8,128)(2,1)S(1)}, u32[]{:S(2)}, u32[]{:S(2)}) collective-permute-start(bf16[320,128]{1,0:T(8,128)(2,1)S(1)} %fusion.1), channel_id=1, source_target_pairs={{0,4},{2,6},{4,0},{6,2},{8,12},{10,14},{12,8},{14,10},{16,20},{18,... | collective-permute-start | bytes 245768 | tf_op jit(solution)/shard_map/terms_x/ppermute | solution.py:34
  108.1 2.2 %collective-permute-done.18 = bf16[2,320,256]{2,1,0:T(8,128)(2,1)S(1)} collective-permute-done((bf16[2,320,256]{2,1,0:T(8,128)(2,1)S(1)}, bf16[2,320,256]{2,1,0:T(8,128)(2,1)S(1)}, u32[]{:S(2)}, u32[]{:S(2)}) %collective-permute-start.18) | collective-permute-done | bytes 327712 | tf_op jit(solution)/shard_map/terms_z1/ppermute | solution.py:34
  110.4 1.7 %collective-permute-start.25 = (bf16[320,256]{1,0:T(8,128)(2,1)S(1)}, bf16[320,256]{1,0:T(8,128)(2,1)S(1)}, u32[]{:S(2)}, u32[]{:S(2)}) collective-permute-start(bf16[320,256]{1,0:T(8,128)(2,1)S(1)} %fusion), channel_id=1, source_target_pairs={{0,16},{2,18},{4,20},{6,22},{8,24},{10,26},{12,28},{14,30},{16,0},... | collective-permute-start | bytes 491528 | tf_op jit(solution)/shard_map/terms_z2/ppermute | solution.py:34
  112.1 2.0 %collective-permute-done.23 = bf16[2,320,128]{2,1,0:T(8,128)(2,1)S(1)} collective-permute-done((bf16[2,320,128]{2,1,0:T(8,128)(2,1)S(1)}, bf16[2,320,128]{2,1,0:T(8,128)(2,1)S(1)}, u32[]{:S(2)}, u32[]{:S(2)}) %collective-permute-start.23) | collective-permute-done | bytes 163872 | tf_op jit(solution)/shard_map/terms_z1/ppermute | solution.py:34
  114.1 1.5 %collective-permute-start.27 = (bf16[320,128]{1,0:T(8,128)(2,1)S(1)}, bf16[320,128]{1,0:T(8,128)(2,1)S(1)}, u32[]{:S(2)}, u32[]{:S(2)}) collective-permute-start(bf16[320,128]{1,0:T(8,128)(2,1)S(1)} %fusion.2), channel_id=1, source_target_pairs={{0,16},{2,18},{4,20},{6,22},{8,24},{10,26},{12,28},{14,30},{16,0},... | collective-permute-start | bytes 245768 | tf_op jit(solution)/shard_map/terms_z2/ppermute | solution.py:34
  115.6 6.3 %hidden_grads.1 = bf16[512,2560]{1,0:T(8,128)(2,1)} custom-call(s32[2]{0:T(128)S(1)} %copy-done.7, bf16[512,256]{1,0:T(8,128)(2,1)S(1)} %pad_maximum_fusion.2.own_ref.rest_0_, bf16[512,256]{1,0:T(8,128)(2,1)S(1)} %pad_maximum_fusion.3.own_ref.rest_1_, bf16[512,256]{1,0:T(8,128)(2,1)} %collective-permute-done.17.rest_2_, ...), custom_call_target="tpu_custom_call" | custom-call | flops 2684354560 | bytes 7864320 | tf_op jit(solution)/shard_map/hidden_grads/pallas_call | solution.py:382
  121.9 0.3 collective-permute-done.27
  122.2 0.1 bitcast_add_fusion
  122.3 0.1 bitcast_add_fusion.1
  122.3 0.7 pad_maximum_fusion.1
  123.1 0.7 pad_maximum_fusion
  (57 shorter events, 0.3 us)
Async XLA Ops:
  1.2 13.0 %copy-start.16 = (s32[2]{0:T(128)S(1)}, s32[2]{0:T(128)}, u32[]{:S(2)}) copy-start(s32[2]{0:T(128)} %param.16) | copy-start | bytes 28
  9.5 36.6 %collective-permute-start.4 = (bf16[8,320,512]{2,1,0:T(8,128)(2,1)}, bf16[8,320,512]{2,1,0:T(8,128)(2,1)}, u32[]{:S(2)}, u32[]{:S(2)}) collective-permute-start(bf16[8,320,512]{2,1,0:T(8,128)(2,1)} %get-tuple-element.68), channel_id=1, source_target_pairs={{0,2},{2,0},{4,6},{6,4},{8,10},{10,8},{12,14},{14,12},{16,18},{18,... | collective-permute-start | bytes 7864328 | tf_op jit(solution)/shard_map/turned_core/ppermute | solution.py:34
  10.0 13.0 %collective-permute-start = (bf16[2,512,128]{2,1,0:T(8,128)(2,1)}, bf16[2,512,128]{2,1,0:T(8,128)(2,1)S(1)}, u32[]{:S(2)}, u32[]{:S(2)}) collective-permute-start(bf16[2,512,128]{2,1,0:T(8,128)(2,1)} %get-tuple-element.66.rest_0_), channel_id=1, source_target_pairs={{0,4},{2,6},{4,8},{6,10},{8,12},{10,14},{12,16},{14,18},{16,20},{1... | collective-permute-start | bytes 786440 | tf_op jit(solution)/shard_map/pair_two/ppermute | solution.py:34
  12.5 10.5 %collective-permute-start.6 = (bf16[2,512,128]{2,1,0:T(8,128)(2,1)}, bf16[2,512,128]{2,1,0:T(8,128)(2,1)S(1)}, u32[]{:S(2)}, u32[]{:S(2)}) collective-permute-start(bf16[2,512,128]{2,1,0:T(8,128)(2,1)} %get-tuple-element.66.rest_0_), channel_id=1, source_target_pairs={{0,2},{2,8},{4,6},{6,12},{8,10},{10,16},{12,14},{14,20},{16,18},{1... | collective-permute-start | bytes 786440 | tf_op jit(solution)/shard_map/pair_other/ppermute | solution.py:34
  12.7 33.4 %collective-permute-start.5 = (bf16[2560,256]{1,0:T(8,128)(2,1)}, bf16[2560,256]{1,0:T(8,128)(2,1)S(1)}, u32[]{:S(2)}, u32[]{:S(2)}) collective-permute-start(bf16[2560,256]{1,0:T(8,128)(2,1)} %get-tuple-element.69), channel_id=1, source_target_pairs={{0,1},{1,0},{2,3},{3,2},{4,5},{5,4},{6,7},{7,6},{8,9},{9,8},{10,11... | collective-permute-start | bytes 3932168 | tf_op jit(solution)/shard_map/weights_y/ppermute | solution.py:34
  22.9 3.1 %copy-start.13 = (bf16[2,512,128]{2,1,0:T(8,128)(2,1)}, bf16[2,512,128]{2,1,0:T(8,128)(2,1)S(1)}, u32[]{:S(2)}) copy-start(bf16[2,512,128]{2,1,0:T(8,128)(2,1)S(1)} %collective-permute-done.rest_2_) | copy-start | bytes 786436
  22.9 3.1 %collective-permute-start.7 = (bf16[2,512,128]{2,1,0:T(8,128)(2,1)S(1)}, bf16[2,512,128]{2,1,0:T(8,128)(2,1)S(1)}, u32[]{:S(2)}, u32[]{:S(2)}) collective-permute-start(bf16[2,512,128]{2,1,0:T(8,128)(2,1)S(1)} %collective-permute-done.rest_2_), channel_id=1, source_target_pairs={{0,2},{2,0},{4,6},{6,4},{8,10},{10,8},{12,14},{14,12},{16,18},{18,... | collective-permute-start | bytes 786440 | tf_op jit(solution)/shard_map/pair_core/ppermute | solution.py:34
  22.9 23.2 %copy-start.8 = (bf16[2,512,128]{2,1,0:T(8,128)(2,1)S(1)}, bf16[2,512,128]{2,1,0:T(8,128)(2,1)}, u32[]{:S(2)}) copy-start(bf16[2,512,128]{2,1,0:T(8,128)(2,1)} %get-tuple-element.76.rest_0_) | copy-start | bytes 786436
  22.9 23.2 %copy-start.9 = (s32[2]{0:T(128)S(1)}, s32[2]{0:T(128)}, u32[]{:S(2)}) copy-start(s32[2]{0:T(128)} %len_ref.3) | copy-start | bytes 28
  22.9 23.2 %copy-start.10 = (s32[2]{0:T(128)S(1)}, s32[2]{0:T(128)}, u32[]{:S(2)}) copy-start(s32[2]{0:T(128)} %and_select_fusion.sel_ref) | copy-start | bytes 28
  23.0 18.9 %collective-permute-start.3 = (bf16[2,512,128]{2,1,0:T(8,128)(2,1)}, bf16[2,512,128]{2,1,0:T(8,128)(2,1)S(1)}, u32[]{:S(2)}, u32[]{:S(2)}) collective-permute-start(bf16[2,512,128]{2,1,0:T(8,128)(2,1)} %get-tuple-element.76.rest_0_), channel_id=1, source_target_pairs={{0,6},{2,4},{4,10},{6,8},{8,14},{10,12},{12,18},{14,16},{16,22},{1... | collective-permute-start | bytes 786440 | tf_op jit(solution)/shard_map/pair_cross/ppermute | solution.py:34
  23.0 3.1 %copy-start.14 = (bf16[2,512,128]{2,1,0:T(8,128)(2,1)}, bf16[2,512,128]{2,1,0:T(8,128)(2,1)S(1)}, u32[]{:S(2)}) copy-start(bf16[2,512,128]{2,1,0:T(8,128)(2,1)S(1)} %collective-permute-done.6.rest_1_) | copy-start | bytes 786436
  23.0 21.8 %collective-permute-start.2 = (bf16[2,512,128]{2,1,0:T(8,128)(2,1)}, bf16[2,512,128]{2,1,0:T(8,128)(2,1)S(1)}, u32[]{:S(2)}, u32[]{:S(2)}) collective-permute-start(bf16[2,512,128]{2,1,0:T(8,128)(2,1)} %get-tuple-element.76.rest_0_), channel_id=1, source_target_pairs={{0,4},{2,6},{4,8},{6,10},{8,12},{10,14},{12,16},{14,18},{16,20},{1... | collective-permute-start | bytes 786440 | tf_op jit(solution)/shard_map/pair_two/ppermute | solution.py:34
  26.1 0.7 copy-start.15
  26.1 18.8 %collective-permute-start.1 = (bf16[2,512,128]{2,1,0:T(8,128)(2,1)}, bf16[2,512,128]{2,1,0:T(8,128)(2,1)S(1)}, u32[]{:S(2)}, u32[]{:S(2)}) collective-permute-start(bf16[2,512,128]{2,1,0:T(8,128)(2,1)} %get-tuple-element.76.rest_0_), channel_id=1, source_target_pairs={{0,2},{2,8},{4,6},{6,12},{8,10},{10,16},{12,14},{14,20},{16,18},{1... | collective-permute-start | bytes 786440 | tf_op jit(solution)/shard_map/pair_other/ppermute | solution.py:34
  41.9 4.2 %copy-start.12 = (bf16[2,512,128]{2,1,0:T(8,128)(2,1)}, bf16[2,512,128]{2,1,0:T(8,128)(2,1)S(1)}, u32[]{:S(2)}) copy-start(bf16[2,512,128]{2,1,0:T(8,128)(2,1)S(1)} %collective-permute-done.3.rest_3_) | copy-start | bytes 786436
  41.9 21.1 %collective-permute-start.8 = (bf16[2,512,128]{2,1,0:T(8,128)(2,1)}, bf16[2,512,128]{2,1,0:T(8,128)(2,1)S(1)}, u32[]{:S(2)}, u32[]{:S(2)}) collective-permute-start(bf16[2,512,128]{2,1,0:T(8,128)(2,1)} %get-tuple-element.92), channel_id=1, source_target_pairs={{0,26},{2,0},{4,30},{6,4},{8,2},{10,8},{12,6},{14,12},{16,10},{18,... | collective-permute-start | bytes 786440 | tf_op jit(solution)/shard_map/grad_other/ppermute | solution.py:34
  44.8 18.2 %collective-permute-start.9 = (bf16[2,512,128]{2,1,0:T(8,128)(2,1)}, bf16[2,512,128]{2,1,0:T(8,128)(2,1)S(1)}, u32[]{:S(2)}, u32[]{:S(2)}) collective-permute-start(bf16[2,512,128]{2,1,0:T(8,128)(2,1)} %get-tuple-element.93), channel_id=1, source_target_pairs={{0,28},{2,30},{4,0},{6,2},{8,4},{10,6},{12,8},{14,10},{16,12},{18,... | collective-permute-start | bytes 786440 | tf_op jit(solution)/shard_map/grad_two/ppermute | solution.py:34
  44.9 18.2 %collective-permute-start.10 = (bf16[2,512,128]{2,1,0:T(8,128)(2,1)}, bf16[2,512,128]{2,1,0:T(8,128)(2,1)S(1)}, u32[]{:S(2)}, u32[]{:S(2)}) collective-permute-start(bf16[2,512,128]{2,1,0:T(8,128)(2,1)} %get-tuple-element.94), channel_id=1, source_target_pairs={{0,30},{2,28},{4,2},{6,0},{8,6},{10,4},{12,10},{14,8},{16,14},{18,... | collective-permute-start | bytes 786440 | tf_op jit(solution)/shard_map/grad_cross/ppermute | solution.py:34
  46.1 16.9 %copy-start.11 = (bf16[2,512,128]{2,1,0:T(8,128)(2,1)S(1)}, bf16[2,512,128]{2,1,0:T(8,128)(2,1)}, u32[]{:S(2)}) copy-start(bf16[2,512,128]{2,1,0:T(8,128)(2,1)} %get-tuple-element.91) | copy-start | bytes 786436
  61.6 2.0 %collective-permute-start.11 = (bf16[2,512,128]{2,1,0:T(8,128)(2,1)S(1)}, bf16[2,512,128]{2,1,0:T(8,128)(2,1)S(1)}, u32[]{:S(2)}, u32[]{:S(2)}) collective-permute-start(bf16[2,512,128]{2,1,0:T(8,128)(2,1)S(1)} %get-tuple-element.97), channel_id=1, source_target_pairs={{0,2},{2,0},{4,6},{6,4},{8,10},{10,8},{12,14},{14,12},{16,18},{18,... | collective-permute-start | bytes 786440 | tf_op jit(solution)/shard_map/grad_core/ppermute | solution.py:34
  62.5 10.2 %collective-permute-start.13 = (bf16[2,512,128]{2,1,0:T(8,128)(2,1)S(1)}, bf16[2,512,128]{2,1,0:T(8,128)(2,1)S(1)}, u32[]{:S(2)}, u32[]{:S(2)}) collective-permute-start(bf16[2,512,128]{2,1,0:T(8,128)(2,1)S(1)} %get-tuple-element.101), channel_id=1, source_target_pairs={{0,26},{2,0},{4,30},{6,4},{8,2},{10,8},{12,6},{14,12},{16,10},{18,... | collective-permute-start | bytes 786440 | tf_op jit(solution)/shard_map/grad_other/ppermute | solution.py:34
  63.3 4.1 %collective-permute-start.12 = (bf16[512,256]{1,0:T(8,128)(2,1)S(1)}, bf16[512,256]{1,0:T(8,128)(2,1)S(1)}, u32[]{:S(2)}, u32[]{:S(2)}) collective-permute-start(bf16[512,256]{1,0:T(8,128)(2,1)S(1)} %pad_maximum_fusion.2.own_ref.rest_0_), channel_id=1, source_target_pairs={{0,2},{2,0},{4,6},{6,4},{8,10},{10,8},{12,14},{14,12},{16,18},{18,... | collective-permute-start | bytes 786440 | tf_op jit(solution)/shard_map/own_core/ppermute | solution.py:34
  63.7 10.0 %collective-permute-start.14 = (bf16[2,512,128]{2,1,0:T(8,128)(2,1)S(1)}, bf16[2,512,128]{2,1,0:T(8,128)(2,1)S(1)}, u32[]{:S(2)}, u32[]{:S(2)}) collective-permute-start(bf16[2,512,128]{2,1,0:T(8,128)(2,1)S(1)} %add_convert_fusion.1), channel_id=1, source_target_pairs={{0,28},{2,30},{4,0},{6,2},{8,4},{10,6},{12,8},{14,10},{16,12},{18,... | collective-permute-start | bytes 786440 | tf_op jit(solution)/shard_map/grad_two/ppermute | solution.py:34
  67.4 4.8 %copy-start.5 = (bf16[512,256]{1,0:T(8,128)(2,1)}, bf16[512,256]{1,0:T(8,128)(2,1)S(1)}, u32[]{:S(2)}) copy-start(bf16[512,256]{1,0:T(8,128)(2,1)S(1)} %collective-permute-done.12.pair_ref) | copy-start | bytes 786436
  67.4 2.6 %copy-start = (bf16[2,8,320,512]{3,2,1,0:T(8,128)(2,1)S(1)}, bf16[2,8,320,512]{3,2,1,0:T(8,128)(2,1)}, u32[]{:S(2)}) copy-start(bf16[2,8,320,512]{3,2,1,0:T(8,128)(2,1)} %get-tuple-element.95.both_ref) | copy-start | bytes 15728644
  72.2 18.5 %collective-permute-start.15 = (bf16[4,320,256]{2,1,0:T(8,128)(2,1)}, bf16[4,320,256]{2,1,0:T(8,128)(2,1)}, u32[]{:S(2)}, u32[]{:S(2)}) collective-permute-start(bf16[4,320,256]{2,1,0:T(8,128)(2,1)} %weight_terms.6), channel_id=1, source_target_pairs={{0,4},{2,6},{4,0},{6,2},{8,12},{10,14},{12,8},{14,10},{16,20},{18,... | collective-permute-start | bytes 1966088 | tf_op jit(solution)/shard_map/terms_x/ppermute | solution.py:34
  73.8 2.2 %collective-permute-start.16 = (bf16[512,256]{1,0:T(8,128)(2,1)S(1)}, bf16[512,256]{1,0:T(8,128)(2,1)S(1)}, u32[]{:S(2)}, u32[]{:S(2)}) collective-permute-start(bf16[512,256]{1,0:T(8,128)(2,1)S(1)} %pad_maximum_fusion.3.own_ref.rest_1_), channel_id=1, source_target_pairs={{0,2},{2,0},{4,6},{6,4},{8,10},{10,8},{12,14},{14,12},{16,18},{18,... | collective-permute-start | bytes 786440 | tf_op jit(solution)/shard_map/own_core/ppermute | solution.py:34
  73.9 41.6 %collective-permute-start.24 = (bf16[2560,256]{1,0:T(8,128)(2,1)S(1)}, bf16[2560,256]{1,0:T(8,128)(2,1)S(1)}, u32[]{:S(2)}, u32[]{:S(2)}) collective-permute-start(bf16[2560,256]{1,0:T(8,128)(2,1)S(1)} %collective-permute-done.5.rest_6_), channel_id=1, source_target_pairs={{0,2},{2,0},{4,6},{6,4},{8,10},{10,8},{12,14},{14,12},{16,18},{18,... | collective-permute-start | bytes 3932168 | tf_op jit(solution)/shard_map/weights_core/ppermute | solution.py:34
  74.4 16.3 %collective-permute-start.17 = (bf16[512,256]{1,0:T(8,128)(2,1)S(1)}, bf16[512,256]{1,0:T(8,128)(2,1)}, u32[]{:S(2)}, u32[]{:S(2)}) collective-permute-start(bf16[512,256]{1,0:T(8,128)(2,1)S(1)} %pad_maximum_fusion.2.own_ref.rest_0_), channel_id=1, source_target_pairs={{0,1},{1,0},{2,3},{3,2},{4,5},{5,4},{6,7},{7,6},{8,9},{9,8},{10,11... | collective-permute-start | bytes 786440 | tf_op jit(solution)/shard_map/own_y/ppermute | solution.py:34
  76.0 2.5 %copy-start.1 = (bf16[2,8,320,512]{3,2,1,0:T(8,128)(2,1)S(1)}, bf16[2,8,320,512]{3,2,1,0:T(8,128)(2,1)}, u32[]{:S(2)}) copy-start(bf16[2,8,320,512]{3,2,1,0:T(8,128)(2,1)} %get-tuple-element.95.both_ref) | copy-start | bytes 15728644
  80.6 13.2 %collective-permute-start.19 = (bf16[4,320,128]{2,1,0:T(8,128)(2,1)}, bf16[4,320,128]{2,1,0:T(8,128)(2,1)}, u32[]{:S(2)}, u32[]{:S(2)}) collective-permute-start(bf16[4,320,128]{2,1,0:T(8,128)(2,1)} %weight_terms.7), channel_id=1, source_target_pairs={{0,8},{2,10},{4,12},{6,14},{8,0},{10,2},{12,4},{14,6},{16,24},{18,... | collective-permute-start | bytes 983048 | tf_op jit(solution)/shard_map/terms_z1/ppermute | solution.py:34
  83.7 2.5 %copy-start.2 = (bf16[2,8,320,512]{3,2,1,0:T(8,128)(2,1)S(1)}, bf16[2,8,320,512]{3,2,1,0:T(8,128)(2,1)}, u32[]{:S(2)}) copy-start(bf16[2,8,320,512]{3,2,1,0:T(8,128)(2,1)} %get-tuple-element.95.both_ref) | copy-start | bytes 15728644
  86.2 4.5 %copy-start.6 = (bf16[512,256]{1,0:T(8,128)(2,1)S(1)}, bf16[512,256]{1,0:T(8,128)(2,1)}, u32[]{:S(2)}) copy-start(bf16[512,256]{1,0:T(8,128)(2,1)} %copy-done.5) | copy-start | bytes 786436
  87.6 10.5 %collective-permute-start.21 = (bf16[4,320,128]{2,1,0:T(8,128)(2,1)S(1)}, bf16[4,320,128]{2,1,0:T(8,128)(2,1)S(1)}, u32[]{:S(2)}, u32[]{:S(2)}) collective-permute-start(bf16[4,320,128]{2,1,0:T(8,128)(2,1)S(1)} %weight_terms.8), channel_id=1, source_target_pairs={{0,4},{2,6},{4,0},{6,2},{8,12},{10,14},{12,8},{14,10},{16,20},{18,... | collective-permute-start | bytes 983048 | tf_op jit(solution)/shard_map/terms_x/ppermute | solution.py:34
  92.7 7.5 %collective-permute-start.22 = (bf16[512,256]{1,0:T(8,128)(2,1)S(1)}, bf16[512,256]{1,0:T(8,128)(2,1)S(1)}, u32[]{:S(2)}, u32[]{:S(2)}) collective-permute-start(bf16[512,256]{1,0:T(8,128)(2,1)S(1)} %pad_maximum_fusion.3.own_ref.rest_1_), channel_id=1, source_target_pairs={{0,1},{1,0},{2,3},{3,2},{4,5},{5,4},{6,7},{7,6},{8,9},{9,8},{10,11... | collective-permute-start | bytes 786440 | tf_op jit(solution)/shard_map/own_y/ppermute | solution.py:34
  95.6 10.0 %collective-permute-start.20 = (bf16[2,320,128]{2,1,0:T(8,128)(2,1)S(1)}, bf16[2,320,128]{2,1,0:T(8,128)(2,1)S(1)}, u32[]{:S(2)}, u32[]{:S(2)}) collective-permute-start(bf16[2,320,128]{2,1,0:T(8,128)(2,1)S(1)} %get-tuple-element.109), channel_id=1, source_target_pairs={{0,16},{2,18},{4,20},{6,22},{8,24},{10,26},{12,28},{14,30},{16,0},... | collective-permute-start | bytes 491528 | tf_op jit(solution)/shard_map/terms_z2/ppermute | solution.py:34
  97.3 13.1 %collective-permute-start.18 = (bf16[2,320,256]{2,1,0:T(8,128)(2,1)S(1)}, bf16[2,320,256]{2,1,0:T(8,128)(2,1)S(1)}, u32[]{:S(2)}, u32[]{:S(2)}) collective-permute-start(bf16[2,320,256]{2,1,0:T(8,128)(2,1)S(1)} %get-tuple-element.106), channel_id=1, source_target_pairs={{0,8},{2,10},{4,12},{6,14},{8,0},{10,2},{12,4},{14,6},{16,24},{18,... | collective-permute-start | bytes 983048 | tf_op jit(solution)/shard_map/terms_z1/ppermute | solution.py:34
  100.2 15.4 %copy-start.3 = (bf16[5120,256]{1,0:T(8,128)(2,1)S(1)}, bf16[5120,256]{1,0:T(8,128)(2,1)}, u32[]{:S(2)}) copy-start(bf16[5120,256]{1,0:T(8,128)(2,1)} %rest_4_.5) | copy-start | bytes 7864324
  100.2 15.4 %copy-start.4 = (bf16[5120,256]{1,0:T(8,128)(2,1)S(1)}, bf16[5120,256]{1,0:T(8,128)(2,1)}, u32[]{:S(2)}) copy-start(bf16[5120,256]{1,0:T(8,128)(2,1)} %rest_5_.5) | copy-start | bytes 7864324
  100.2 15.4 %copy-start.7 = (s32[2]{0:T(128)S(1)}, s32[2]{0:T(128)}, u32[]{:S(2)}) copy-start(s32[2]{0:T(128)} %pad_add_fusion.at_ref) | copy-start | bytes 28
  101.6 12.4 %collective-permute-start.23 = (bf16[2,320,128]{2,1,0:T(8,128)(2,1)S(1)}, bf16[2,320,128]{2,1,0:T(8,128)(2,1)S(1)}, u32[]{:S(2)}, u32[]{:S(2)}) collective-permute-start(bf16[2,320,128]{2,1,0:T(8,128)(2,1)S(1)} %get-tuple-element.115), channel_id=1, source_target_pairs={{0,8},{2,10},{4,12},{6,14},{8,0},{10,2},{12,4},{14,6},{16,24},{18,... | collective-permute-start | bytes 491528 | tf_op jit(solution)/shard_map/terms_z1/ppermute | solution.py:34
  105.7 16.2 %collective-permute-start.26 = (bf16[320,128]{1,0:T(8,128)(2,1)S(1)}, bf16[320,128]{1,0:T(8,128)(2,1)S(1)}, u32[]{:S(2)}, u32[]{:S(2)}) collective-permute-start(bf16[320,128]{1,0:T(8,128)(2,1)S(1)} %fusion.1), channel_id=1, source_target_pairs={{0,4},{2,6},{4,0},{6,2},{8,12},{10,14},{12,8},{14,10},{16,20},{18,... | collective-permute-start | bytes 245768 | tf_op jit(solution)/shard_map/terms_x/ppermute | solution.py:34
  110.4 11.8 %collective-permute-start.25 = (bf16[320,256]{1,0:T(8,128)(2,1)S(1)}, bf16[320,256]{1,0:T(8,128)(2,1)S(1)}, u32[]{:S(2)}, u32[]{:S(2)}) collective-permute-start(bf16[320,256]{1,0:T(8,128)(2,1)S(1)} %fusion), channel_id=1, source_target_pairs={{0,16},{2,18},{4,20},{6,22},{8,24},{10,26},{12,28},{14,30},{16,0},... | collective-permute-start | bytes 491528 | tf_op jit(solution)/shard_map/terms_z2/ppermute | solution.py:34
  114.1 8.1 %collective-permute-start.27 = (bf16[320,128]{1,0:T(8,128)(2,1)S(1)}, bf16[320,128]{1,0:T(8,128)(2,1)S(1)}, u32[]{:S(2)}, u32[]{:S(2)}) collective-permute-start(bf16[320,128]{1,0:T(8,128)(2,1)S(1)} %fusion.2), channel_id=1, source_target_pairs={{0,16},{2,18},{4,20},{6,22},{8,24},{10,26},{12,28},{14,30},{16,0},... | collective-permute-start | bytes 245768 | tf_op jit(solution)/shard_map/terms_z2/ppermute | solution.py:34

commit v5 on v3

--- a/solution.py
+++ b/solution.py
@@ -443,7 +443,8 @@
     *pairs, near, turned, mine = project(at, prompt_hidden, w_key, w_value, size)
     two = permute(pairs[0], "dp", lambda i: (i + 2) % size, "pair_two")
     one = permute(pairs[0], "dp", other, "pair_other")
-    received = [[pairs[0], one, two, permute(two, "dp", lambda i: i ^ 1, "pair_core")]]
+    core_two = permute(after(two, sel), "dp", lambda i: i ^ 1, "pair_core")
+    received = [[pairs[0], one, two, core_two]]
     far_a = permute(mine, "mp", lambda i: 1 - i, "weights_y")
     far = permute(turned, "dp", lambda i: i ^ 1, "turned_core")
     later = after(pairs[1], two)

time: 122 us -> 123 us (level)
  starting transfers between devices: 27.3 us -> 31.3 us
  waiting for transfers between devices: 32.3 us -> 28.7 us
    ppermute x28, starting transfers between devices: 27.3 us -> 31.3 us  [permute(): lax.ppermute(block, axis, [(i, target(i)) for i in range(lax.axis_size(ax...]
    ppermute x28, waiting for transfers between devices: 32.3 us -> 28.7 us  [permute(): lax.ppermute(block, axis, [(i, target(i)) for i in range(lax.axis_size(ax...]
where the time goes in v5:
time: 123 us; the launch traced here: 122 us
  Pallas kernels  50.7 us (41%)
  starting transfers between devices  31.3 us (25%)
  waiting for transfers between devices  28.7 us (23%)
  local copies, waits for them, and re-layouts  7.38 us (6%)
  other arithmetic  3.08 us (3%)
    ppermute x28, starting transfers between devices, permute(): lax.ppermute(block, axis, [(i, target(i)) for i in range(lax.axis_size(ax...  31.3 us
    ppermute x28, waiting for transfers between devices, permute(): lax.ppermute(block, axis, [(i, target(i)) for i in range(lax.axis_size(ax...  28.7 us
    pallas_call x2, Pallas kernels, attend(): pl.pallas_call(functools.partial(attend_kernel, heads, len(loads)), out_s...  26.5 us
    pallas_call x6, Pallas kernels, weight_terms(): pl.pallas_call(functools.partial(weight_kernel, first), out_shape=[jax.Sh...  9.7 us
    pallas_call x1, Pallas kernels, project(): pl.pallas_call(functools.partial(project_kernel, groups), out_shape=[jax....  8.21 us
    unnamed x48, local copies, waits for them, and re-layouts  7.32 us
    pallas_call x1, Pallas kernels, hidden_grads(): pl.pallas_call(functools.partial(hidden_kernel, groups), out_shape=jax.Sh...  6.29 us
  transfers between devices with their start and end apart: 28, of which 11 were waited for; matrix products, arithmetic and copies ran while one was open for 1% of the time, Pallas kernels for 33%

profile of v5, /device:TPU:0, one launch (start us, length us, event | category | flops | bytes accessed | tf_op | source)
XLA Modules:
  0.0 122.2 jit_solution(18171442754795020811)
XLA Ops:
  0.6 0.7 pad_add_fusion.at_ref
  1.3 8.2 %project.1 = (bf16[2,512,128]{2,1,0:T(8,128)(2,1)}, bf16[2,512,128]{2,1,0:T(8,128)(2,1)}, bf16[8,320,512]{2,1,0:T(8,128)(2,1)}, bf16[8,320,512]{2,1,0:T(8,128)(2,1)}, bf16[2560,256]{1,0:T(8,128)(2,1)}) custom-call(s32[2]{0:T(128)} %pad_add_fusion.at_ref, bf16[512,5120]{1,0:T(8,128)(2,1)} %h_ref.1, bf16[5120,256]{1,0:T(8,128)(2,1)} %rest_4_.5, ...), custom_call_target="tpu_custom_call" | custom-call | flops 2684354560 | bytes 15728640 | tf_op jit(solution)/shard_map/project/pallas_call | solution.py:105
  9.5 0.5 collective-permute-start.4
  10.0 2.5 %collective-permute-start = (bf16[2,512,128]{2,1,0:T(8,128)(2,1)}, bf16[2,512,128]{2,1,0:T(8,128)(2,1)}, u32[]{:S(2)}, u32[]{:S(2)}) collective-permute-start(bf16[2,512,128]{2,1,0:T(8,128)(2,1)} %get-tuple-element.67.rest_0_), channel_id=1, source_target_pairs={{0,4},{2,6},{4,8},{6,10},{8,12},{10,14},{12,16},{14,18},{16,20},{1... | collective-permute-start | bytes 786440 | tf_op jit(solution)/shard_map/pair_two/ppermute | solution.py:34
  12.6 0.2 collective-permute-start.6
  12.8 1.5 %collective-permute-start.5 = (bf16[2560,256]{1,0:T(8,128)(2,1)}, bf16[2560,256]{1,0:T(8,128)(2,1)S(1)}, u32[]{:S(2)}, u32[]{:S(2)}) collective-permute-start(bf16[2560,256]{1,0:T(8,128)(2,1)} %get-tuple-element.70), channel_id=1, source_target_pairs={{0,1},{1,0},{2,3},{3,2},{4,5},{5,4},{6,7},{7,6},{8,9},{9,8},{10,11... | collective-permute-start | bytes 3932168 | tf_op jit(solution)/shard_map/weights_y/ppermute | solution.py:34
  14.3 8.8 %collective-permute-done.rest_2_ = bf16[2,512,128]{2,1,0:T(8,128)(2,1)} collective-permute-done((bf16[2,512,128]{2,1,0:T(8,128)(2,1)}, bf16[2,512,128]{2,1,0:T(8,128)(2,1)}, u32[]{:S(2)}, u32[]{:S(2)}) %collective-permute-start) | collective-permute-done | bytes 262176 | tf_op jit(solution)/shard_map/pair_two/ppermute | solution.py:34
  23.1 0.1 collective-permute-start.3
  23.2 3.0 %collective-permute-start.2 = (bf16[2,512,128]{2,1,0:T(8,128)(2,1)}, bf16[2,512,128]{2,1,0:T(8,128)(2,1)S(1)}, u32[]{:S(2)}, u32[]{:S(2)}) collective-permute-start(bf16[2,512,128]{2,1,0:T(8,128)(2,1)} %get-tuple-element.77.rest_0_), channel_id=1, source_target_pairs={{0,4},{2,6},{4,8},{6,10},{8,12},{10,14},{12,16},{14,18},{16,20},{1... | collective-permute-start | bytes 786440 | tf_op jit(solution)/shard_map/pair_two/ppermute | solution.py:34
  26.3 0.0 copy-start.14
  26.3 1.6 %copy-done.14 = bf16[512,2048]{1,0:T(8,128)(2,1)S(1)} copy-done((bf16[512,2048]{1,0:T(8,128)(2,1)S(1)}, bf16[512,2048]{1,0:T(8,128)(2,1)}, u32[]{:S(2)}) %copy-start.14) | copy-done | bytes 2097176
  27.9 0.9 copy-done.16
  28.8 0.9 copy-done.18
  29.8 0.9 copy-done.21
  30.7 13.6 %attend_0.1 = (bf16[512,2048]{1,0:T(8,128)(2,1)}, bf16[512,2048]{1,0:T(8,128)(2,1)}, bf16[512,256]{1,0:T(8,128)(2,1)}, bf16[512,256]{1,0:T(8,128)(2,1)}, bf16[2,...) custom-call(s32[2]{0:T(128)S(1)} %and_select_fusion.sel_ref, ...), custom_call_target="tpu_custom_call" | custom-call | flops 9663676416 | bytes 8388608 | tf_op jit(solution)/shard_map/attend_0/pallas_call | solution.py:261
  44.3 3.6 %collective-permute-start.8 = (bf16[2,512,128]{2,1,0:T(8,128)(2,1)S(1)}, bf16[2,512,128]{2,1,0:T(8,128)(2,1)S(1)}, u32[]{:S(2)}, u32[]{:S(2)}) collective-permute-start(bf16[2,512,128]{2,1,0:T(8,128)(2,1)S(1)} %get-tuple-element.93), channel_id=1, source_target_pairs={{0,26},{2,0},{4,30},{6,4},{8,2},{10,8},{12,6},{14,12},{16,10},{18,... | collective-permute-start | bytes 786440 | tf_op jit(solution)/shard_map/grad_other/ppermute | solution.py:34
  47.9 1.3 %collective-permute-start.10 = (bf16[2,512,128]{2,1,0:T(8,128)(2,1)S(1)}, bf16[2,512,128]{2,1,0:T(8,128)(2,1)S(1)}, u32[]{:S(2)}, u32[]{:S(2)}) collective-permute-start(bf16[2,512,128]{2,1,0:T(8,128)(2,1)S(1)} %get-tuple-element.95), channel_id=1, source_target_pairs={{0,30},{2,28},{4,2},{6,0},{8,6},{10,4},{12,10},{14,8},{16,14},{18,... | collective-permute-start | bytes 786440 | tf_op jit(solution)/shard_map/grad_cross/ppermute | solution.py:34
  49.2 1.1 copy-done.4
  50.3 12.9 %attend_1.1 = (bf16[512,2048]{1,0:T(8,128)(2,1)}, bf16[512,2048]{1,0:T(8,128)(2,1)}, bf16[512,256]{1,0:T(8,128)(2,1)}, bf16[512,256]{1,0:T(8,128)(2,1)}, bf16[2,...) custom-call(s32[2]{0:T(128)S(1)} %and_select_fusion.sel_ref, ...), custom_call_target="tpu_custom_call", output_to_operand_aliasing={{0}: (12, {}), {1}: (13, {}), {2}: (14, {}), {3}: (15, {})} | custom-call | flops 9663676416 | bytes 8388608 | tf_op jit(solution)/shard_map/attend_1/pallas_call | solution.py:261
  63.3 0.1 collective-permute-start.11
  63.4 0.1 add_convert_fusion.2
  63.6 0.5 collective-permute-start.12
  64.1 0.1 add_add_fusion.at_ref
  64.2 0.7 collective-permute-done.11
  64.9 0.1 add_convert_fusion.1
  64.9 0.4 collective-permute-done.12.pair_ref
  65.3 2.2 %weight_terms.6 = bf16[4,320,256]{2,1,0:T(8,128)(2,1)} custom-call(s32[4]{0:T(128)S(1)} %add_add_fusion.at_ref, bf16[8,320,512]{2,1,0:T(8,128)(2,1)S(1)} %get-tuple-element.96.near_ref, bf16[8,320,512]{2,1,0:T(8,128)(2,1)S(1)} %get-tuple-element.97.far_ref, bf16[512,256]{1,0:T(8,128)(2,1)S(1)} %pad_maximum_fusion.2.own_ref.rest_0_, ...), custom_call_target="tpu_custom_call" | custom-call | flops 671088640 | bytes 3932160 | tf_op jit(solution)/shard_map/weight_terms/pallas_call | solution.py:316
  67.5 1.5 %collective-permute-start.13 = (bf16[512,256]{1,0:T(8,128)(2,1)S(1)}, bf16[512,256]{1,0:T(8,128)(2,1)S(1)}, u32[]{:S(2)}, u32[]{:S(2)}) collective-permute-start(bf16[512,256]{1,0:T(8,128)(2,1)S(1)} %pad_maximum_fusion.2.own_ref.rest_0_), channel_id=1, source_target_pairs={{0,1},{1,0},{2,3},{3,2},{4,5},{5,4},{6,7},{7,6},{8,9},{9,8},{10,11... | collective-permute-start | bytes 786440 | tf_op jit(solution)/shard_map/own_y/ppermute | solution.py:34
  69.0 3.2 %collective-permute-start.15 = (bf16[2,512,128]{2,1,0:T(8,128)(2,1)S(1)}, bf16[2,512,128]{2,1,0:T(8,128)(2,1)S(1)}, u32[]{:S(2)}, u32[]{:S(2)}) collective-permute-start(bf16[2,512,128]{2,1,0:T(8,128)(2,1)S(1)} %add_convert_fusion.1), channel_id=1, source_target_pairs={{0,28},{2,30},{4,0},{6,2},{8,4},{10,6},{12,8},{14,10},{16,12},{18,... | collective-permute-start | bytes 786440 | tf_op jit(solution)/shard_map/grad_two/ppermute | solution.py:34
  72.2 0.2 collective-permute-start.16
  72.5 3.6 %collective-permute-done.13.rest_2_ = bf16[512,256]{1,0:T(8,128)(2,1)S(1)} collective-permute-done((bf16[512,256]{1,0:T(8,128)(2,1)S(1)}, bf16[512,256]{1,0:T(8,128)(2,1)S(1)}, u32[]{:S(2)}, u32[]{:S(2)}) %collective-permute-start.13) | collective-permute-done | bytes 262176 | tf_op jit(solution)/shard_map/own_y/ppermute | solution.py:34
  76.1 3.6 %collective-permute-done.15 = bf16[2,512,128]{2,1,0:T(8,128)(2,1)S(1)} collective-permute-done((bf16[2,512,128]{2,1,0:T(8,128)(2,1)S(1)}, bf16[2,512,128]{2,1,0:T(8,128)(2,1)S(1)}, u32[]{:S(2)}, u32[]{:S(2)}) %collective-permute-start.15) | collective-permute-done | bytes 262176 | tf_op jit(solution)/shard_map/grad_two/ppermute | solution.py:34
  79.7 0.1 add_convert_fusion
  79.9 0.1 collective-permute-start.17
  80.0 0.5 collective-permute-start.24
  80.4 0.1 add_add_fusion.1.at_ref
  80.5 0.1 pad_add_fusion.1.at_ref
  80.6 0.9 collective-permute-done.17.pair_ref
  81.5 1.7 %copy-done.1 = bf16[8,320,512]{2,1,0:T(8,128)(2,1)S(1)} copy-done((bf16[8,320,512]{2,1,0:T(8,128)(2,1)S(1)}, bf16[8,320,512]{2,1,0:T(8,128)(2,1)}, u32[]{:S(2)}) %copy-start.1) | copy-done | bytes 2621464
  83.2 1.4 %weight_terms.7 = bf16[4,320,128]{2,1,0:T(8,128)(2,1)S(1)} custom-call(s32[4]{0:T(128)S(1)} %add_add_fusion.1.at_ref, bf16[8,320,512]{2,1,0:T(8,128)(2,1)S(1)} %get-tuple-element.96.near_ref, bf16[8,320,512]{2,1,0:T(8,128)(2,1)S(1)} %copy-done.1, bf16[512,256]{1,0:T(8,128)(2,1)S(1)} %pad_maximum_fusion.3.own_ref.rest_1_, ...), custom_call_target="tpu_custom_call" | custom-call | flops 335544320 | bytes 3276800 | tf_op jit(solution)/shard_map/weight_terms/pallas_call | solution.py:316
  84.6 1.0 collective-permute-start.20
  85.6 1.4 %weight_terms.8 = bf16[4,320,128]{2,1,0:T(8,128)(2,1)S(1)} custom-call(s32[4]{0:T(128)S(1)} %add_add_fusion.at_ref, bf16[8,320,512]{2,1,0:T(8,128)(2,1)S(1)} %get-tuple-element.96.near_ref, bf16[8,320,512]{2,1,0:T(8,128)(2,1)S(1)} %copy-done.1, bf16[512,256]{1,0:T(8,128)(2,1)S(1)} %pad_maximum_fusion.3.own_ref.rest_1_, ...), custom_call_target="tpu_custom_call" | custom-call | flops 335544320 | bytes 3276800 | tf_op jit(solution)/shard_map/weight_terms/pallas_call | solution.py:316
  87.0 3.3 %collective-permute-start.19 = (bf16[4,320,128]{2,1,0:T(8,128)(2,1)S(1)}, bf16[4,320,128]{2,1,0:T(8,128)(2,1)S(1)}, u32[]{:S(2)}, u32[]{:S(2)}) collective-permute-start(bf16[4,320,128]{2,1,0:T(8,128)(2,1)S(1)} %weight_terms.8), channel_id=1, source_target_pairs={{0,4},{2,6},{4,0},{6,2},{8,12},{10,14},{12,8},{14,10},{16,20},{18,... | collective-permute-start | bytes 983048 | tf_op jit(solution)/shard_map/terms_x/ppermute | solution.py:34
  90.2 2.5 %collective-permute-done.16.rest_0_ = bf16[4,320,256]{2,1,0:T(8,128)(2,1)} collective-permute-done((bf16[4,320,256]{2,1,0:T(8,128)(2,1)}, bf16[4,320,256]{2,1,0:T(8,128)(2,1)}, u32[]{:S(2)}, u32[]{:S(2)}) %collective-permute-start.16) | collective-permute-done | bytes 655392 | tf_op jit(solution)/shard_map/terms_x/ppermute | solution.py:34
  92.7 2.0 %weight_terms.9 = (bf16[2,320,256]{2,1,0:T(8,128)(2,1)S(1)}, bf16[2,320,256]{2,1,0:T(8,128)(2,1)S(1)}) custom-call(s32[4]{0:T(128)S(1)} %pad_add_fusion.1.at_ref, bf16[8,320,512]{2,1,0:T(8,128)(2,1)S(1)} %get-tuple-element.96.near_ref, bf16[8,320,512]{2,1,0:T(8,128)(2,1)S(1)} %copy-done.1, bf16[512,256]{1,0:T(8,128)(2,1)S(1)} %pad_maximum_fusion.2.own_ref.rest_0_, ...), custom_call_target="tpu_custom_call" | custom-call | flops 671088640 | bytes 3932160 | tf_op jit(solution)/shard_map/weight_terms/pallas_call | solution.py:316
  94.7 1.9 %collective-permute-start.18 = (bf16[2,320,256]{2,1,0:T(8,128)(2,1)S(1)}, bf16[2,320,256]{2,1,0:T(8,128)(2,1)S(1)}, u32[]{:S(2)}, u32[]{:S(2)}) collective-permute-start(bf16[2,320,256]{2,1,0:T(8,128)(2,1)S(1)} %get-tuple-element.108), channel_id=1, source_target_pairs={{0,8},{2,10},{4,12},{6,14},{8,0},{10,2},{12,4},{14,6},{16,24},{18,... | collective-permute-start | bytes 983048 | tf_op jit(solution)/shard_map/terms_z1/ppermute | solution.py:34
  96.5 0.5 collective-permute-start.21
  97.0 0.1 pad_add_fusion.2.at_ref
  97.1 1.4 %weight_terms.10 = (bf16[2,320,128]{2,1,0:T(8,128)(2,1)S(1)}, bf16[2,320,128]{2,1,0:T(8,128)(2,1)S(1)}) custom-call(s32[4]{0:T(128)S(1)} %pad_add_fusion.2.at_ref, bf16[8,320,512]{2,1,0:T(8,128)(2,1)S(1)} %get-tuple-element.96.near_ref, bf16[8,320,512]{2,1,0:T(8,128)(2,1)S(1)} %copy-done.1, bf16[512,256]{1,0:T(8,128)(2,1)S(1)} %pad_maximum_fusion.3.own_ref.rest_1_, ...), custom_call_target="tpu_custom_call" | custom-call | flops 335544320 | bytes 3276800 | tf_op jit(solution)/shard_map/weight_terms/pallas_call | solution.py:316
  98.5 0.2 collective-permute-start.22
  98.8 0.2 collective-permute-done.19.rest_0_
  98.9 4.9 %collective-permute-done.21.rest_3_ = bf16[512,256]{1,0:T(8,128)(2,1)S(1)} collective-permute-done((bf16[512,256]{1,0:T(8,128)(2,1)S(1)}, bf16[512,256]{1,0:T(8,128)(2,1)S(1)}, u32[]{:S(2)}, u32[]{:S(2)}) %collective-permute-start.21) | collective-permute-done | bytes 262176 | tf_op jit(solution)/shard_map/own_y/ppermute | solution.py:34
  103.8 1.4 %weight_terms.11 = (bf16[2,320,128]{2,1,0:T(8,128)(2,1)S(1)}, bf16[2,320,128]{2,1,0:T(8,128)(2,1)S(1)}) custom-call(s32[4]{0:T(128)S(1)} %pad_add_fusion.1.at_ref, bf16[8,320,512]{2,1,0:T(8,128)(2,1)S(1)} %get-tuple-element.96.near_ref, bf16[8,320,512]{2,1,0:T(8,128)(2,1)S(1)} %copy-done.1, bf16[512,256]{1,0:T(8,128)(2,1)S(1)} %pad_maximum_fusion.3.own_ref.rest_1_, ...), custom_call_target="tpu_custom_call" | custom-call | flops 335544320 | bytes 3276800 | tf_op jit(solution)/shard_map/weight_terms/pallas_call | solution.py:316
  105.2 0.4 collective-permute-start.23
  105.6 1.5 %collective-permute-done.18 = bf16[2,320,256]{2,1,0:T(8,128)(2,1)S(1)} collective-permute-done((bf16[2,320,256]{2,1,0:T(8,128)(2,1)S(1)}, bf16[2,320,256]{2,1,0:T(8,128)(2,1)S(1)}, u32[]{:S(2)}, u32[]{:S(2)}) %collective-permute-start.18) | collective-permute-done | bytes 327712 | tf_op jit(solution)/shard_map/terms_z1/ppermute | solution.py:34
  107.2 1.3 %collective-permute-start.25 = (bf16[320,256]{1,0:T(8,128)(2,1)S(1)}, bf16[320,256]{1,0:T(8,128)(2,1)S(1)}, u32[]{:S(2)}, u32[]{:S(2)}) collective-permute-start(bf16[320,256]{1,0:T(8,128)(2,1)S(1)} %fusion), channel_id=1, source_target_pairs={{0,16},{2,18},{4,20},{6,22},{8,24},{10,26},{12,28},{14,30},{16,0},... | collective-permute-start | bytes 491528 | tf_op jit(solution)/shard_map/terms_z2/ppermute | solution.py:34
  108.5 2.7 %collective-permute-start.26 = (bf16[320,128]{1,0:T(8,128)(2,1)S(1)}, bf16[320,128]{1,0:T(8,128)(2,1)S(1)}, u32[]{:S(2)}, u32[]{:S(2)}) collective-permute-start(bf16[320,128]{1,0:T(8,128)(2,1)S(1)} %fusion.1), channel_id=1, source_target_pairs={{0,4},{2,6},{4,0},{6,2},{8,12},{10,14},{12,8},{14,10},{16,20},{18,... | collective-permute-start | bytes 245768 | tf_op jit(solution)/shard_map/terms_x/ppermute | solution.py:34
  111.2 1.8 %collective-permute-done.23 = bf16[2,320,128]{2,1,0:T(8,128)(2,1)S(1)} collective-permute-done((bf16[2,320,128]{2,1,0:T(8,128)(2,1)S(1)}, bf16[2,320,128]{2,1,0:T(8,128)(2,1)S(1)}, u32[]{:S(2)}, u32[]{:S(2)}) %collective-permute-start.23) | collective-permute-done | bytes 163872 | tf_op jit(solution)/shard_map/terms_z1/ppermute | solution.py:34
  113.0 1.2 collective-permute-start.27
  114.2 6.3 %hidden_grads.1 = bf16[512,2560]{1,0:T(8,128)(2,1)} custom-call(s32[2]{0:T(128)S(1)} %copy-done.10, bf16[512,256]{1,0:T(8,128)(2,1)S(1)} %pad_maximum_fusion.2.own_ref.rest_0_, bf16[512,256]{1,0:T(8,128)(2,1)S(1)} %pad_maximum_fusion.3.own_ref.rest_1_, bf16[512,256]{1,0:T(8,128)(2,1)S(1)} %copy-done.9, bf16[512,256]{1,0:T(8,128)(2,1)S(1)} %collective-permute-done.21.rest_3_, ...), custom_call_target="tpu_custom_call" | custom-call | flops 2684354560 | bytes 7864320 | tf_op jit(solution)/shard_map/hidden_grads/pallas_call | solution.py:382
  120.6 0.1 bitcast_add_fusion
  120.7 0.1 bitcast_add_fusion.1
  120.7 0.7 pad_maximum_fusion.1
  121.5 0.8 pad_maximum_fusion
  (71 shorter events, 0.4 us)
Async XLA Ops:
  1.3 13.0 %copy-start.23 = (s32[2]{0:T(128)S(1)}, s32[2]{0:T(128)}, u32[]{:S(2)}) copy-start(s32[2]{0:T(128)} %param.16) | copy-start | bytes 28
  1.3 24.9 %copy-start.12 = (bf16[512,2048]{1,0:T(8,128)(2,1)S(1)}, bf16[512,2048]{1,0:T(8,128)(2,1)}, u32[]{:S(2)}) copy-start(bf16[512,2048]{1,0:T(8,128)(2,1)} %q_ref.3) | copy-start | bytes 6291460
  1.3 24.9 %copy-start.22 = (s32[2]{0:T(128)S(1)}, s32[2]{0:T(128)}, u32[]{:S(2)}) copy-start(s32[2]{0:T(128)} %len_ref.3) | copy-start | bytes 28
  9.5 39.7 %collective-permute-start.4 = (bf16[8,320,512]{2,1,0:T(8,128)(2,1)}, bf16[8,320,512]{2,1,0:T(8,128)(2,1)}, u32[]{:S(2)}, u32[]{:S(2)}) collective-permute-start(bf16[8,320,512]{2,1,0:T(8,128)(2,1)} %get-tuple-element.69), channel_id=1, source_target_pairs={{0,2},{2,0},{4,6},{6,4},{8,10},{10,8},{12,14},{14,12},{16,18},{18,... | collective-permute-start | bytes 7864328 | tf_op jit(solution)/shard_map/turned_core/ppermute | solution.py:34
  10.0 13.1 %collective-permute-start = (bf16[2,512,128]{2,1,0:T(8,128)(2,1)}, bf16[2,512,128]{2,1,0:T(8,128)(2,1)}, u32[]{:S(2)}, u32[]{:S(2)}) collective-permute-start(bf16[2,512,128]{2,1,0:T(8,128)(2,1)} %get-tuple-element.67.rest_0_), channel_id=1, source_target_pairs={{0,4},{2,6},{4,8},{6,10},{8,12},{10,14},{12,16},{14,18},{16,20},{1... | collective-permute-start | bytes 786440 | tf_op jit(solution)/shard_map/pair_two/ppermute | solution.py:34
  12.6 10.6 %collective-permute-start.6 = (bf16[2,512,128]{2,1,0:T(8,128)(2,1)}, bf16[2,512,128]{2,1,0:T(8,128)(2,1)}, u32[]{:S(2)}, u32[]{:S(2)}) collective-permute-start(bf16[2,512,128]{2,1,0:T(8,128)(2,1)} %get-tuple-element.67.rest_0_), channel_id=1, source_target_pairs={{0,2},{2,8},{4,6},{6,12},{8,10},{10,16},{12,14},{14,20},{16,18},{1... | collective-permute-start | bytes 786440 | tf_op jit(solution)/shard_map/pair_other/ppermute | solution.py:34
  12.8 36.4 %collective-permute-start.5 = (bf16[2560,256]{1,0:T(8,128)(2,1)}, bf16[2560,256]{1,0:T(8,128)(2,1)S(1)}, u32[]{:S(2)}, u32[]{:S(2)}) collective-permute-start(bf16[2560,256]{1,0:T(8,128)(2,1)} %get-tuple-element.70), channel_id=1, source_target_pairs={{0,1},{1,0},{2,3},{3,2},{4,5},{5,4},{6,7},{7,6},{8,9},{9,8},{10,11... | collective-permute-start | bytes 3932168 | tf_op jit(solution)/shard_map/weights_y/ppermute | solution.py:34
  23.1 3.1 %collective-permute-start.7 = (bf16[2,512,128]{2,1,0:T(8,128)(2,1)}, bf16[2,512,128]{2,1,0:T(8,128)(2,1)}, u32[]{:S(2)}, u32[]{:S(2)}) collective-permute-start(bf16[2,512,128]{2,1,0:T(8,128)(2,1)} %collective-permute-done.rest_2_), channel_id=1, source_target_pairs={{0,2},{2,0},{4,6},{6,4},{8,10},{10,8},{12,14},{14,12},{16,18},{18,... | collective-permute-start | bytes 786440 | tf_op jit(solution)/shard_map/pair_core/ppermute | solution.py:34
  23.1 27.2 %copy-start.11 = (bf16[8,320,512]{2,1,0:T(8,128)(2,1)S(1)}, bf16[8,320,512]{2,1,0:T(8,128)(2,1)}, u32[]{:S(2)}) copy-start(bf16[8,320,512]{2,1,0:T(8,128)(2,1)} %get-tuple-element.81.rest_6_) | copy-start | bytes 7864324
  23.1 27.2 %copy-start.13 = (bf16[512,2048]{1,0:T(8,128)(2,1)S(1)}, bf16[512,2048]{1,0:T(8,128)(2,1)}, u32[]{:S(2)}) copy-start(bf16[512,2048]{1,0:T(8,128)(2,1)} %q_ref.3) | copy-start | bytes 6291460
  23.1 21.2 %collective-permute-start.3 = (bf16[2,512,128]{2,1,0:T(8,128)(2,1)}, bf16[2,512,128]{2,1,0:T(8,128)(2,1)S(1)}, u32[]{:S(2)}, u32[]{:S(2)}) collective-permute-start(bf16[2,512,128]{2,1,0:T(8,128)(2,1)} %get-tuple-element.77.rest_0_), channel_id=1, source_target_pairs={{0,6},{2,4},{4,10},{6,8},{8,14},{10,12},{12,18},{14,16},{16,22},{1... | collective-permute-start | bytes 786440 | tf_op jit(solution)/shard_map/pair_cross/ppermute | solution.py:34
  23.2 24.7 %collective-permute-start.2 = (bf16[2,512,128]{2,1,0:T(8,128)(2,1)}, bf16[2,512,128]{2,1,0:T(8,128)(2,1)S(1)}, u32[]{:S(2)}, u32[]{:S(2)}) collective-permute-start(bf16[2,512,128]{2,1,0:T(8,128)(2,1)} %get-tuple-element.77.rest_0_), channel_id=1, source_target_pairs={{0,4},{2,6},{4,8},{6,10},{8,12},{10,14},{12,16},{14,18},{16,20},{1... | collective-permute-start | bytes 786440 | tf_op jit(solution)/shard_map/pair_two/ppermute | solution.py:34
  26.2 21.7 %collective-permute-start.1 = (bf16[2,512,128]{2,1,0:T(8,128)(2,1)}, bf16[2,512,128]{2,1,0:T(8,128)(2,1)S(1)}, u32[]{:S(2)}, u32[]{:S(2)}) collective-permute-start(bf16[2,512,128]{2,1,0:T(8,128)(2,1)} %get-tuple-element.77.rest_0_), channel_id=1, source_target_pairs={{0,2},{2,8},{4,6},{6,12},{8,10},{10,16},{12,14},{14,20},{16,18},{1... | collective-permute-start | bytes 786440 | tf_op jit(solution)/shard_map/pair_other/ppermute | solution.py:34
  26.3 1.6 %copy-start.14 = (bf16[512,2048]{1,0:T(8,128)(2,1)S(1)}, bf16[512,2048]{1,0:T(8,128)(2,1)}, u32[]{:S(2)}) copy-start(bf16[512,2048]{1,0:T(8,128)(2,1)} %do_ref.3) | copy-start | bytes 6291460
  27.9 0.9 copy-start.16
  28.8 0.9 copy-start.18
  29.8 0.9 copy-start.21
  30.7 19.6 %copy-start.15 = (bf16[512,2048]{1,0:T(8,128)(2,1)S(1)}, bf16[512,2048]{1,0:T(8,128)(2,1)}, u32[]{:S(2)}) copy-start(bf16[512,2048]{1,0:T(8,128)(2,1)} %do_ref.3) | copy-start | bytes 6291460
  30.7 19.6 %copy-start.17 = (bf16[512,256]{1,0:T(8,128)(2,1)S(1)}, bf16[512,256]{1,0:T(8,128)(2,1)}, u32[]{:S(2)}) copy-start(bf16[512,256]{1,0:T(8,128)(2,1)} %rest_4_.4) | copy-start | bytes 786436
  30.7 19.6 %copy-start.19 = (bf16[512,256]{1,0:T(8,128)(2,1)S(1)}, bf16[512,256]{1,0:T(8,128)(2,1)}, u32[]{:S(2)}) copy-start(bf16[512,256]{1,0:T(8,128)(2,1)} %rest_5_.4) | copy-start | bytes 786436
  30.7 19.6 %copy-start.20 = (bf16[2,512,128]{2,1,0:T(8,128)(2,1)S(1)}, bf16[2,512,128]{2,1,0:T(8,128)(2,1)}, u32[]{:S(2)}) copy-start(bf16[2,512,128]{2,1,0:T(8,128)(2,1)} %get-tuple-element.77.rest_0_) | copy-start | bytes 786436
  44.3 19.0 %collective-permute-start.8 = (bf16[2,512,128]{2,1,0:T(8,128)(2,1)S(1)}, bf16[2,512,128]{2,1,0:T(8,128)(2,1)S(1)}, u32[]{:S(2)}, u32[]{:S(2)}) collective-permute-start(bf16[2,512,128]{2,1,0:T(8,128)(2,1)S(1)} %get-tuple-element.93), channel_id=1, source_target_pairs={{0,26},{2,0},{4,30},{6,4},{8,2},{10,8},{12,6},{14,12},{16,10},{18,... | collective-permute-start | bytes 786440 | tf_op jit(solution)/shard_map/grad_other/ppermute | solution.py:34
  47.9 15.4 %collective-permute-start.9 = (bf16[2,512,128]{2,1,0:T(8,128)(2,1)S(1)}, bf16[2,512,128]{2,1,0:T(8,128)(2,1)S(1)}, u32[]{:S(2)}, u32[]{:S(2)}) collective-permute-start(bf16[2,512,128]{2,1,0:T(8,128)(2,1)S(1)} %get-tuple-element.94), channel_id=1, source_target_pairs={{0,28},{2,30},{4,0},{6,2},{8,4},{10,6},{12,8},{14,10},{16,12},{18,... | collective-permute-start | bytes 786440 | tf_op jit(solution)/shard_map/grad_two/ppermute | solution.py:34
  47.9 15.4 %collective-permute-start.10 = (bf16[2,512,128]{2,1,0:T(8,128)(2,1)S(1)}, bf16[2,512,128]{2,1,0:T(8,128)(2,1)S(1)}, u32[]{:S(2)}, u32[]{:S(2)}) collective-permute-start(bf16[2,512,128]{2,1,0:T(8,128)(2,1)S(1)} %get-tuple-element.95), channel_id=1, source_target_pairs={{0,30},{2,28},{4,2},{6,0},{8,6},{10,4},{12,10},{14,8},{16,14},{18,... | collective-permute-start | bytes 786440 | tf_op jit(solution)/shard_map/grad_cross/ppermute | solution.py:34
  49.2 1.1 copy-start.4
  63.2 4.3 %copy-start = (bf16[8,320,512]{2,1,0:T(8,128)(2,1)}, bf16[8,320,512]{2,1,0:T(8,128)(2,1)S(1)}, u32[]{:S(2)}) copy-start(bf16[8,320,512]{2,1,0:T(8,128)(2,1)S(1)} %get-tuple-element.97.far_ref) | copy-start | bytes 7864324
  63.3 1.6 %collective-permute-start.11 = (bf16[2,512,128]{2,1,0:T(8,128)(2,1)S(1)}, bf16[2,512,128]{2,1,0:T(8,128)(2,1)S(1)}, u32[]{:S(2)}, u32[]{:S(2)}) collective-permute-start(bf16[2,512,128]{2,1,0:T(8,128)(2,1)S(1)} %get-tuple-element.99), channel_id=1, source_target_pairs={{0,2},{2,0},{4,6},{6,4},{8,10},{10,8},{12,14},{14,12},{16,18},{18,... | collective-permute-start | bytes 786440 | tf_op jit(solution)/shard_map/grad_core/ppermute | solution.py:34
  63.6 1.7 %collective-permute-start.12 = (bf16[512,256]{1,0:T(8,128)(2,1)S(1)}, bf16[512,256]{1,0:T(8,128)(2,1)S(1)}, u32[]{:S(2)}, u32[]{:S(2)}) collective-permute-start(bf16[512,256]{1,0:T(8,128)(2,1)S(1)} %pad_maximum_fusion.2.own_ref.rest_0_), channel_id=1, source_target_pairs={{0,2},{2,0},{4,6},{6,4},{8,10},{10,8},{12,14},{14,12},{16,18},{18,... | collective-permute-start | bytes 786440 | tf_op jit(solution)/shard_map/own_core/ppermute | solution.py:34
  65.3 2.2 %copy-start.6 = (bf16[512,256]{1,0:T(8,128)(2,1)}, bf16[512,256]{1,0:T(8,128)(2,1)S(1)}, u32[]{:S(2)}) copy-start(bf16[512,256]{1,0:T(8,128)(2,1)S(1)} %collective-permute-done.12.pair_ref) | copy-start | bytes 786436
  67.5 8.6 %collective-permute-start.13 = (bf16[512,256]{1,0:T(8,128)(2,1)S(1)}, bf16[512,256]{1,0:T(8,128)(2,1)S(1)}, u32[]{:S(2)}, u32[]{:S(2)}) collective-permute-start(bf16[512,256]{1,0:T(8,128)(2,1)S(1)} %pad_maximum_fusion.2.own_ref.rest_0_), channel_id=1, source_target_pairs={{0,1},{1,0},{2,3},{3,2},{4,5},{5,4},{6,7},{7,6},{8,9},{9,8},{10,11... | collective-permute-start | bytes 786440 | tf_op jit(solution)/shard_map/own_y/ppermute | solution.py:34
  69.0 7.1 %collective-permute-start.14 = (bf16[2,512,128]{2,1,0:T(8,128)(2,1)S(1)}, bf16[2,512,128]{2,1,0:T(8,128)(2,1)S(1)}, u32[]{:S(2)}, u32[]{:S(2)}) collective-permute-start(bf16[2,512,128]{2,1,0:T(8,128)(2,1)S(1)} %get-tuple-element.104), channel_id=1, source_target_pairs={{0,26},{2,0},{4,30},{6,4},{8,2},{10,8},{12,6},{14,12},{16,10},{18,... | collective-permute-start | bytes 786440 | tf_op jit(solution)/shard_map/grad_other/ppermute | solution.py:34
  69.0 10.6 %collective-permute-start.15 = (bf16[2,512,128]{2,1,0:T(8,128)(2,1)S(1)}, bf16[2,512,128]{2,1,0:T(8,128)(2,1)S(1)}, u32[]{:S(2)}, u32[]{:S(2)}) collective-permute-start(bf16[2,512,128]{2,1,0:T(8,128)(2,1)S(1)} %add_convert_fusion.1), channel_id=1, source_target_pairs={{0,28},{2,30},{4,0},{6,2},{8,4},{10,6},{12,8},{14,10},{16,12},{18,... | collective-permute-start | bytes 786440 | tf_op jit(solution)/shard_map/grad_two/ppermute | solution.py:34
  72.2 20.5 %collective-permute-start.16 = (bf16[4,320,256]{2,1,0:T(8,128)(2,1)}, bf16[4,320,256]{2,1,0:T(8,128)(2,1)}, u32[]{:S(2)}, u32[]{:S(2)}) collective-permute-start(bf16[4,320,256]{2,1,0:T(8,128)(2,1)} %weight_terms.6), channel_id=1, source_target_pairs={{0,4},{2,6},{4,0},{6,2},{8,12},{10,14},{12,8},{14,10},{16,20},{18,... | collective-permute-start | bytes 1966088 | tf_op jit(solution)/shard_map/terms_x/ppermute | solution.py:34
  76.1 3.7 %copy-start.8 = (bf16[512,256]{1,0:T(8,128)(2,1)}, bf16[512,256]{1,0:T(8,128)(2,1)S(1)}, u32[]{:S(2)}) copy-start(bf16[512,256]{1,0:T(8,128)(2,1)S(1)} %collective-permute-done.13.rest_2_) | copy-start | bytes 786436
  79.9 1.6 %collective-permute-start.17 = (bf16[512,256]{1,0:T(8,128)(2,1)S(1)}, bf16[512,256]{1,0:T(8,128)(2,1)S(1)}, u32[]{:S(2)}, u32[]{:S(2)}) collective-permute-start(bf16[512,256]{1,0:T(8,128)(2,1)S(1)} %pad_maximum_fusion.3.own_ref.rest_1_), channel_id=1, source_target_pairs={{0,2},{2,0},{4,6},{6,4},{8,10},{10,8},{12,14},{14,12},{16,18},{18,... | collective-permute-start | bytes 786440 | tf_op jit(solution)/shard_map/own_core/ppermute | solution.py:34
  80.0 34.2 %collective-permute-start.24 = (bf16[2560,256]{1,0:T(8,128)(2,1)}, bf16[2560,256]{1,0:T(8,128)(2,1)}, u32[]{:S(2)}, u32[]{:S(2)}) collective-permute-start(bf16[2560,256]{1,0:T(8,128)(2,1)} %copy-done.4), channel_id=1, source_target_pairs={{0,2},{2,0},{4,6},{6,4},{8,10},{10,8},{12,14},{14,12},{16,18},{18,... | collective-permute-start | bytes 3932168 | tf_op jit(solution)/shard_map/weights_core/ppermute | solution.py:34
  81.5 1.7 %copy-start.1 = (bf16[8,320,512]{2,1,0:T(8,128)(2,1)S(1)}, bf16[8,320,512]{2,1,0:T(8,128)(2,1)}, u32[]{:S(2)}) copy-start(bf16[8,320,512]{2,1,0:T(8,128)(2,1)} %copy-done) | copy-start | bytes 7864324
  84.6 8.1 %copy-start.7 = (bf16[512,256]{1,0:T(8,128)(2,1)S(1)}, bf16[512,256]{1,0:T(8,128)(2,1)}, u32[]{:S(2)}) copy-start(bf16[512,256]{1,0:T(8,128)(2,1)} %copy-done.6) | copy-start | bytes 786436
  84.6 12.5 %collective-permute-start.20 = (bf16[4,320,128]{2,1,0:T(8,128)(2,1)S(1)}, bf16[4,320,128]{2,1,0:T(8,128)(2,1)S(1)}, u32[]{:S(2)}, u32[]{:S(2)}) collective-permute-start(bf16[4,320,128]{2,1,0:T(8,128)(2,1)S(1)} %weight_terms.7), channel_id=1, source_target_pairs={{0,8},{2,10},{4,12},{6,14},{8,0},{10,2},{12,4},{14,6},{16,24},{18,... | collective-permute-start | bytes 983048 | tf_op jit(solution)/shard_map/terms_z1/ppermute | solution.py:34
  87.0 11.9 %collective-permute-start.19 = (bf16[4,320,128]{2,1,0:T(8,128)(2,1)S(1)}, bf16[4,320,128]{2,1,0:T(8,128)(2,1)S(1)}, u32[]{:S(2)}, u32[]{:S(2)}) collective-permute-start(bf16[4,320,128]{2,1,0:T(8,128)(2,1)S(1)} %weight_terms.8), channel_id=1, source_target_pairs={{0,4},{2,6},{4,0},{6,2},{8,12},{10,14},{12,8},{14,10},{16,20},{18,... | collective-permute-start | bytes 983048 | tf_op jit(solution)/shard_map/terms_x/ppermute | solution.py:34
  94.7 12.5 %collective-permute-start.18 = (bf16[2,320,256]{2,1,0:T(8,128)(2,1)S(1)}, bf16[2,320,256]{2,1,0:T(8,128)(2,1)S(1)}, u32[]{:S(2)}, u32[]{:S(2)}) collective-permute-start(bf16[2,320,256]{2,1,0:T(8,128)(2,1)S(1)} %get-tuple-element.108), channel_id=1, source_target_pairs={{0,8},{2,10},{4,12},{6,14},{8,0},{10,2},{12,4},{14,6},{16,24},{18,... | collective-permute-start | bytes 983048 | tf_op jit(solution)/shard_map/terms_z1/ppermute | solution.py:34
  96.5 7.3 %collective-permute-start.21 = (bf16[512,256]{1,0:T(8,128)(2,1)S(1)}, bf16[512,256]{1,0:T(8,128)(2,1)S(1)}, u32[]{:S(2)}, u32[]{:S(2)}) collective-permute-start(bf16[512,256]{1,0:T(8,128)(2,1)S(1)} %pad_maximum_fusion.3.own_ref.rest_1_), channel_id=1, source_target_pairs={{0,1},{1,0},{2,3},{3,2},{4,5},{5,4},{6,7},{7,6},{8,9},{9,8},{10,11... | collective-permute-start | bytes 786440 | tf_op jit(solution)/shard_map/own_y/ppermute | solution.py:34
  98.5 10.0 %collective-permute-start.22 = (bf16[2,320,128]{2,1,0:T(8,128)(2,1)S(1)}, bf16[2,320,128]{2,1,0:T(8,128)(2,1)S(1)}, u32[]{:S(2)}, u32[]{:S(2)}) collective-permute-start(bf16[2,320,128]{2,1,0:T(8,128)(2,1)S(1)} %get-tuple-element.115), channel_id=1, source_target_pairs={{0,16},{2,18},{4,20},{6,22},{8,24},{10,26},{12,28},{14,30},{16,0},... | collective-permute-start | bytes 491528 | tf_op jit(solution)/shard_map/terms_z2/ppermute | solution.py:34
  103.8 10.4 %copy-start.2 = (bf16[5120,256]{1,0:T(8,128)(2,1)S(1)}, bf16[5120,256]{1,0:T(8,128)(2,1)}, u32[]{:S(2)}) copy-start(bf16[5120,256]{1,0:T(8,128)(2,1)} %rest_4_.5) | copy-start | bytes 7864324
  103.8 10.4 %copy-start.3 = (bf16[5120,256]{1,0:T(8,128)(2,1)S(1)}, bf16[5120,256]{1,0:T(8,128)(2,1)}, u32[]{:S(2)}) copy-start(bf16[5120,256]{1,0:T(8,128)(2,1)} %rest_5_.5) | copy-start | bytes 7864324
  103.8 10.4 %copy-start.5 = (bf16[2560,256]{1,0:T(8,128)(2,1)S(1)}, bf16[2560,256]{1,0:T(8,128)(2,1)}, u32[]{:S(2)}) copy-start(bf16[2560,256]{1,0:T(8,128)(2,1)} %copy-done.4) | copy-start | bytes 3932164
  103.8 10.4 %copy-start.9 = (bf16[512,256]{1,0:T(8,128)(2,1)S(1)}, bf16[512,256]{1,0:T(8,128)(2,1)}, u32[]{:S(2)}) copy-start(bf16[512,256]{1,0:T(8,128)(2,1)} %copy-done.8) | copy-start | bytes 786436
  103.8 10.4 %copy-start.10 = (s32[2]{0:T(128)S(1)}, s32[2]{0:T(128)}, u32[]{:S(2)}) copy-start(s32[2]{0:T(128)} %pad_add_fusion.at_ref) | copy-start | bytes 28
  105.2 7.8 %collective-permute-start.23 = (bf16[2,320,128]{2,1,0:T(8,128)(2,1)S(1)}, bf16[2,320,128]{2,1,0:T(8,128)(2,1)S(1)}, u32[]{:S(2)}, u32[]{:S(2)}) collective-permute-start(bf16[2,320,128]{2,1,0:T(8,128)(2,1)S(1)} %get-tuple-element.117), channel_id=1, source_target_pairs={{0,8},{2,10},{4,12},{6,14},{8,0},{10,2},{12,4},{14,6},{16,24},{18,... | collective-permute-start | bytes 491528 | tf_op jit(solution)/shard_map/terms_z1/ppermute | solution.py:34
  107.2 13.4 %collective-permute-start.25 = (bf16[320,256]{1,0:T(8,128)(2,1)S(1)}, bf16[320,256]{1,0:T(8,128)(2,1)S(1)}, u32[]{:S(2)}, u32[]{:S(2)}) collective-permute-start(bf16[320,256]{1,0:T(8,128)(2,1)S(1)} %fusion), channel_id=1, source_target_pairs={{0,16},{2,18},{4,20},{6,22},{8,24},{10,26},{12,28},{14,30},{16,0},... | collective-permute-start | bytes 491528 | tf_op jit(solution)/shard_map/terms_z2/ppermute | solution.py:34
  108.5 12.0 %collective-permute-start.26 = (bf16[320,128]{1,0:T(8,128)(2,1)S(1)}, bf16[320,128]{1,0:T(8,128)(2,1)S(1)}, u32[]{:S(2)}, u32[]{:S(2)}) collective-permute-start(bf16[320,128]{1,0:T(8,128)(2,1)S(1)} %fusion.1), channel_id=1, source_target_pairs={{0,4},{2,6},{4,0},{6,2},{8,12},{10,14},{12,8},{14,10},{16,20},{18,... | collective-permute-start | bytes 245768 | tf_op jit(solution)/shard_map/terms_x/ppermute | solution.py:34
  113.0 7.6 %collective-permute-start.27 = (bf16[320,128]{1,0:T(8,128)(2,1)S(1)}, bf16[320,128]{1,0:T(8,128)(2,1)S(1)}, u32[]{:S(2)}, u32[]{:S(2)}) collective-permute-start(bf16[320,128]{1,0:T(8,128)(2,1)S(1)} %fusion.2), channel_id=1, source_target_pairs={{0,16},{2,18},{4,20},{6,22},{8,24},{10,26},{12,28},{14,30},{16,0},... | collective-permute-start | bytes 245768 | tf_op jit(solution)/shard_map/terms_z2/ppermute | solution.py:34
